TPU v7x, 32 devices: a whole 2x2x4 slice. The times are simulated.
32 devices in a mesh: dp: 8 (over z, x), mp: 4 (over y, core).
Axes of the slice: x: 2, y: 2, z: 4, core: 2. Of those that a mesh axis runs over, the one named last changes fastest.
Arguments:
- tokens: float32 [2048, 1024], P('dp'), may hold values from -6 to 6
- w_qkv: bfloat16 [1024, 3072], P('dp', 'mp'), may hold values from -0.1875 to 0.1875
- w_out: bfloat16 [1024, 1024], P('mp', 'dp'), may hold values from -4 to 4
- w_up: bfloat16 [1024, 4096], P('dp', 'mp'), may hold values from -0.1875 to 0.1875
- w_down: bfloat16 [4096, 1024], P('mp', 'dp'), may hold values from -0.09375 to 0.09375
- ln1_gain: bfloat16 [1024], P('dp'), may hold values from 0.5 to 1.5
- ln1_bias: bfloat16 [1024], P('dp'), may hold values from -3 to 3
- ln2_gain: bfloat16 [1024], P('dp'), may hold values from 0.5 to 1.5
- ln2_bias: bfloat16 [1024], P('dp'), may hold values from -3 to 3
- scene_lengths: int32 [8], replicated, may hold values from 1 to 1792, as said below
- grad_out: float32 [2048, 1024], P('dp'), may hold values from -6 to 6
Outputs:
- result: float32 [2048, 1024], P('dp')
- grad_tokens: float32 [2048, 1024], P('dp')
- grad_w_qkv: float32 [1024, 3072], P('dp', 'mp')
- grad_w_out: float32 [1024, 1024], P('mp', 'dp')
- grad_w_up: float32 [1024, 4096], P('dp', 'mp')
- grad_w_down: float32 [4096, 1024], P('mp', 'dp')
- grad_ln1_gain: float32 [1024], P('dp')
- grad_ln1_bias: float32 [1024], P('dp')
- grad_ln2_gain: float32 [1024], P('dp')
- grad_ln2_bias: float32 [1024], P('dp')
Inputs may be any that keep to these rules, and one draw needn't show every extreme that they name: `scene_lengths`: the lengths sum to 2048; one scene, at a place drawn from the seed, has exactly 1792 tokens, and the other scenes together hold 256 tokens.
All inputs are finite; a program needn't handle non-finite values.
Results may differ from a plain program's by a relative error of at most 0.017.
Values may be sent and summed in bfloat16 or wider, within the bound.
A program may use at most 128 MiB of HBM per device.

v0:
```python
import math

import jax
import jax.numpy as jnp
from jax import lax
from jax.sharding import PartitionSpec as P

HEADS = 16
HEAD_DIM = 64


highest = lax.Precision.HIGHEST
very_low = -1e30


def norm_forward(values, gain, bias):
    center = values - jnp.mean(values, axis=-1, keepdims=True)
    inverse = lax.rsqrt(jnp.mean(center * center, axis=-1, keepdims=True) + 1e-05)
    normed = center * inverse
    return (normed * gain + bias, normed, inverse)


def norm_backward(upstream, normed, inverse, gain):
    scaled = upstream * gain
    return inverse * (
        scaled
        - jnp.mean(scaled, axis=-1, keepdims=True)
        - normed * jnp.mean(scaled * normed, axis=-1, keepdims=True)
    )


def scene_index(positions, scene_ends):
    return jnp.sum((positions[:, None] >= scene_ends[None, :]).astype(jnp.int32), axis=1)


def rows_product(left, right):
    return lax.dot_general(
        left, right, (((0,), (0,)), ((), ())), preferred_element_type=jnp.float32
    )


def cols_product(left, right):
    return lax.dot_general(
        left, right, (((1,), (1,)), ((), ())), preferred_element_type=jnp.float32
    )


def over_blocks(running, arrays, step_fn):
    total_rows = arrays[0].shape[0]
    block_rows = math.gcd(total_rows, 1024)
    block_number = total_rows // block_rows
    stacked = tuple(
        (member.reshape((block_number, block_rows) + member.shape[1:]) for member in arrays)
    )

    def visit(running_state, visit_item):
        block_index, blocks = visit_item
        return (step_fn(running_state, blocks, block_index * block_rows), None)

    running, unused_out = lax.scan(
        visit, running, (jnp.arange(block_number, dtype=jnp.int32), stacked)
    )
    return running


def on_device(
    tokens,
    w_qkv,
    w_out,
    w_up,
    w_down,
    ln1_gain,
    ln1_bias,
    ln2_gain,
    ln2_bias,
    scene_lengths,
    grad_out,
):
    row_count = tokens.shape[0]
    local_heads = HEADS // lax.axis_size("mp")
    score_scale = HEAD_DIM ** (-0.5)
    gathered = (
        lax.all_gather(w_qkv, "dp", axis=0, tiled=True),
        lax.all_gather(w_up, "dp", axis=0, tiled=True),
        lax.all_gather(w_out, "dp", axis=1, tiled=True),
        lax.all_gather(w_down, "dp", axis=1, tiled=True),
        lax.all_gather(ln1_gain, "dp", axis=0, tiled=True),
        lax.all_gather(ln1_bias, "dp", axis=0, tiled=True),
        lax.all_gather(ln2_gain, "dp", axis=0, tiled=True),
        lax.all_gather(ln2_bias, "dp", axis=0, tiled=True),
    )
    full_qkv, full_up, full_out, full_down = (gathered[0], gathered[1], gathered[2], gathered[3])
    gain_one = gathered[4].astype(jnp.float32)
    bias_one = gathered[5].astype(jnp.float32)
    gain_two = gathered[6].astype(jnp.float32)
    bias_two = gathered[7].astype(jnp.float32)
    scene_ends = jnp.cumsum(scene_lengths)
    first_row = lax.axis_index("dp") * row_count
    own_scene = scene_index(first_row + jnp.arange(row_count, dtype=jnp.int32), scene_ends)
    own_lowest = own_scene[0]
    own_highest = own_scene[row_count - 1]

    def touches(start, length):
        bounds = scene_index(jnp.stack([start, start + length - 1]), scene_ends)
        return (bounds[0] <= own_highest) & (own_lowest <= bounds[1])

    hidden_one, normed_one, inverse_one = norm_forward(tokens, gain_one, bias_one)
    hidden_one = hidden_one.astype(jnp.bfloat16)
    mixed = jnp.dot(hidden_one, full_qkv, preferred_element_type=jnp.float32).astype(jnp.bfloat16)
    mixed = mixed.reshape(row_count, local_heads, 3, HEAD_DIM)
    query = mixed[:, :, 0]
    keys_own = mixed[:, :, 1]
    values_own = mixed[:, :, 2]
    keys_flat = keys_own.reshape(row_count, local_heads * HEAD_DIM)
    values_flat = values_own.reshape(row_count, local_heads * HEAD_DIM)

    def key_scores(key_block, key_start):
        length = key_block.shape[0]
        key_scene = scene_index(key_start + jnp.arange(length, dtype=jnp.int32), scene_ends)
        same = own_scene[:, None] == key_scene[None, :]
        scores = (
            jnp.einsum(
                "qhd,khd->hqk",
                query,
                key_block.reshape(length, local_heads, HEAD_DIM),
                preferred_element_type=jnp.float32,
            )
            * score_scale
        )
        return (scores, same)

    def forward_step(running, blocks, key_start):
        key_block, value_block = blocks

        def forward_work(running_state):
            top, total, accum = running_state
            scores, same = key_scores(key_block, key_start)
            masked = jnp.where(same[None], scores, very_low)
            new_top = jnp.maximum(top, jnp.max(masked, axis=-1))
            expo = jnp.where(same[None], jnp.exp(masked - new_top[..., None]), 0.0)
            factor = jnp.exp(top - new_top)
            total = total * factor + jnp.sum(expo, axis=-1)
            value_float = value_block.reshape(-1, local_heads, HEAD_DIM).astype(jnp.float32)
            accum = accum * factor.T[..., None] + jnp.einsum(
                "hqk,khd->qhd", expo, value_float, precision=highest
            )
            return (new_top, total, accum)

        return lax.cond(
            touches(key_start, key_block.shape[0]),
            forward_work,
            lambda running_state: running_state,
            running,
        )

    start_state = (
        jnp.full((local_heads, row_count), very_low, jnp.float32),
        jnp.zeros((local_heads, row_count), jnp.float32),
        jnp.zeros((row_count, local_heads, HEAD_DIM), jnp.float32),
    )
    top, total, accum = over_blocks(
        start_state,
        (
            lax.all_gather(keys_flat, "dp", axis=0, tiled=True),
            lax.all_gather(values_flat, "dp", axis=0, tiled=True),
        ),
        forward_step,
    )
    log_total = top + jnp.log(total)
    attended = accum / total.T[..., None]
    att_low = attended.reshape(row_count, local_heads * HEAD_DIM).astype(jnp.bfloat16)
    branch = lax.psum(jnp.dot(att_low, full_out, preferred_element_type=jnp.float32), "mp")
    middle = tokens + branch
    hidden_two, normed_two, inverse_two = norm_forward(middle, gain_two, bias_two)
    hidden_two = hidden_two.astype(jnp.bfloat16)
    inner = jnp.dot(hidden_two, full_up, preferred_element_type=jnp.float32)
    active, gelu_pull = jax.vjp(jax.nn.gelu, inner)
    active_low = active.astype(jnp.bfloat16)
    result = middle + lax.psum(
        jnp.dot(active_low, full_down, preferred_element_type=jnp.float32).astype(jnp.bfloat16),
        "mp",
    ).astype(jnp.float32)
    out_low = grad_out.astype(jnp.bfloat16)
    grad_down = rows_product(active_low, out_low)
    (grad_inner,) = gelu_pull(cols_product(out_low, full_down))
    inner_low = grad_inner.astype(jnp.bfloat16)
    grad_up = rows_product(hidden_two, inner_low)
    back_two = lax.psum(cols_product(inner_low, full_up), "mp")
    grad_middle = grad_out + norm_backward(back_two, normed_two, inverse_two, gain_two)
    middle_low = grad_middle.astype(jnp.bfloat16)
    gain_grad_two = jnp.sum(back_two * normed_two, axis=0)
    bias_grad_two = jnp.sum(back_two, axis=0)
    grad_proj = rows_product(att_low, middle_low)
    grad_att = (
        cols_product(middle_low, full_out)
        .astype(jnp.bfloat16)
        .reshape(row_count, local_heads, HEAD_DIM)
    )
    shift_term = jnp.sum(grad_att.astype(jnp.float32) * attended, axis=-1).T

    def query_step(running, blocks, key_start):
        key_block, value_block = blocks

        def query_work(accum):
            length = key_block.shape[0]
            scores, same = key_scores(key_block, key_start)
            prob = jnp.exp(jnp.where(same[None], scores - log_total[..., None], very_low))
            dprob = jnp.einsum(
                "qhd,khd->hqk",
                grad_att,
                value_block.reshape(length, local_heads, HEAD_DIM),
                preferred_element_type=jnp.float32,
            )
            dscore = (prob * (dprob - shift_term[..., None])).astype(jnp.bfloat16)
            return accum + jnp.einsum(
                "hqk,khd->qhd",
                dscore,
                key_block.reshape(length, local_heads, HEAD_DIM),
                preferred_element_type=jnp.float32,
            )

        return lax.cond(
            touches(key_start, key_block.shape[0]), query_work, lambda accum: accum, running
        )

    zero_grad = jnp.zeros((row_count, local_heads, HEAD_DIM), jnp.float32)
    grad_query = over_blocks(
        zero_grad,
        (
            lax.all_gather(keys_flat, "dp", axis=0, tiled=True),
            lax.all_gather(values_flat, "dp", axis=0, tiled=True),
        ),
        query_step,
    )
    all_log, all_shift = (
        lax.all_gather(log_total.T, "dp", axis=0, tiled=True),
        lax.all_gather(shift_term.T, "dp", axis=0, tiled=True),
    )

    def key_step(running, blocks, query_start):
        query_block, grad_block = blocks

        def key_work(running_state):
            grad_keys, grad_values = running_state
            length = query_block.shape[0]
            query_scene = scene_index(query_start + jnp.arange(length, dtype=jnp.int32), scene_ends)
            same = query_scene[:, None] == own_scene[None, :]
            query_three = query_block.reshape(length, local_heads, HEAD_DIM)
            grad_three = grad_block.reshape(length, local_heads, HEAD_DIM)
            scores = (
                jnp.einsum(
                    "qhd,khd->hqk", query_three, keys_own, preferred_element_type=jnp.float32
                )
                * score_scale
            )
            block_log = lax.dynamic_slice_in_dim(all_log, query_start, length, 0).T
            block_shift = lax.dynamic_slice_in_dim(all_shift, query_start, length, 0).T
            prob = jnp.exp(jnp.where(same[None], scores - block_log[..., None], very_low))
            grad_values = grad_values + jnp.einsum(
                "hqk,qhd->khd", prob, grad_three.astype(jnp.float32), precision=highest
            )
            dprob = jnp.einsum(
                "qhd,khd->hqk", grad_three, values_own, preferred_element_type=jnp.float32
            )
            dscore = (prob * (dprob - block_shift[..., None])).astype(jnp.bfloat16)
            grad_keys = grad_keys + jnp.einsum(
                "hqk,qhd->khd", dscore, query_three, preferred_element_type=jnp.float32
            )
            return (grad_keys, grad_values)

        return lax.cond(
            touches(query_start, query_block.shape[0]),
            key_work,
            lambda running_state: running_state,
            running,
        )

    query_flat = query.reshape(row_count, local_heads * HEAD_DIM)
    grad_att_flat = grad_att.reshape(row_count, local_heads * HEAD_DIM)
    grad_keys, grad_values = over_blocks(
        (zero_grad, zero_grad),
        (
            lax.all_gather(query_flat, "dp", axis=0, tiled=True),
            lax.all_gather(grad_att_flat, "dp", axis=0, tiled=True),
        ),
        key_step,
    )
    grad_mixed = jnp.stack([grad_query * score_scale, grad_keys * score_scale, grad_values], axis=2)
    grad_mixed = grad_mixed.reshape(row_count, local_heads * 3 * HEAD_DIM).astype(jnp.bfloat16)
    grad_qkv = rows_product(hidden_one, grad_mixed)
    back_one = lax.psum(cols_product(grad_mixed, full_qkv).astype(jnp.bfloat16), "mp").astype(
        jnp.float32
    )
    grad_tokens = grad_middle + norm_backward(back_one, normed_one, inverse_one, gain_one)
    gain_grad_one = jnp.sum(back_one * normed_one, axis=0)
    bias_grad_one = jnp.sum(back_one, axis=0)
    shards = (
        lax.psum_scatter(grad_qkv, "dp", scatter_dimension=0, tiled=True),
        lax.psum_scatter(grad_proj, "dp", scatter_dimension=1, tiled=True),
        lax.psum_scatter(grad_up, "dp", scatter_dimension=0, tiled=True),
        lax.psum_scatter(grad_down, "dp", scatter_dimension=1, tiled=True),
        lax.psum_scatter(gain_grad_one, "dp", scatter_dimension=0, tiled=True),
        lax.psum_scatter(bias_grad_one, "dp", scatter_dimension=0, tiled=True),
        lax.psum_scatter(gain_grad_two, "dp", scatter_dimension=0, tiled=True),
        lax.psum_scatter(bias_grad_two, "dp", scatter_dimension=0, tiled=True),
    )
    return (
        result,
        grad_tokens,
        shards[0],
        shards[1],
        shards[2],
        shards[3],
        shards[4],
        shards[5],
        shards[6],
        shards[7],
    )


def solution(mesh):
    in_specs = (
        P("dp", None),
        P("dp", "mp"),
        P("mp", "dp"),
        P("dp", "mp"),
        P("mp", "dp"),
        P("dp"),
        P("dp"),
        P("dp"),
        P("dp"),
        P(),
        P("dp", None),
    )
    out_specs = (
        P("dp", None),
        P("dp", None),
        P("dp", "mp"),
        P("mp", "dp"),
        P("dp", "mp"),
        P("mp", "dp"),
        P("dp"),
        P("dp"),
        P("dp"),
        P("dp"),
    )
    return jax.shard_map(
        on_device, mesh=mesh, in_specs=in_specs, out_specs=out_specs, check_vma=False
    )
```

profile of v0, /device:TPU:0, one launch (start us, length us, event | category | flops | bytes accessed | tf_op | source)
XLA Modules:
  0.0 906.2 jit_solution(1932563432292803729)
XLA Ops:
  8.0 22.3 %all-gather = bf16[8,1,128]{2,1,0:T(2,128)(2,1)S(1)} all-gather(bf16[1,1,128]{2,1,0:T(2,128)(2,1)} %bitcast.215), channel_id=1, replica_groups=mesh['dp'=8,'mp'=4] {'dp'}, dimensions={0}, use_global_device_ids=true | all-gather | bytes 2304 | tf_op jit(solution)/shard_map/all_gather | solution.py:87
  30.3 16.4 %all-gather.1 = bf16[8,1,128]{2,1,0:T(2,128)(2,1)S(1)} all-gather(bf16[1,1,128]{2,1,0:T(2,128)(2,1)} %bitcast.216), channel_id=1, replica_groups=mesh['dp'=8,'mp'=4] {'dp'}, dimensions={0}, use_global_device_ids=true | all-gather | bytes 2304 | tf_op jit(solution)/shard_map/all_gather | solution.py:88
  62.1 29.3 %all_gather.49 = bf16[256,1024]{1,0:T(8,128)(2,1)} all-gather(bf16[256,128]{1,0:T(8,128)(2,1)S(1)} %copy-done.15), channel_id=1, replica_groups=mesh['dp'=8,'mp'=4] {'dp'}, dimensions={1}, use_global_device_ids=true | all-gather | bytes 589824 | tf_op jit(solution)/shard_map/all_gather | solution.py:85
  91.4 10.6 %all-gather.16.cloned.1.call-done = bf16[2048,256]{0,1:T(8,128)(2,1)} async-done(((bf16[256,256]{0,1:T(8,128)(2,1)}), bf16[2048,256]{0,1:T(8,128)(2,1)}) %all-gather.16.cloned.1.call-update) | async-done | bytes 1048592 | tf_op jit(solution)/shard_map/all_gather | solution.py:165
  103.2 40.2 %all-gather.14.cloned.1.call-done = bf16[2048,256]{1,0:T(8,128)(2,1)} async-done(((bf16[256,256]{1,0:T(8,128)(2,1)}), bf16[2048,256]{1,0:T(8,128)(2,1)}) %all-gather.14.cloned.1.call-update) | async-done | bytes 1048592 | tf_op jit(solution)/shard_map/all_gather | solution.py:164
  145.0 19.6 %while.51 = (s32[]{:T(128)}, f32[4,256]{1,0:T(4,128)S(1)}, f32[4,256]{1,0:T(4,128)S(1)}, f32[256,4,64]{0,2,1:T(8,128)S(1)}, s32[2]{0:T(128)S(1)}, /*index=5*/s32...) while((s32[]{:T(128)}, f32[4,256]{1,0:T(4,128)S(1)}, ...), condition=%wide.region_11.12_spmd, body=%wide.region_4.11_spmd.sunk | while | flops 952527936 | bytes 17515988 | solution.py:60
  168.9 18.4 %all-gather.2 = bf16[8,1,128]{2,1,0:T(2,128)(2,1)S(1)} all-gather(bf16[1,1,128]{2,1,0:T(2,128)(2,1)} %bitcast.217), channel_id=1, replica_groups=mesh['dp'=8,'mp'=4] {'dp'}, dimensions={0}, use_global_device_ids=true | all-gather | bytes 2304 | tf_op jit(solution)/shard_map/all_gather | solution.py:89
  187.9 16.4 %all-gather.3 = bf16[8,1,128]{2,1,0:T(2,128)(2,1)S(1)} all-gather(bf16[1,1,128]{2,1,0:T(2,128)(2,1)} %bitcast.218), channel_id=1, replica_groups=mesh['dp'=8,'mp'=4] {'dp'}, dimensions={0}, use_global_device_ids=true | all-gather | bytes 2304 | tf_op jit(solution)/shard_map/all_gather | solution.py:90
  208.1 46.5 %all-gather.18.cloned.1.call-done = bf16[1024,1024]{1,0:T(8,128)(2,1)} async-done(((bf16[128,1024]{1,0:T(8,128)(2,1)}), bf16[1024,1024]{1,0:T(8,128)(2,1)}) %all-gather.18.cloned.1.call-update) | async-done | bytes 2097168 | tf_op jit(solution)/shard_map/all_gather | solution.py:84
  258.2 48.0 %all-gather.20.cloned.1.call-done = bf16[1024,1024]{1,0:T(8,128)(2,1)} async-done(((bf16[1024,128]{1,0:T(8,128)(2,1)}), bf16[1024,1024]{1,0:T(8,128)(2,1)}) %all-gather.20.cloned.1.call-update) | async-done | bytes 2097168 | tf_op jit(solution)/shard_map/all_gather | solution.py:86
  313.0 33.5 %all-reduce.12.cloned.1.call-done = f32[256,1024]{1,0:T(8,128)} async-done(((f32[256,1024]{1,0:T(8,128)}), f32[256,1024]{1,0:T(8,128)}) %all-reduce.12.cloned.1.call-update) | async-done | bytes 1048592 | tf_op jit(solution)/shard_map/psum | solution.py:188
  353.4 35.0 %all-gather.22.cloned.1.call-done = bf16[2048,256]{0,1:T(8,128)(2,1)} async-done(((bf16[256,256]{0,1:T(8,128)(2,1)}), bf16[2048,256]{0,1:T(8,128)(2,1)}) %all-gather.22.cloned.1.call-update) | async-done | bytes 1048592 | tf_op jit(solution)/shard_map/all_gather | solution.py:283
  391.9 32.1 %all_gather.55 = f32[2048,4]{0,1:T(4,128)} all-gather(f32[256,4]{0,1:T(4,128)} %bitcast.54), channel_id=1, replica_groups=mesh['dp'=8,'mp'=4] {'dp'}, dimensions={0}, use_global_device_ids=true | all-gather | bytes 36864 | tf_op jit(solution)/shard_map/all_gather | solution.py:236
  427.5 32.4 %all_gather.57 = f32[2048,4]{0,1:T(4,128)} all-gather(f32[256,4]{0,1:T(4,128)} %get-tuple-element.1374), channel_id=1, replica_groups=mesh['dp'=8,'mp'=4] {'dp'}, dimensions={0}, use_global_device_ids=true | all-gather | bytes 36864 | tf_op jit(solution)/shard_map/all_gather | solution.py:237
  460.7 25.3 %while.52 = (s32[]{:T(128)}, f32[256,4,64]{0,2,1:T(8,128)}, s32[2]{0:T(128)S(1)}, s32[8]{0:T(128)S(1)}, s32[]{:T(128)}, /*index=5*/s32[]{:T(128)}, s32[256]{0:T(...) while((s32[]{:T(128)}, f32[256,4,64]{0,2,1:T(8,128)}, ...), condition=%wide.region_25.26_spmd, body=%wide.region_20.25_spmd.sunk | while | flops 409296960 | bytes 13395379 | solution.py:60
  489.7 39.1 %while.53 = (s32[]{:T(128)}, f32[256,4,64]{0,2,1:T(8,128)}, f32[256,4,64]{0,2,1:T(8,128)S(1)}, s32[2]{0:T(128)S(1)}, s32[8]{0:T(128)S(1)}, /*index=5*/s32[]{:T(1...) while((s32[]{:T(128)}, f32[256,4,64]{0,2,1:T(8,128)}, ...), condition=%wide.region_31.32_spmd, body=%wide.region_26.31_spmd.sunk | while | flops 1217814528 | bytes 19531300 | solution.py:60
  494.2 15.0 %conditional.8 = ((f32[256,4,64]{0,2,1:T(8,128)}, f32[256,4,64]{0,2,1:T(8,128)S(1)})) conditional(s32[]{:T(128)} %convert_element_type.256, (f32[256,4,64]{0,2,1:T(8,128)}, f32[256,4,64]{0,2,1:T(8,128)S(1)}) %tuple.199, (s32[]{:T(128)}, s32[8]{0:T(128)S(1)}, s32[256]{0:T(256)S(1)}, bf16[2,1024,256]{1,2,0:T(8,128)(2,1)}, s32[]{:T(128)}, ...), branch_computations={%region_28.28_spmd, %region_29.30_spmd} | conditional | flops 1217814528 | bytes 19530882 | solution.py:271
  513.8 15.0 %conditional.8 = ((f32[256,4,64]{0,2,1:T(8,128)}, f32[256,4,64]{0,2,1:T(8,128)S(1)})) conditional(s32[]{:T(128)} %convert_element_type.256, (f32[256,4,64]{0,2,1:T(8,128)}, f32[256,4,64]{0,2,1:T(8,128)S(1)}) %tuple.199, (s32[]{:T(128)}, s32[8]{0:T(128)S(1)}, s32[256]{0:T(256)S(1)}, bf16[2,1024,256]{1,2,0:T(8,128)(2,1)}, s32[]{:T(128)}, ...), branch_computations={%region_28.28_spmd, %region_29.30_spmd} | conditional | flops 1217814528 | bytes 19530882 | solution.py:271
  548.2 20.8 %all-reduce.14.cloned.1.call-done = (bf16[256,1024]{1,0:T(8,128)(2,1)}, bf16[256,1024]{1,0:T(8,128)(2,1)}) async-done(((bf16[256,1024]{1,0:T(8,128)(2,1)}, bf16[256,1024]{1,0:T(8,128)(2,1)}), (bf16[256,1024]{1,0:T(8,128)(2,1)}, bf16[256,1024]{1,0:T(8,128)(2,1)})) %all-reduce.14.cloned.1.call-update) | async-done | bytes 1048592 | tf_op jit(solution)/shard_map/psum | solution.py:179
  570.5 37.3 %all-reduce.4 = (f32[1024]{0:T(1024)S(1)}, f32[1024]{0:T(1024)S(1)}, f32[1024]{0:T(1024)S(1)}, f32[1024]{0:T(1024)S(1)}) all-reduce(f32[1024]{0:T(1024)S(1)} %get-tuple-element.1256, f32[1024]{0:T(1024)S(1)} %get-tuple-element.1261, f32[1024]{0:T(1024)S(1)} %copy-done.23, ...), channel_id=6, replica_groups=mesh['dp'=8,'mp'=4] {'dp'}, use_global_device_ids=true, to_apply=%region_40.41.clone | all-reduce | flops 4096 | bytes 32768
  614.7 23.0 %reduce-scatter.7.cloned.1.call-done = f32[256,128]{1,0:T(8,128)} async-done(((f32[256,1024]{1,0:T(8,128)}), f32[256,128]{1,0:T(8,128)}) %reduce-scatter.7.cloned.1.call-update) | async-done | bytes 131088 | tf_op jit(solution)/shard_map/reduce_scatter | solution.py:299
  637.7 91.0 %reduce-scatter.9.cloned.1.call-done = f32[128,1024]{1,0:T(8,128)} async-done(((f32[1024,1024]{1,0:T(8,128)}), f32[128,1024]{1,0:T(8,128)}) %reduce-scatter.9.cloned.1.call-update) | async-done | bytes 524304 | tf_op jit(solution)/shard_map/reduce_scatter | solution.py:300
  728.7 92.9 %reduce-scatter.11.cloned.1.call-done = f32[1024,128]{1,0:T(8,128)} async-done(((f32[1024,1024]{1,0:T(8,128)}), f32[1024,128]{1,0:T(8,128)}) %reduce-scatter.11.cloned.1.call-update) | async-done | bytes 524304 | tf_op jit(solution)/shard_map/reduce_scatter | solution.py:301
  821.6 78.0 %reduce-scatter.5.cloned.1.call-done = f32[128,768]{1,0:T(8,128)} async-done(((f32[1024,768]{1,0:T(8,128)}), f32[128,768]{1,0:T(8,128)}) %reduce-scatter.5.cloned.1.call-update) | async-done | bytes 393232 | tf_op jit(solution)/shard_map/reduce_scatter | solution.py:298
  (235 shorter events, 173.2 us)
Async XLA Ops:
  7.2 54.0 %copy-start.30 = (s32[8]{0:T(128)S(1)}, s32[8]{0:T(128)}, u32[]{:S(2)}) copy-start(s32[8]{0:T(128)} %param.32) | copy-start | bytes 100
  7.2 54.9 %copy-start.15 = (bf16[256,128]{1,0:T(8,128)(2,1)S(1)}, bf16[256,128]{1,0:T(8,128)(2,1)}, u32[]{:S(2)}) copy-start(bf16[256,128]{1,0:T(8,128)(2,1)} %param.25) | copy-start | bytes 196612
  7.2 49.7 %all-gather.12.cloned.1.call-start = ((), (), s32[]{:S(2)}) async-start(), calls=%async_computation.4 | async-start | bytes 1769472 | tf_op jit(solution)/shard_map/all_gather | solution.py:83
  7.9 94.0 %all-gather.16.cloned.1.call-start = ((), (), s32[]{:S(2)}) async-start(), calls=%async_computation.6 | async-start | bytes 1179648 | tf_op jit(solution)/shard_map/all_gather | solution.py:165
  30.3 26.6 %copy-start.16 = (f32[8,1,128]{2,1,0:T(1,128)}, f32[8,1,128]{2,1,0:T(1,128)S(1)}, u32[]{:S(2)}) copy-start(f32[8,1,128]{2,1,0:T(1,128)S(1)} %convert_element_type.166) | copy-start | bytes 12292
  46.7 10.2 %copy-start.25 = (f32[8,1,128]{2,1,0:T(1,128)}, f32[8,1,128]{2,1,0:T(1,128)S(1)}, u32[]{:S(2)}) copy-start(f32[8,1,128]{2,1,0:T(1,128)S(1)} %convert_element_type.167) | copy-start | bytes 12292
  60.3 83.1 %all-gather.14.cloned.1.call-start = ((), (), s32[]{:S(2)}) async-start(), calls=%async_computation.5 | async-start | bytes 1179648 | tf_op jit(solution)/shard_map/all_gather | solution.py:164
  61.2 143.7 %all-reduce.10.cloned.1.call-start = ((), (), s32[]{:S(2)}) async-start(), calls=%async_computation.7 | async-start | bytes 2097152 | tf_op jit(solution)/shard_map/psum | solution.py:172
  164.6 40.3 %copy-start = (f32[256,1024]{1,0:T(8,128)S(1)}, f32[256,1024]{1,0:T(8,128)}, u32[]{:S(2)}) copy-start(f32[256,1024]{1,0:T(8,128)} %param.23) | copy-start | bytes 3145732
  167.7 86.8 %all-gather.18.cloned.1.call-start = ((), (), s32[]{:S(2)}) async-start(), calls=%async_computation.8 | async-start | bytes 2359296 | tf_op jit(solution)/shard_map/all_gather | solution.py:84
  168.3 137.9 %all-gather.20.cloned.1.call-start = ((), (), s32[]{:S(2)}) async-start(), calls=%async_computation.9 | async-start | bytes 2359296 | tf_op jit(solution)/shard_map/all_gather | solution.py:86
  168.8 177.6 %all-reduce.12.cloned.1.call-start = ((), (), s32[]{:S(2)}) async-start(), calls=%async_computation.10 | async-start | bytes 2097152 | tf_op jit(solution)/shard_map/psum | solution.py:188
  206.3 99.9 %copy-start.8 = (f32[256,1024]{1,0:T(8,128)S(1)}, f32[256,1024]{1,0:T(8,128)}, u32[]{:S(2)}) copy-start(f32[256,1024]{1,0:T(8,128)} %param.33) | copy-start | bytes 3145732
  310.3 36.2 %copy-start.3 = (f32[256,1024]{1,0:T(8,128)S(1)}, f32[256,1024]{1,0:T(8,128)}, u32[]{:S(2)}) copy-start(f32[256,1024]{1,0:T(8,128)} %copy-done.2) | copy-start | bytes 3145732
  312.0 76.4 %all-gather.22.cloned.1.call-start = ((), (), s32[]{:S(2)}) async-start(), calls=%async_computation.11 | async-start | bytes 1179648 | tf_op jit(solution)/shard_map/all_gather | solution.py:283
  312.8 174.8 %all-gather.24.cloned.1.call-start = ((), (), s32[]{:S(2)}) async-start(), calls=%async_computation.12 | async-start | bytes 1179648 | tf_op jit(solution)/shard_map/all_gather | solution.py:284
  353.4 215.6 %all-reduce.14.cloned.1.call-start = ((), (), s32[]{:S(2)}) async-start(), calls=%async_computation.17 | async-start | bytes 2097152 | tf_op jit(solution)/shard_map/psum | solution.py:179
  533.9 103.8 %reduce-scatter.7.cloned.1.call-start = ((), (), s32[]{:S(2)}) async-start(), calls=%async_computation.14 | async-start | bytes 1179648 | tf_op jit(solution)/shard_map/reduce_scatter | solution.py:299
  535.3 193.4 %reduce-scatter.9.cloned.1.call-start = ((), (), s32[]{:S(2)}) async-start(), calls=%async_computation.15 | async-start | bytes 4718592 | tf_op jit(solution)/shard_map/reduce_scatter | solution.py:300
  538.3 283.4 %reduce-scatter.11.cloned.1.call-start = ((), (), s32[]{:S(2)}) async-start(), calls=%async_computation.16 | async-start | bytes 4718592 | tf_op jit(solution)/shard_map/reduce_scatter | solution.py:301
  543.0 27.5 %copy-start.23 = (f32[1024]{0:T(1024)S(1)}, f32[1024]{0:T(1024)}, u32[]{:S(2)}) copy-start(f32[1024]{0:T(1024)} %get-tuple-element.1254) | copy-start | bytes 12292
  543.0 27.5 %copy-start.24 = (f32[1024]{0:T(1024)S(1)}, f32[1024]{0:T(1024)}, u32[]{:S(2)}) copy-start(f32[1024]{0:T(1024)} %get-tuple-element.1259) | copy-start | bytes 12292
  543.0 356.6 %reduce-scatter.5.cloned.1.call-start = ((), (), s32[]{:S(2)}) async-start(), calls=%async_computation.13 | async-start | bytes 3538944 | tf_op jit(solution)/shard_map/reduce_scatter | solution.py:298
  546.2 66.0 %copy-start.28 = (f32[256]{0:T(256)S(1)}, f32[256]{0:T(256)}, u32[]{:S(2)}) copy-start(f32[256]{0:T(256)} %copy-done.27) | copy-start | bytes 3076
  (22 other events, 105.4 us)
Sparse Core Ops, SparseCore 0:
  10.2 46.6 all-gather.11
  60.4 41.4 all-gather.15
  104.6 38.7 all-gather.13
  167.8 34.8 all-reduce.9
  204.9 49.5 all-gather.17
  256.6 49.5 all-gather.19
  312.2 34.2 all-reduce.11
  348.5 39.8 all-gather.21
  390.5 38.5 all-gather.23
  534.0 34.9 all-reduce.13
  573.3 64.3 reduce-scatter.6
  641.8 86.8 reduce-scatter.8
  733.3 88.2 reduce-scatter.10
  825.6 73.9 reduce-scatter.4
where the time goes:
time: 907 us; the launch traced here: 906 us
  waiting for transfers between devices  529 us (58%)
  blocking collectives  205 us (23%)
  matrix products  80.5 us (9%)
  local copies, waits for them, and re-layouts  29.3 us (3%)
  other arithmetic  26.7 us (3%)
  loops' own time  19.7 us (2%)
  between operations  15.1 us (2%)
    reduce_scatter x1, waiting for transfers between devices, on_device(): lax.psum_scatter(grad_down, 'dp', scatter_dimension=1, tiled=True)  92.9 us
    reduce_scatter x1, waiting for transfers between devices, on_device(): lax.psum_scatter(grad_up, 'dp', scatter_dimension=0, tiled=True)  91 us
    reduce_scatter x1, waiting for transfers between devices, on_device(): lax.psum_scatter(grad_qkv, 'dp', scatter_dimension=0, tiled=True)  78 us
    all_gather x1, waiting for transfers between devices, on_device(): lax.all_gather(w_down, 'dp', axis=1, tiled=True)  48 us
    all_gather x1, waiting for transfers between devices, on_device(): lax.all_gather(w_up, 'dp', axis=0, tiled=True)  46.5 us
    all_gather x1, waiting for transfers between devices, on_device(): lax.all_gather(keys_flat, 'dp', axis=0, tiled=True)  40.2 us
    unnamed x1, blocking collectives  37.3 us
    all_gather x1, waiting for transfers between devices, on_device(): lax.all_gather(query_flat, 'dp', axis=0, tiled=True)  35 us
  transfers between devices with their start and end apart: 14, of which 12 were waited for; matrix products, arithmetic and copies ran while one was open for 8% of the time, Pallas kernels for 0%

commit v1 on v0

v1 whole, which is shorter than its diff:
```python
import functools

import jax
import jax.numpy as jnp
from jax import lax
from jax.experimental import pallas as pl
from jax.experimental.pallas import tpu as pltpu
from jax.sharding import PartitionSpec as P

HEAD_DIM = 64
LANES = 128
FAR = -1e30
MESH = pl.DeviceIdType.MESH
bf16 = jnp.bfloat16
f32 = jnp.float32


def nn(a, b):
    return lax.dot_general(a, b, (((1,), (0,)), ((), ())), preferred_element_type=f32)


def nt(a, b):
    return lax.dot_general(a, b, (((1,), (1,)), ((), ())), preferred_element_type=f32)


class Plan:
    def __init__(self, tokens, w_qkv, w_up, scenes, dp, mp):
        self.R, self.M = dp, mp
        self.tl, self.D = tokens.shape
        self.rb = self.D // dp
        self.L = dp // 2
        self.H = w_qkv.shape[1] // (3 * HEAD_DIM)
        self.g = dp // self.H
        self.U = w_up.shape[1]
        self.rm = self.tl // mp
        self.HF = self.H * HEAD_DIM
        self.scenes = scenes.shape[0]
        self.NQ = self.H * self.tl
        self.keep = dp * self.tl <= 4096
        widths = (LANES, 3 * self.HF, self.HF, self.U, self.U)
        self.cols = []
        start = 0
        for width in widths:
            self.cols.append((start, width))
            start += width
        self.WC = start
        self.gw = (self.U, self.U, self.HF, LANES, 3 * self.HF, LANES)


def kernel(p, names, *refs):
    r = dict(zip(names, refs))
    R, M, L, H, g = p.R, p.M, p.L, p.H, p.g
    tl, D, rb, rm, U, HF, NQ = p.tl, p.D, p.rb, p.rm, p.U, p.HF, p.NQ
    half = tl // 2
    d = lax.axis_index("dp")
    m = lax.axis_index("mp")
    z, x = d // 2, lax.rem(d, 2)
    dh, di = d // g, lax.rem(d, g)
    sent = []

    def add(a, k, n):
        return lax.rem(a + k, n)

    def copy(src, dst, name, index, peer):
        return pltpu.make_async_remote_copy(
            src_ref=src,
            dst_ref=dst,
            send_sem=r[name + "_s"].at[index],
            recv_sem=r[name + "_r"].at[index],
            device_id=peer,
            device_id_type=MESH,
        )

    def send(src, dst, name, index, peer):
        one = copy(src, dst, name, index, peer)
        one.start()
        sent.append(one)

    def arrive(dst, name, index, peer):
        copy(dst, dst, name, index, peer).wait_recv()

    pair = (d + 1 - 2 * x, m)

    def line(k):
        return (add(z, k, L) * 2 + x, m)

    def row_peer(k):
        return (d, add(m, k, M))

    W = r["W"]
    local = [
        pltpu.make_async_copy(r["tokens"], r["tok"], r["loc"].at[0]),
        pltpu.make_async_copy(r["grad_out"], r["go"], r["loc"].at[1]),
        pltpu.make_async_copy(r["wblk"], W.at[d], r["loc"].at[2]),
    ]
    for one in local:
        one.start()

    barrier = pltpu.get_barrier_semaphore()
    for k in range(1, R):
        pl.semaphore_signal(barrier, 1, device_id=(add(d, k, R), m), device_id_type=MESH)
    for k in range(1, M):
        pl.semaphore_signal(barrier, 1, device_id=row_peer(k), device_id_type=MESH)
    pl.semaphore_wait(barrier, R - 1 + M - 1)

    def wcols(b, s):
        c0, width = p.cols[s]
        return W.at[b, :, pl.ds(c0, width)]

    def weights_start(s):
        for k in range(1, L):
            send(wcols(d, s), wcols(d, s), "wz", (s, k - 1), line(k))
        send(wcols(d, s), wcols(d, s), "wx", (s, 0), pair)

    def weights_relay(s):
        for k in range(1, L):
            b = add(z, L - k, L) * 2 + x
            arrive(wcols(b, s), "wz", (s, k - 1), line(L - k))
            send(wcols(b, s), wcols(b, s), "wx", (s, k), pair)

    def weights_end(s):
        for k in range(L):
            b = add(z, L - k, L) * 2 + 1 - x
            arrive(wcols(b, s), "wx", (s, k), pair)

    def weight(s, first=0, width=None):
        c0, full = p.cols[s]
        width = full if width is None else width
        return W[:, :, pl.ds(c0 + first, width)].reshape(D, width)

    local[2].wait()
    for s in range(5):
        weights_start(s)
    local[0].wait()
    local[1].wait()

    def transposed(src_ref, dst_ref, rows, chunk):
        for c in range(rows // chunk):
            part = src_ref[pl.ds(c * chunk, chunk), :].astype(f32)
            dst_ref[:, :, :, pl.ds(c * chunk, chunk)] = (
                part.T.astype(bf16).reshape(L, 2, rb, chunk)
            )

    outlow = r["outlow"]
    outlow[...] = r["go"][...].astype(bf16)

    weights_relay(0)
    weights_end(0)
    lnp = r["lnp"]
    lnp[...] = weight(0).astype(f32).T[0:8, :]
    gain1, bias1, gain2, bias2 = (lnp[pl.ds(k, 1), :] for k in range(4))

    def norm(values):
        center = values - jnp.mean(values, axis=-1, keepdims=True)
        inverse = lax.rsqrt(jnp.mean(center * center, axis=-1, keepdims=True) + 1e-05)
        return center * inverse, inverse

    def norm_back(upstream, normed, inverse, gain):
        scaled = upstream * gain
        return inverse * (
            scaled
            - jnp.mean(scaled, axis=-1, keepdims=True)
            - normed * jnp.mean(scaled * normed, axis=-1, keepdims=True)
        )

    h1 = r["h1"]

    @pl.loop(0, tl // 32)
    def _(c):
        rows = pl.ds(pl.multiple_of(c * 32, 32), 32)
        n1, _ = norm(r["tok"][rows, :])
        h1[rows, :] = (n1 * gain1 + bias1).astype(bf16)

    weights_relay(1)
    weights_end(1)

    lane = lax.broadcasted_iota(jnp.int32, (1, LANES), 1)
    low = lane < HEAD_DIM

    def swap(v):
        return pltpu.roll(v, HEAD_DIM, 1)

    qs, kvs, qin, KV = r["qs"], r["kvs"], r["qin"], r["KV"]
    for t in range(H // 2):
        mixed = nn(h1[...], weight(1, 6 * HEAD_DIM * t, 6 * HEAD_DIM))
        t0, t1, t2 = (mixed[:, k * LANES : (k + 1) * LANES] for k in range(3))
        q_even, q_odd = t0 * 0.125, swap(t1) * 0.125
        for h, q in ((2 * t, q_even), (2 * t + 1, q_odd)):
            qs[h] = jnp.where(low, q[:half], swap(q[half:])).astype(bf16)
        kvs[2 * t] = jnp.where(low, swap(t0), swap(t1)).astype(bf16)
        kvs[2 * t + 1] = t2.astype(bf16)

    def head_dev(h, member):
        return (h * g + member, m)

    for k in range(1, H):
        h = add(dh, k, H)
        peer = head_dev(h, di)
        send(kvs.at[h], KV.at[d], "kv", k, peer)
        send(qs.at[h], qin.at[dh], "q", k, peer)
    KV[d] = kvs[dh]
    qin[dh] = qs[dh]
    for k in range(H):
        j = add(dh, H - k, H)
        own = j * g + di
        if k:
            arrive(KV.at[own], "kv", k, head_dev(j, di))
        for q in range(1, g):
            send(KV.at[own], KV.at[own], "kvx", (k, q - 1), head_dev(dh, add(di, q, g)))
    for k in range(1, H):
        j = add(dh, H - k, H)
        arrive(qin.at[j], "q", k, head_dev(j, di))
    for k in range(H):
        j = add(dh, H - k, H)
        for q in range(1, g):
            member = add(di, g - q, g)
            arrive(KV.at[j * g + member], "kvx", (k, q - 1), head_dev(dh, member))

    qall, KVT = r["qall"], r["KVT"]
    for j in range(H):
        packed = qin[j].astype(f32)
        qall[pl.ds(j * tl, half), :] = jnp.where(low, packed, 0.0).astype(bf16)
        qall[pl.ds(j * tl + half, half), :] = jnp.where(low, swap(packed), 0.0).astype(bf16)

    ends = []
    total = 0
    for k in range(p.scenes):
        total = total + r["scene"][k]
        ends.append(total)

    def scene_of(pos):
        count = jnp.zeros(pos.shape, jnp.int32)
        for end in ends:
            count = count + (pos >= end).astype(jnp.int32)
        return count

    token_lane = lax.broadcasted_iota(jnp.int32, (1, tl), 1)
    q_scene = jnp.concatenate(
        [scene_of((j * g + di) * tl + token_lane) for j in range(H)], axis=1
    )
    token_row = lax.broadcasted_iota(jnp.int32, (tl, 1), 0)

    def masked_scores(o):
        scores = nt(KV[o], qall[...])
        return jnp.where(scene_of(o * tl + token_row) == q_scene, scores, FAR)

    unit = (
        lax.broadcasted_iota(jnp.int32, (LANES, LANES), 0)
        == lax.broadcasted_iota(jnp.int32, (LANES, LANES), 1)
    ).astype(bf16)

    top8, sum8, acc = r["top8"], r["sum8"], r["acc"]
    top8[...] = jnp.full((8, NQ), FAR, f32)
    sum8[...] = jnp.zeros((8, NQ), f32)
    acc[...] = jnp.zeros((LANES, NQ), f32)

    @pl.loop(0, R)
    def _(o):
        KVT[o] = nt(unit, KV[o]).astype(bf16)
        top8[...] = jnp.maximum(
            top8[...], jnp.max(masked_scores(o).reshape(tl // 8, 8, NQ), axis=0)
        )

    top = r["top"]
    top[...] = jnp.max(top8[...], axis=0, keepdims=True)

    @pl.loop(0, R)
    def _(o):
        expo = jnp.exp(masked_scores(o) - top[...])
        sum8[...] += jnp.sum(expo.reshape(tl // 8, 8, NQ), axis=0)
        low_expo = expo.astype(bf16)
        if p.keep:
            r["prob"][o] = low_expo
        acc[...] += nn(KVT[o], low_expo)

    scale_row = 1.0 / jnp.sum(sum8[...], axis=0, keepdims=True)
    inv = r["inv"]
    inv[...] = scale_row
    attf, atts, attT = r["attf"], r["atts"], r["attT"]
    attf[...] = acc[pl.ds(HEAD_DIM, HEAD_DIM), :] * scale_row
    for j in range(H):
        atts[j] = attf[:, pl.ds(j * tl, tl)].astype(bf16)
    for k in range(1, H):
        j = add(dh, k, H)
        send(atts.at[j], attT.at[dh], "att", k, head_dev(j, di))
    attT[dh] = atts[dh]
    for k in range(1, H):
        h = add(dh, H - k, H)
        arrive(attT.at[h], "att", k, head_dev(h, di))
    att = r["att"]
    att[...] = attT[...].reshape(HF, tl).astype(f32).T.astype(bf16)

    rs_send, rs_recv = r["rs_send"], r["rs_recv"]

    def rows_send(n, values):
        rs_send[n] = values.astype(bf16).reshape(M, rm, D)
        for k in range(1, M):
            send(rs_send.at[n, add(m, k, M)], rs_recv.at[n, k - 1], "rs", (n, k - 1), row_peer(k))

    def rows_sum(n):
        value = rs_send[n, m].astype(f32)
        for k in range(1, M):
            arrive(rs_recv.at[n, k - 1], "rs", (n, k - 1), row_peer(M - k))
            value = value + rs_recv[n, k - 1].astype(f32)
        return value

    def gather_send(n, ref):
        for k in range(1, M):
            send(ref.at[m], ref.at[m], "ag", (n, k - 1), row_peer(k))

    def gather_end(n, ref):
        for k in range(1, M):
            b = add(m, M - k, M)
            arrive(ref.at[b], "ag", (n, k - 1), row_peer(M - k))

    weights_relay(2)
    weights_end(2)
    rows_send(0, nt(att[...], weight(2)))
    transposed(r["go"], r["outT"], tl, LANES)
    transposed(h1, r["h1T"], tl, LANES)

    own_rows = pl.ds(pl.multiple_of(m * rm, rm), rm)
    mid, n2, r2, h2 = r["mid"], r["n2"], r["r2"], r["h2"]
    middle = r["tok"][own_rows, :] + rows_sum(0)
    mid[...] = middle
    normed, inverse = norm(middle)
    n2[...] = normed
    r2[...] = jnp.broadcast_to(inverse, (rm, LANES))
    h2[m] = (normed * gain2 + bias2).astype(bf16)
    gather_send(0, h2)
    weights_relay(3)
    weights_relay(4)
    weights_end(3)
    weights_end(4)
    gather_end(0, h2)

    active, il = r["active"], r["il"]
    c_one, c_two = 0.7978845608028654, 0.044715
    step = 256
    for c in range(U // step):
        inner = nn(h2[...].reshape(tl, D), weight(3, c * step, step))
        dact = nn(outlow[...], weight(4, c * step, step))
        square = inner * inner
        t = jnp.tanh(c_one * inner * (1.0 + c_two * square))
        cdf = 0.5 * (1.0 + t)
        active[:, pl.ds(c * step, step)] = (inner * cdf).astype(bf16)
        slope = cdf + 0.5 * inner * (1.0 - t * t) * (c_one + 3.0 * c_one * c_two * square)
        il[:, pl.ds(c * step, step)] = (dact * slope).astype(bf16)

    rows_send(1, nt(il[...], weight(3)))
    rows_send(2, nt(active[...], weight(4)))

    def grad_x(s, others):
        value = others()
        width = p.gw[s]
        r["gxs%d" % s][...] = value.astype(bf16).reshape(L, rb, width)
        for k in range(L):
            l = add(z, k, L)
            send(r["gxs%d" % s].at[l], r["gxr%d" % s].at[l], "gx", (s, k), pair)

    def grad_z(s, mine, out):
        for k in [*range(1, L), 0]:
            l = add(z, k, L)
            arrive(r["gxr%d" % s].at[l], "gx", (s, k), pair)
            value = mine(l) + r["gxr%d" % s][l].astype(f32)
            if k:
                r["gzs%d" % s][k - 1] = value.astype(bf16)
                send(r["gzs%d" % s].at[k - 1], r["gzr%d" % s].at[k - 1], "gz", (s, k - 1), line(k))
            else:
                out[...] = value

    def grad_end(s, out):
        for k in range(1, L):
            arrive(r["gzr%d" % s].at[k - 1], "gz", (s, k - 1), line(L - k))
            out[...] += r["gzr%d" % s][k - 1].astype(f32)

    def others(lhs, rhs):
        return lambda: nn(lhs[:, 1 - x].reshape(L * rb, tl), rhs[...])

    def mine(lhs, rhs):
        return lambda l: nn(lhs[l, x], rhs[...])

    outT, h1T, h2T, midT = r["outT"], r["h1T"], r["h2T"], r["midT"]
    for k in range(M // 2):
        part = h2[pl.ds(2 * k, 2)].reshape(2 * rm, D).astype(f32)
        h2T[:, :, :, pl.ds(2 * k * rm, 2 * rm)] = part.T.astype(bf16).reshape(L, 2, rb, 2 * rm)

    grad_x(0, others(outT, active))
    grad_x(1, others(h2T, il))

    back2 = rows_sum(1)
    gm, ml = r["gm"], r["ml"]
    grad_middle = r["go"][own_rows, :] + norm_back(back2, n2[...], r2[:, 0:1], gain2)
    gm[...] = grad_middle
    ml[m] = grad_middle.astype(bf16)
    gather_send(1, ml)

    col = lax.broadcasted_iota(jnp.int32, (rm, LANES), 1)

    def norm_columns(upstream, normed, c):
        gain_part = (upstream * normed).T.astype(bf16)
        bias_part = upstream.T.astype(bf16)
        value = nn(gain_part, (col == c).astype(bf16)) + nn(bias_part, (col == c + 1).astype(bf16))
        return value.reshape(L, 2, rb, LANES)

    ln2c, ln1c = r["ln2c"], r["ln1c"]
    ln2c[...] = norm_columns(back2, n2[...], 0)

    gather_end(1, ml)
    midlow = ml[...].reshape(tl, D)

    gs, gin, gall = r["gs"], r["gin"], r["gall"]
    gatt = nn(midlow, weight(2))
    for h in range(H):
        tile = gatt[:, (h // 2) * LANES : (h // 2 + 1) * LANES]
        even = h % 2 == 0
        first = tile[:half] if even else swap(tile[:half])
        second = swap(tile[half:]) if even else tile[half:]
        gs[h] = jnp.where(low, first, second).astype(bf16)
    for k in range(1, H):
        h = add(dh, k, H)
        send(gs.at[h], gin.at[dh], "ga", k, head_dev(h, di))
    gin[dh] = gs[dh]

    for k in range(M // 2):
        part = ml[pl.ds(2 * k, 2)].reshape(2 * rm, D).astype(f32)
        midT[:, :, :, pl.ds(2 * k * rm, 2 * rm)] = part.T.astype(bf16).reshape(L, 2, rb, 2 * rm)
    grad_x(2, others(midT, att))
    grad_x(3, lambda: ln2c[:, 1 - x].reshape(L * rb, LANES))
    for k in range(1, H):
        j = add(dh, H - k, H)
        arrive(gin.at[j], "ga", k, head_dev(j, di))

    inv_col = jnp.broadcast_to(inv[...], (LANES, NQ)).T
    shift_parts = []
    for j in range(H):
        packed = gin[j].astype(f32)
        top_half = jnp.where(low, 0.0, swap(packed))
        bottom = jnp.where(low, 0.0, packed)
        ga = jnp.concatenate([top_half, bottom], axis=0)
        gaT = ga.T[HEAD_DIM:, :]
        shift_parts.append(
            jnp.sum(gaT * attf[:, pl.ds(j * tl, tl)], axis=0, keepdims=True)
            * inv[:, pl.ds(j * tl, tl)]
        )
        gall[pl.ds(j * tl, tl), :] = (ga * inv_col[j * tl : (j + 1) * tl]).astype(bf16)
    shift = r["shift"]
    shift[...] = jnp.concatenate(shift_parts, axis=1)

    acc[...] = jnp.zeros((LANES, NQ), f32)
    dkvs, dkv_in = r["dkvs"], r["dkv_in"]

    for k in [*range(1, R), 0]:
        o = add(d, k, R)
        prob = r["prob"][o] if p.keep else jnp.exp(masked_scores(o) - top[...]).astype(bf16)
        dprob = nt(KV[o], gall[...])
        dscore = (prob.astype(f32) * (dprob - shift[...])).astype(bf16)
        acc[...] += nn(KVT[o], dscore)
        dkv = nn(dscore, qall[...]) + nn(prob, gall[...])
        if k:
            dkvs[k] = dkv.astype(bf16)
            send(dkvs.at[k], dkv_in.at[d], "dkv", k, (o, m))
        else:
            dkv_in[d] = dkv.astype(bf16)

    dqs, dqT = r["dqs"], r["dqT"]
    for j in range(H):
        dqs[j] = (acc[pl.ds(0, HEAD_DIM), pl.ds(j * tl, tl)] * 0.125).astype(bf16)
    for k in range(1, H):
        j = add(dh, k, H)
        send(dqs.at[j], dqT.at[dh], "dq", k, head_dev(j, di))
    dqT[dh] = dqs[dh]

    res = r["res"]
    res[m] = (mid[...] + rows_sum(2)).astype(bf16)
    gather_send(2, res)

    grad_z(0, mine(outT, active), r["o_down"])
    grad_z(1, mine(h2T, il), r["o_up"])
    grad_z(2, mine(midT, att), r["o_out"])
    lnsum = r["lnsum"]
    grad_z(3, lambda l: ln2c[l, x], lnsum.at[0])

    for k in range(1, H):
        h = add(dh, H - k, H)
        arrive(dqT.at[h], "dq", k, head_dev(h, di))
    for k in range(1, R):
        o = add(d, R - k, R)
        arrive(dkv_in.at[o], "dkv", k, (o, m))

    gmix = r["gmix"]
    dq = dqT[...].reshape(HF, tl).astype(f32).T

    def head_sum(h):
        value = dkv_in[h * g].astype(f32)
        for q in range(1, g):
            value = value + dkv_in[h * g + q].astype(f32)
        return value

    for t in range(H // 2):
        both = dq[:, t * LANES : (t + 1) * LANES]
        even = swap(head_sum(2 * t))
        base = 6 * HEAD_DIM * t
        gmix[:, pl.ds(base, LANES)] = jnp.where(low, both, even).astype(bf16)
        gmix[:, pl.ds(base + LANES, LANES)] = jnp.where(low, even, both).astype(bf16)
        gmix[:, pl.ds(base + 2 * LANES, LANES)] = head_sum(2 * t + 1).astype(bf16)

    grad_x(4, others(h1T, gmix))
    rows_send(3, nt(gmix[...], weight(1)))

    back1 = rows_sum(3)
    n1, r1 = norm(r["tok"][own_rows, :])
    gt = r["gt"]
    gt[m] = (gm[...] + norm_back(back1, n1, r1, gain1)).astype(bf16)
    gather_send(3, gt)
    ln1c[...] = norm_columns(back1, n1, 2)
    grad_x(5, lambda: ln1c[:, 1 - x].reshape(L * rb, LANES))
    grad_z(5, lambda l: ln1c[l, x], lnsum.at[1])
    grad_z(4, mine(h1T, gmix), r["o_qkv"])

    grad_end(3, lnsum.at[0])
    grad_end(5, lnsum.at[1])
    lnx = r["lnx"]
    both = lnsum[0] + lnsum[1]
    if rb < LANES:
        both = jnp.concatenate([both, jnp.zeros((LANES - rb, LANES), f32)], axis=0)
    lnx[m] = both.T[0:8, :]
    for k in range(1, M):
        send(lnx.at[m], lnx.at[m], "ln", k - 1, row_peer(k))

    gather_end(2, res)
    r["o_result"][...] = res[...].reshape(tl, D).astype(f32)
    grad_end(0, r["o_down"])
    grad_end(1, r["o_up"])
    grad_end(2, r["o_out"])
    gather_end(3, gt)
    r["o_tokens"][...] = gt[...].reshape(tl, D).astype(f32)
    for k in range(1, M):
        arrive(lnx.at[add(m, M - k, M)], "ln", k - 1, row_peer(M - k))
    value = lnx[0]
    for k in range(1, M):
        value = value + lnx[k]
    r["o_ln"][...] = value
    grad_end(4, r["o_qkv"])
    for one in sent:
        one.wait_send()


def layer(p, tokens, grad_out, wblk, scene):
    R, M, L, H, g = p.R, p.M, p.L, p.H, p.g
    tl, D, rb, rm, U, HF, NQ = p.tl, p.D, p.rb, p.rm, p.U, p.HF, p.NQ
    half = tl // 2
    ins = {"tokens": tokens, "grad_out": grad_out, "wblk": wblk, "scene": scene}
    outs = {
        "o_result": (tl, D),
        "o_tokens": (tl, D),
        "o_qkv": (rb, 3 * HF),
        "o_out": (rb, HF),
        "o_up": (rb, U),
        "o_down": (rb, U),
        "o_ln": (8, max(rb, LANES)),
    }
    v = pltpu.VMEM
    scratch = {
        "W": v((R, rb, p.WC), bf16),
        "tok": v((tl, D), f32),
        "go": v((tl, D), f32),
        "outlow": v((tl, D), bf16),
        "lnp": v((8, D), f32),
        "h1": v((tl, D), bf16),
        "qs": v((H, half, LANES), bf16),
        "kvs": v((H, tl, LANES), bf16),
        "qin": v((H, half, LANES), bf16),
        "KV": v((R, tl, LANES), bf16),
        "KVT": v((R, LANES, tl), bf16),
        "qall": v((NQ, LANES), bf16),
        "top8": v((8, NQ), f32),
        "sum8": v((8, NQ), f32),
        "top": v((1, NQ), f32),
        "inv": v((1, NQ), f32),
        "shift": v((1, NQ), f32),
        "acc": v((LANES, NQ), f32),
        "attf": v((HEAD_DIM, NQ), f32),
        "atts": v((H, HEAD_DIM, tl), bf16),
        "attT": v((H, HEAD_DIM, tl), bf16),
        "att": v((tl, HF), bf16),
        "rs_send": v((4, M, rm, D), bf16),
        "rs_recv": v((4, M - 1, rm, D), bf16),
        "mid": v((rm, D), f32),
        "n2": v((rm, D), f32),
        "r2": v((rm, LANES), f32),
        "h2": v((M, rm, D), bf16),
        "active": v((tl, U), bf16),
        "il": v((tl, U), bf16),
        "outT": v((L, 2, rb, tl), bf16),
        "h1T": v((L, 2, rb, tl), bf16),
        "h2T": v((L, 2, rb, tl), bf16),
        "midT": v((L, 2, rb, tl), bf16),
        "gm": v((rm, D), f32),
        "ml": v((M, rm, D), bf16),
        "ln2c": v((L, 2, rb, LANES), f32),
        "ln1c": v((L, 2, rb, LANES), f32),
        "lnsum": v((2, rb, LANES), f32),
        "lnx": v((M, 8, max(rb, LANES)), f32),
        "gs": v((H, half, LANES), bf16),
        "gin": v((H, half, LANES), bf16),
        "gall": v((NQ, LANES), bf16),
        "dkvs": v((R, tl, LANES), bf16),
        "dkv_in": v((R, tl, LANES), bf16),
        "dqs": v((H, HEAD_DIM, tl), bf16),
        "dqT": v((H, HEAD_DIM, tl), bf16),
        "gmix": v((tl, 3 * HF), bf16),
        "res": v((M, rm, D), bf16),
        "gt": v((M, rm, D), bf16),
    }
    if p.keep:
        scratch["prob"] = v((R, tl, NQ), bf16)
    for s, width in enumerate(p.gw):
        scratch["gxs%d" % s] = v((L, rb, width), bf16)
        scratch["gxr%d" % s] = v((L, rb, width), bf16)
        scratch["gzs%d" % s] = v((L - 1, rb, width), bf16)
        scratch["gzr%d" % s] = v((L - 1, rb, width), bf16)
    sems = {
        "wz": (5, L - 1),
        "wx": (5, L),
        "kv": (H,),
        "q": (H,),
        "kvx": (H, max(g - 1, 1)),
        "att": (H,),
        "rs": (4, M - 1),
        "ag": (4, M - 1),
        "gx": (6, L),
        "gz": (6, L - 1),
        "ga": (H,),
        "dkv": (R,),
        "dq": (H,),
        "ln": (M - 1,),
    }
    for name, shape in sems.items():
        scratch[name + "_s"] = pltpu.SemaphoreType.DMA(shape)
        scratch[name + "_r"] = pltpu.SemaphoreType.DMA(shape)
    scratch["loc"] = pltpu.SemaphoreType.DMA((3,))
    names = (*ins, *outs, *scratch)
    any_spec = pl.BlockSpec(memory_space=pl.ANY)
    flops = 6 * tl * D * p.WC + 14 * NQ * R * tl * HEAD_DIM
    return pl.pallas_call(
        functools.partial(kernel, p, names),
        out_shape=[jax.ShapeDtypeStruct(shape, f32) for shape in outs.values()],
        in_specs=[any_spec, any_spec, any_spec, pl.BlockSpec(memory_space=pltpu.SMEM)],
        out_specs=[pl.BlockSpec(memory_space=pltpu.VMEM)] * len(outs),
        scratch_shapes=list(scratch.values()),
        compiler_params=pltpu.CompilerParams(
            collective_id=0, has_side_effects=True, vmem_limit_bytes=60 << 20
        ),
        cost_estimate=pl.CostEstimate(flops=flops, bytes_accessed=8 << 20, transcendentals=NQ * R * tl),
        name="layer",
    )(*ins.values())


def on_device(
    tokens,
    w_qkv,
    w_out,
    w_up,
    w_down,
    ln1_gain,
    ln1_bias,
    ln2_gain,
    ln2_bias,
    scene_lengths,
    grad_out,
):
    p = Plan(tokens, w_qkv, w_up, scene_lengths, lax.axis_size("dp"), lax.axis_size("mp"))
    vectors = jnp.stack([ln1_gain, ln1_bias, ln2_gain, ln2_bias], axis=1)
    vectors = jnp.pad(vectors, ((0, 0), (0, LANES - 4)))
    wblk = jnp.concatenate([vectors, w_qkv, w_out.T, w_up, w_down.T], axis=1)
    result, grad_tokens, qkv, out, up, down, ln = layer(p, tokens, grad_out, wblk, scene_lengths)
    rb = p.rb
    return (
        result,
        grad_tokens,
        qkv,
        out.T,
        up,
        down.T,
        ln[2, :rb],
        ln[3, :rb],
        ln[0, :rb],
        ln[1, :rb],
    )


def solution(mesh):
    weights = (P("dp", "mp"), P("mp", "dp"), P("dp", "mp"), P("mp", "dp"))
    rows = P("dp", None)
    vector = P("dp")
    return jax.shard_map(
        on_device,
        mesh=mesh,
        in_specs=(rows, *weights, vector, vector, vector, vector, P(), rows),
        out_specs=(rows, rows, *weights, vector, vector, vector, vector),
        check_vma=False,
    )
```

time: 907 us -> 280 us (0.31)
  waiting for transfers between devices: 529 us -> 0 us
  Pallas kernels: 0 us -> 263 us
  blocking collectives: 205 us -> 0 us
  matrix products: 80.5 us -> 0 us
  other arithmetic: 26.7 us -> 0.01 us
  loops' own time: 19.7 us -> 0 us
  local copies, waits for them, and re-layouts: 29.3 us -> 13.8 us
  between operations: 15.1 us -> 0.79 us
    reduce_scatter x4 -> x0, waiting for transfers between devices: 285 us -> none  [the longest x1 92.9 us: on_device(): lax.psum_scatter(grad_down, 'dp', scatter_dimension=1, tiled=True)]
    pallas_call x0 -> x1, Pallas kernels: none -> 263 us  [layer(): pl.pallas_call(functools.partial(kernel, p, names), out_shape=[jax.ShapeD...]
    all_gather x7 -> x0, waiting for transfers between devices: 188 us -> none  [the longest x1 48 us: on_device(): lax.all_gather(w_down, 'dp', axis=1, tiled=True)]
    all_gather x7 -> x0, blocking collectives: 167 us -> none  [the longest x1 32.4 us: on_device(): lax.all_gather(shift_term.T, 'dp', axis=0, tiled=True)]
    dot_general x26 -> x0, matrix products: 80.5 us -> none  [the longest x4 11.7 us: rows_product(): lax.dot_general(left, right, (((0,), (0,)), ((), ())), preferred_element_...]
    psum x3 -> x0, waiting for transfers between devices: 54.3 us -> none  [the longest x1 33.5 us: on_device(): back_two = lax.psum(cols_product(inner_low, full_up), 'mp')]
    unnamed x1 -> x0, blocking collectives: 37.3 us -> none
    another operation x9 -> x0, loops' own time: 19.7 us -> none  [the longest x3 19.3 us: over_blocks(): lax.scan(visit, running, (jnp.arange(block_number, dtype=jnp.int32), stac...]
  transfers between devices with their start and end apart: 14 -> 0, of which waited for: 12 -> 0; matrix products, arithmetic and copies ran while one was open for 8% -> 0% of each run, Pallas kernels for 0% -> 0%
where the time goes in v1:
time: 280 us; the launch traced here: 278 us
  Pallas kernels  263 us (94%)
  local copies, waits for them, and re-layouts  13.8 us (5%)
    pallas_call x1, Pallas kernels, layer(): pl.pallas_call(functools.partial(kernel, p, names), out_shape=[jax.ShapeD...  263 us
    unnamed x36, local copies, waits for them, and re-layouts  12.3 us

profile of v1, /device:TPU:0, one launch (start us, length us, event | category | flops | bytes accessed | tf_op | source)
XLA Modules:
  0.0 278.0 jit_solution(16787144113478506276)
XLA Ops:
  0.7 0.6 copy-done.11
  1.3 0.0 copy-done.8
  1.3 0.0 copy-done.9
  1.3 0.0 copy-done.10
  1.4 0.1 copy.29
  1.5 0.0 copy-start.6
  1.5 0.0 copy-start.4
  1.5 1.0 constant_dynamic-update-slice_fusion.1
  2.5 0.1 copy.30
  2.7 0.9 copy-done.5
  3.6 0.1 copy.31
  3.8 0.0 copy-start.7
  3.8 0.9 copy-done.7
  4.7 263.4 %layer.1 = (f32[256,1024]{1,0:T(8,128)}, f32[256,1024]{1,0:T(8,128)}, f32[128,768]{1,0:T(8,128)}, f32[128,256]{1,0:T(8,128)}, f32[128,1024]{1,0:T(8,128)}, /*index=5*/f32[128,1024]{1,0:T(8,128)}, f32[8,128]{1,0:T(8,128)}) custom-call(f32[256,1024]{1,0:T(8,128)} %refs_0_.1, f32[256,1024]{1,0:T(8,128)} %refs_1_.1, bf16[128,3200]{1,0:T(8,128)(2,1)} %copy-done.7, ...), custom_call_target="tpu_custom_call" | custom-call | flops 6912212992 | bytes 8388608 | tf_op jit(solution)/shard_map/layer/pallas_call | solution.py:646
  268.1 1.4 slice_bitcast_fusion
  269.5 2.0 copy.33
  271.5 1.7 copy.32
  273.2 1.0 copy.42
  274.2 0.6 copy-done
  274.8 1.0 copy.43
  275.8 0.3 copy-done.3
  276.0 0.7 copy.44
  276.8 0.4 copy-done.2
  277.2 0.8 copy.45
  (17 shorter events, 0.1 us)
Async XLA Ops:
  0.6 0.7 copy-start.11
  0.7 0.7 copy-start.8
  0.7 0.7 copy-start.9
  0.7 0.7 copy-start.10
  1.5 1.0 copy-start.6
  1.5 1.1 copy-start.4
  2.7 1.0 copy-start.5
  3.8 0.9 copy-start.7
  268.1 5.1 %copy-start.1 = (f32[256,1024]{1,0:T(8,128)S(1)}, f32[256,1024]{1,0:T(8,128)}, u32[]{:S(2)}) copy-start(f32[256,1024]{1,0:T(8,128)} %get-tuple-element.58) | copy-start | bytes 3145732
  273.2 1.6 copy-start
  274.8 1.2 copy-start.3
  276.0 1.2 copy-start.2

commit v2 on v1

v2 whole, which is shorter than its diff:
```python
import functools

import jax
import jax.numpy as jnp
from jax import lax
from jax.experimental import pallas as pl
from jax.experimental.pallas import tpu as pltpu
from jax.sharding import PartitionSpec as P

HEAD_DIM = 64
LANES = 128
FAR = -1e30
MESH = pl.DeviceIdType.MESH
bf16 = jnp.bfloat16
f32 = jnp.float32


def nn(a, b):
    return lax.dot_general(a, b, (((1,), (0,)), ((), ())), preferred_element_type=f32)


def nt(a, b):
    return lax.dot_general(a, b, (((1,), (1,)), ((), ())), preferred_element_type=f32)


def tn(a, b):
    return lax.dot_general(a, b, (((0,), (0,)), ((), ())), preferred_element_type=f32)


class Plan:
    def __init__(self, tokens, w_qkv, w_up, scenes, dp, mp):
        self.R, self.M = dp, mp
        self.tl, self.D = tokens.shape
        self.rb = self.D // dp
        self.L = dp // 2
        self.H = w_qkv.shape[1] // (3 * HEAD_DIM)
        self.g = dp // self.H
        self.U = w_up.shape[1]
        self.rm = self.tl // mp
        self.HF = self.H * HEAD_DIM
        self.scenes = scenes.shape[0]
        self.NQ = self.H * self.tl
        self.keep = dp * self.tl <= 4096
        self.whole_lanes = self.rb % LANES == 0
        widths = (3 * self.HF, self.HF, self.U, self.U)
        self.cols = []
        start = 0
        for width in widths:
            self.cols.append((start, width))
            start += width
        self.WC = start
        far, near = dp // 2, dp - 1 - dp // 2
        self.far = far
        self.streams = []
        for s, width in enumerate(widths):
            half = width // 2
            for first, way in ((0, 1), (half, -1)):
                self.streams.append((s, first, half, way, far))
                self.streams.append((s, first, half, -way, near))


def kernel(p, names, *refs):
    r = dict(zip(names, refs))
    R, M, L, H, g = p.R, p.M, p.L, p.H, p.g
    tl, D, rb, rm, U, HF, NQ = p.tl, p.D, p.rb, p.rm, p.U, p.HF, p.NQ
    half = tl // 2
    d = lax.axis_index("dp")
    m = lax.axis_index("mp")
    z, x = d // 2, lax.rem(d, 2)
    dh, di = d // g, lax.rem(d, g)
    sent = []

    def add(a, k, n):
        return lax.rem(a + k, n)

    def copy(src, dst, name, index, peer):
        return pltpu.make_async_remote_copy(
            src_ref=src,
            dst_ref=dst,
            send_sem=r[name + "_s"].at[index],
            recv_sem=r[name + "_r"].at[index],
            device_id=peer,
            device_id_type=MESH,
        )

    def send(src, dst, name, index, peer):
        one = copy(src, dst, name, index, peer)
        one.start()
        sent.append(one)

    def arrive(dst, name, index, peer):
        copy(dst, dst, name, index, peer).wait_recv()

    pair = (d + 1 - 2 * x, m)

    def line(k):
        return (add(z, k, L) * 2 + x, m)

    def row_peer(k):
        return (d, add(m, k, M))

    pos = z + x * (R - 1 - 2 * z)

    def ring(q):
        q = lax.rem(q + 2 * R, R)
        far = q // L
        return 2 * q * (1 - far) + (2 * (R - 1 - q) + 1) * far

    W = r["W"]

    def wcols(b, c0, width):
        return W.at[b, :, pl.ds(c0, width)]

    local = []
    for n, (src, dst) in enumerate(
        [
            (r["w_qkv"], wcols(d, *p.cols[0])),
            (r["tokens"], r["tok"]),
            (r["w_up"], wcols(d, *p.cols[2])),
            (r["w_out"], r["raw_out"] if p.whole_lanes else wcols(d, *p.cols[1])),
            (r["w_down"], r["raw_down"] if p.whole_lanes else wcols(d, *p.cols[3])),
            (r["grad_out"], r["go"]),
        ]
    ):
        one = pltpu.make_async_copy(src, dst, r["loc"].at[n])
        one.start()
        local.append(one)

    barrier = pltpu.get_barrier_semaphore()
    greeted = [(ring(pos + 1), m), (ring(pos - 1), m)] + [row_peer(k) for k in range(1, M)]
    for peer in greeted:
        pl.semaphore_signal(barrier, 1, device_id=peer, device_id_type=MESH)

    def norm(values):
        center = values - jnp.mean(values, axis=-1, keepdims=True)
        inverse = lax.rsqrt(jnp.mean(center * center, axis=-1, keepdims=True) + 1e-05)
        return center * inverse, inverse

    local[1].wait()
    h1f = r["h1f"]

    @pl.loop(0, tl // 32)
    def _(c):
        rows = pl.ds(pl.multiple_of(c * 32, 32), 32)
        h1f[rows, :] = norm(r["tok"][rows, :])[0]

    local[0].wait()
    pl.semaphore_wait(barrier, len(greeted))

    class Queue:
        def __init__(self):
            self.steps = []

        def add(self, streams, start):
            for stream in streams:
                self.steps += [(start + t, run) for t, run in enumerate(stream)]
            self.steps.sort(key=lambda one: one[0])

        def run(self, place):
            while self.steps and self.steps[0][0] <= place:
                self.steps.pop(0)[1]()

    def gather_steps(block, name, index, way, hops):
        onward, before = (ring(pos + way), m), (ring(pos - way), m)

        def step(t):
            def run():
                here = block(ring(pos - way * t))
                if t:
                    arrive(here, name, (*index, t - 1), before)
                if t < hops:
                    send(here, here, name, (*index, t), onward)

            return run

        return [step(t) for t in range(hops + 1)]

    def gather_streams(segment):
        return [
            gather_steps(
                lambda b, s=s, first=first, width=width: wcols(b, p.cols[s][0] + first, width),
                "wg",
                (n,),
                way,
                hops,
            )
            for n, (s, first, width, way, hops) in enumerate(p.streams)
            if s == segment
        ]

    def weight(s, first=0, width=None):
        c0, full = p.cols[s]
        width = full if width is None else width
        return W[:, :, pl.ds(c0 + first, width)].reshape(D, width)

    gathers = Queue()
    lnp = r["lnp"]
    if p.whole_lanes:
        lnall = r["lnall"]
        lnall[d] = r["ln_in"][...]
        for k, (way, hops) in enumerate(((1, p.far), (-1, R - 1 - p.far))):
            gathers.add([gather_steps(lambda b: lnall.at[b], "lg", (k,), way, hops)], 0)
    else:
        lnp[...] = r["ln_in"][...].astype(f32)[0:8, :]
    gathers.add(gather_streams(0), 0)
    gathers.run(0)

    for n in range(2, 6):
        local[n].wait()
    if p.whole_lanes:
        for raw, (c0, width) in ((r["raw_out"], p.cols[1]), (r["raw_down"], p.cols[3])):
            W[d, :, pl.ds(c0, width)] = raw[...].astype(f32).T.astype(bf16)

    outlow = r["outlow"]
    outlow[...] = r["go"][...].astype(bf16)

    gathers.run(R)
    if p.whole_lanes:
        for b in range(R):
            lnp[:, pl.ds(b * rb, rb)] = lnall[b].astype(f32)[0:8, :]
    gain1, bias1, gain2, bias2 = (lnp[pl.ds(k, 1), :] for k in range(4))

    def norm_back(upstream, normed, inverse, gain):
        scaled = upstream * gain
        return inverse * (
            scaled
            - jnp.mean(scaled, axis=-1, keepdims=True)
            - normed * jnp.mean(scaled * normed, axis=-1, keepdims=True)
        )

    h1 = r["h1"]

    h1[...] = (h1f[...] * gain1 + bias1).astype(bf16)
    lane = lax.broadcasted_iota(jnp.int32, (1, LANES), 1)
    low = lane < HEAD_DIM

    def swap(v):
        return pltpu.roll(v, HEAD_DIM, 1)

    qs, kvs, qin, KV = r["qs"], r["kvs"], r["qin"], r["KV"]
    for t in range(H // 2):
        mixed = nn(h1[...], weight(0, 6 * HEAD_DIM * t, 6 * HEAD_DIM))
        t0, t1, t2 = (mixed[:, k * LANES : (k + 1) * LANES] for k in range(3))
        q_even, q_odd = t0 * 0.125, swap(t1) * 0.125
        for h, q in ((2 * t, q_even), (2 * t + 1, q_odd)):
            qs[h] = jnp.where(low, q[:half], swap(q[half:])).astype(bf16)
        kvs[2 * t] = jnp.where(low, swap(t0), swap(t1)).astype(bf16)
        kvs[2 * t + 1] = t2.astype(bf16)

    def head_dev(h, member):
        return (h * g + member, m)

    for k in range(1, H):
        h = add(dh, k, H)
        peer = head_dev(h, di)
        send(kvs.at[h], KV.at[d], "kv", k, peer)
        send(qs.at[h], qin.at[dh], "q", k, peer)
    gathers.add(gather_streams(1), 0)
    gathers.add(gather_streams(2), 0.5)
    gathers.add(gather_streams(3), 3)
    gathers.run(0.5)
    KV[d] = kvs[dh]
    qin[dh] = qs[dh]
    for k in range(H):
        j = add(dh, H - k, H)
        own = j * g + di
        if k:
            arrive(KV.at[own], "kv", k, head_dev(j, di))
        for q in range(1, g):
            send(KV.at[own], KV.at[own], "kvx", (k, q - 1), head_dev(dh, add(di, q, g)))
    for k in range(1, H):
        j = add(dh, H - k, H)
        arrive(qin.at[j], "q", k, head_dev(j, di))
    for k in range(H):
        j = add(dh, H - k, H)
        for q in range(1, g):
            member = add(di, g - q, g)
            arrive(KV.at[j * g + member], "kvx", (k, q - 1), head_dev(dh, member))

    gathers.run(1.5)

    qall, KVT = r["qall"], r["KVT"]
    for j in range(H):
        packed = qin[j].astype(f32)
        qall[pl.ds(j * tl, half), :] = jnp.where(low, packed, 0.0).astype(bf16)
        qall[pl.ds(j * tl + half, half), :] = jnp.where(low, swap(packed), 0.0).astype(bf16)

    ends = []
    total = 0
    for k in range(p.scenes):
        total = total + r["scene"][k]
        ends.append(total)

    def scene_of(pos):
        count = jnp.zeros(pos.shape, jnp.int32)
        for end in ends:
            count = count + (pos >= end).astype(jnp.int32)
        return count

    token_lane = lax.broadcasted_iota(jnp.int32, (1, tl), 1)
    q_scene = jnp.concatenate(
        [scene_of((j * g + di) * tl + token_lane) for j in range(H)], axis=1
    )
    token_row = lax.broadcasted_iota(jnp.int32, (tl, 1), 0)

    def masked_scores(o):
        scores = nt(KV[o], qall[...])
        return jnp.where(scene_of(o * tl + token_row) == q_scene, scores, FAR)

    unit = (
        lax.broadcasted_iota(jnp.int32, (LANES, LANES), 0)
        == lax.broadcasted_iota(jnp.int32, (LANES, LANES), 1)
    ).astype(bf16)

    top8, sum8, acc = r["top8"], r["sum8"], r["acc"]
    top8[...] = jnp.full((8, NQ), FAR, f32)
    sum8[...] = jnp.zeros((8, NQ), f32)
    acc[...] = jnp.zeros((LANES, NQ), f32)

    def maxima(o):
        KVT[o] = nt(unit, KV[o]).astype(bf16)
        top8[...] = jnp.maximum(
            top8[...], jnp.max(masked_scores(o).reshape(tl // 8, 8, NQ), axis=0)
        )

    pl.loop(0, R)(maxima)
    gathers.run(2.5)

    top = r["top"]
    top[...] = jnp.max(top8[...], axis=0, keepdims=True)

    def exponentials(o):
        expo = jnp.exp(masked_scores(o) - top[...])
        sum8[...] += jnp.sum(expo.reshape(tl // 8, 8, NQ), axis=0)
        low_expo = expo.astype(bf16)
        if p.keep:
            r["prob"][o] = low_expo
        acc[...] += nn(KVT[o], low_expo)

    pl.loop(0, R // 2)(exponentials)
    gathers.run(3)
    pl.loop(R // 2, R)(exponentials)

    scale_row = 1.0 / jnp.sum(sum8[...], axis=0, keepdims=True)
    inv = r["inv"]
    inv[...] = scale_row
    attf, atts, attT = r["attf"], r["atts"], r["attT"]
    attf[...] = acc[pl.ds(HEAD_DIM, HEAD_DIM), :] * scale_row
    for j in range(H):
        atts[j] = attf[:, pl.ds(j * tl, tl)].astype(bf16)
    for k in range(1, H):
        j = add(dh, k, H)
        send(atts.at[j], attT.at[dh], "att", k, head_dev(j, di))
    attT[dh] = atts[dh]
    gathers.run(3.5)
    for k in range(1, H):
        h = add(dh, H - k, H)
        arrive(attT.at[h], "att", k, head_dev(h, di))
    att = r["att"]
    att[...] = attT[...].reshape(HF, tl).astype(f32).T.astype(bf16)

    rs_send, rs_recv = r["rs_send"], r["rs_recv"]

    def rows_send(n, values):
        rs_send[n] = values.astype(bf16).reshape(M, rm, D)
        for k in range(1, M):
            send(rs_send.at[n, add(m, k, M)], rs_recv.at[n, k - 1], "rs", (n, k - 1), row_peer(k))

    def rows_sum(n):
        value = rs_send[n, m].astype(f32)
        for k in range(1, M):
            arrive(rs_recv.at[n, k - 1], "rs", (n, k - 1), row_peer(M - k))
            value = value + rs_recv[n, k - 1].astype(f32)
        return value

    def gather_send(n, ref):
        for k in range(1, M):
            send(ref.at[m], ref.at[m], "ag", (n, k - 1), row_peer(k))

    def gather_end(n, ref):
        for k in range(1, M):
            b = add(m, M - k, M)
            arrive(ref.at[b], "ag", (n, k - 1), row_peer(M - k))

    gathers.run(4)
    rows_send(0, nt(att[...], weight(1)))
    gathers.run(4.5)
    own_rows = pl.ds(pl.multiple_of(m * rm, rm), rm)
    mid, n2, r2, h2 = r["mid"], r["n2"], r["r2"], r["h2"]
    middle = r["tok"][own_rows, :] + rows_sum(0)
    mid[...] = middle
    normed, inverse = norm(middle)
    n2[...] = normed
    r2[...] = jnp.broadcast_to(inverse, (rm, LANES))
    h2[m] = (normed * gain2 + bias2).astype(bf16)
    gather_send(0, h2)
    gathers.run(5)
    gather_end(0, h2)

    active, il, slope = r["active"], r["il"], r["slope"]
    c_one, c_two = 0.7978845608028654, 0.044715
    step = 256
    for c in range(U // step):
        inner = nn(h2[...].reshape(tl, D), weight(2, c * step, step))
        square = inner * inner
        t = jnp.tanh(c_one * inner * (1.0 + c_two * square))
        cdf = 0.5 * (1.0 + t)
        active[:, pl.ds(c * step, step)] = (inner * cdf).astype(bf16)
        slope[:, pl.ds(c * step, step)] = cdf + 0.5 * inner * (1.0 - t * t) * (
            c_one + 3.0 * c_one * c_two * square
        )
    sums = Queue()

    def grad_part(s, lhs, rhs):
        c0, width = p.cols[s]
        G = r["G"]
        piece = 256 if width % 256 == 0 else LANES
        for c in range(width // piece):
            value = tn(lhs, rhs[:, pl.ds(c * piece, piece)]).astype(bf16)
            G[:, :, pl.ds(c0 + c * piece, piece)] = value.reshape(R, rb, piece)

    def sum_steps(n, stream, out):
        s, first, width, way, hops = stream
        columns = pl.ds(p.cols[s][0] + first, width)
        G, came = r["G"], r["came%d" % n]
        onward, before = (ring(pos + way), m), (ring(pos - way), m)

        def step(t):
            def run():
                b = ring(pos + way * (hops - t))
                if t:
                    arrive(came.at[t - 1], "gg", (n, t - 1), before)
                if t == hops:
                    rest = G[b, :, columns] if hops < p.far else out[:, pl.ds(first, width)]
                    out[:, pl.ds(first, width)] = rest.astype(f32) + came[t - 1].astype(f32)
                    return
                if t:
                    value = G[b, :, columns].astype(f32) + came[t - 1].astype(f32)
                    G[b, :, columns] = value.astype(bf16)
                send(G.at[b, :, columns], came.at[t], "gg", (n, t), onward)

            return run

        return [step(t) for t in range(hops + 1)]

    def sum_streams(segment, out):
        return [
            sum_steps(n, stream, out) for n, stream in enumerate(p.streams) if stream[0] == segment
        ]

    grad_part(3, outlow[...], active)
    sums.add(sum_streams(3, r["o_down"]), 0)
    sums.run(0)
    gathers.run(R)
    for c in range(U // step):
        dact = nn(outlow[...], weight(3, c * step, step))
        il[:, pl.ds(c * step, step)] = (dact * slope[:, pl.ds(c * step, step)]).astype(bf16)
    rows_send(1, nt(il[...], weight(2)))

    grad_part(2, h2[...].reshape(tl, D), il)
    sums.add(sum_streams(2, r["o_up"]), 1)
    sums.run(1)
    rows_send(2, nt(active[...], weight(3)))
    back2 = rows_sum(1)
    gm, ml = r["gm"], r["ml"]
    grad_middle = r["go"][own_rows, :] + norm_back(back2, n2[...], r2[:, 0:1], gain2)
    gm[...] = grad_middle
    ml[m] = grad_middle.astype(bf16)
    gather_send(1, ml)

    sums.run(2)
    ln2g, ln2b = r["ln2g"], r["ln2b"]
    ln2g[...] = jnp.sum(back2 * n2[...], axis=0, keepdims=True)
    ln2b[...] = jnp.sum(back2, axis=0, keepdims=True)

    gather_end(1, ml)
    midlow = ml[...].reshape(tl, D)

    gs, gin, gall = r["gs"], r["gin"], r["gall"]
    gatt = nn(midlow, weight(1))
    for h in range(H):
        tile = gatt[:, (h // 2) * LANES : (h // 2 + 1) * LANES]
        even = h % 2 == 0
        first = tile[:half] if even else swap(tile[:half])
        second = swap(tile[half:]) if even else tile[half:]
        gs[h] = jnp.where(low, first, second).astype(bf16)
    for k in range(1, H):
        h = add(dh, k, H)
        send(gs.at[h], gin.at[dh], "ga", k, head_dev(h, di))
    gin[dh] = gs[dh]

    grad_part(1, midlow, att)
    sums.add(sum_streams(1, r["o_out"]), 2.5)
    sums.run(2.5)
    for k in range(1, H):
        j = add(dh, H - k, H)
        arrive(gin.at[j], "ga", k, head_dev(j, di))

    inv_col = jnp.broadcast_to(inv[...], (LANES, NQ)).T
    shift_parts = []
    for j in range(H):
        packed = gin[j].astype(f32)
        top_half = jnp.where(low, 0.0, swap(packed))
        bottom = jnp.where(low, 0.0, packed)
        ga = jnp.concatenate([top_half, bottom], axis=0)
        gaT = ga.T[HEAD_DIM:, :]
        shift_parts.append(
            jnp.sum(gaT * attf[:, pl.ds(j * tl, tl)], axis=0, keepdims=True)
            * inv[:, pl.ds(j * tl, tl)]
        )
        gall[pl.ds(j * tl, tl), :] = (ga * inv_col[j * tl : (j + 1) * tl]).astype(bf16)
    shift = r["shift"]
    shift[...] = jnp.concatenate(shift_parts, axis=1)

    acc[...] = jnp.zeros((LANES, NQ), f32)
    dkvs, dkvx, dkv_in = r["dkvs"], r["dkvx"], r["dkv_in"]

    def key_grads(o):
        prob = r["prob"][o] if p.keep else jnp.exp(masked_scores(o) - top[...]).astype(bf16)
        dprob = nt(KV[o], gall[...])
        dscore = (prob.astype(f32) * (dprob - shift[...])).astype(bf16)
        acc[...] += nn(KVT[o], dscore)
        return nn(dscore, qall[...]) + nn(prob, gall[...])

    for q in range(1, g):
        member = add(di, q, g)
        for k in range(H):
            j = add(dh, k, H)
            dkvs[q, k] = key_grads(j * g + member).astype(bf16)
            send(dkvs.at[q, k], dkvx.at[q - 1, k], "dkvx", (q - 1, k), head_dev(dh, member))
        sums.run(2.5 + q)
    for k in [*range(1, H), 0]:
        j = add(dh, k, H)
        dkv = key_grads(j * g + di)
        for q in range(1, g):
            arrive(dkvx.at[q - 1, k], "dkvx", (q - 1, k), head_dev(dh, add(di, g - q, g)))
            dkv = dkv + dkvx[q - 1, k].astype(f32)
        if k:
            dkvs[0, k] = dkv.astype(bf16)
            send(dkvs.at[0, k], dkv_in.at[dh], "dkv", k, head_dev(j, di))
        else:
            dkv_in[dh] = dkv.astype(bf16)

    dqs, dqT = r["dqs"], r["dqT"]
    for j in range(H):
        dqs[j] = (acc[pl.ds(0, HEAD_DIM), pl.ds(j * tl, tl)] * 0.125).astype(bf16)
    for k in range(1, H):
        j = add(dh, k, H)
        send(dqs.at[j], dqT.at[dh], "dq", k, head_dev(j, di))
    dqT[dh] = dqs[dh]
    sums.run(4)

    res = r["res"]
    res[m] = (mid[...] + rows_sum(2)).astype(bf16)
    gather_send(2, res)

    sums.run(5)
    for k in range(1, H):
        h = add(dh, H - k, H)
        arrive(dqT.at[h], "dq", k, head_dev(h, di))
        arrive(dkv_in.at[h], "dkv", k, head_dev(h, di))

    gmix = r["gmix"]
    dq = dqT[...].reshape(HF, tl).astype(f32).T

    def head_sum(h):
        return dkv_in[h].astype(f32)

    for t in range(H // 2):
        both = dq[:, t * LANES : (t + 1) * LANES]
        even = swap(head_sum(2 * t))
        base = 6 * HEAD_DIM * t
        gmix[:, pl.ds(base, LANES)] = jnp.where(low, both, even).astype(bf16)
        gmix[:, pl.ds(base + LANES, LANES)] = jnp.where(low, even, both).astype(bf16)
        gmix[:, pl.ds(base + 2 * LANES, LANES)] = head_sum(2 * t + 1).astype(bf16)

    grad_part(0, h1[...], gmix)
    sums.add(sum_streams(0, r["o_qkv"]), 10)
    sums.run(10)
    rows_send(3, nt(gmix[...], weight(0)))
    sums.run(11)
    back1 = rows_sum(3)
    n1, r1 = norm(r["tok"][own_rows, :])
    gt = r["gt"]
    gt[m] = (gm[...] + norm_back(back1, n1, r1, gain1)).astype(bf16)
    gather_send(3, gt)
    ln_rows = jnp.concatenate(
        [
            jnp.sum(back1 * n1, axis=0, keepdims=True),
            jnp.sum(back1, axis=0, keepdims=True),
            ln2g[...],
            ln2b[...],
            jnp.zeros((4, D), f32),
        ],
        axis=0,
    )
    lnrow, lnr_in = r["lnrow"], r["lnr_in"]
    for b in range(D // LANES):
        lnrow[b] = ln_rows[:, b * LANES : (b + 1) * LANES]

    def lane_block(b):
        return b * rb // LANES

    for k in range(1, R):
        o = add(d, k, R)
        send(lnrow.at[lane_block(o)], lnr_in.at[d], "lr", k - 1, (o, m))
    lnr_in[d] = lnrow[lane_block(d)]
    sums.run(12)
    for k in range(1, R):
        o = add(d, R - k, R)
        arrive(lnr_in.at[o], "lr", k - 1, (o, m))
    value = lnr_in[0]
    for b in range(1, R):
        value = value + lnr_in[b]
    lnx = r["lnx"]
    lnx[m] = value
    for k in range(1, M):
        send(lnx.at[m], lnx.at[m], "ln", k - 1, row_peer(k))
    sums.run(10 + R)

    gather_end(2, res)
    r["o_result"][...] = res[...].reshape(tl, D)
    gather_end(3, gt)
    r["o_tokens"][...] = gt[...].reshape(tl, D)
    for k in range(1, M):
        arrive(lnx.at[add(m, M - k, M)], "ln", k - 1, row_peer(M - k))
    value = lnx[0]
    for k in range(1, M):
        value = value + lnx[k]
    r["o_ln"][...] = value
    for one in sent:
        one.wait_send()


def layer(p, tokens, grad_out, w_qkv, w_out, w_up, w_down, ln_in, scene):
    R, M, L, H, g = p.R, p.M, p.L, p.H, p.g
    tl, D, rb, rm, U, HF, NQ = p.tl, p.D, p.rb, p.rm, p.U, p.HF, p.NQ
    half = tl // 2
    ins = {
        "tokens": tokens,
        "grad_out": grad_out,
        "w_qkv": w_qkv,
        "w_out": w_out,
        "w_up": w_up,
        "w_down": w_down,
        "ln_in": ln_in,
        "scene": scene,
    }
    outs = {
        "o_result": ((tl, D), bf16),
        "o_tokens": ((tl, D), bf16),
        "o_qkv": ((rb, 3 * HF), f32),
        "o_out": ((rb, HF), f32),
        "o_up": ((rb, U), f32),
        "o_down": ((rb, U), f32),
        "o_ln": ((8, LANES), f32),
    }
    v = pltpu.VMEM
    scratch = {
        "W": v((R, rb, p.WC), bf16),
        "tok": v((tl, D), f32),
        "go": v((tl, D), f32),
        "outlow": v((tl, D), bf16),
        "lnp": v((8, D), f32),
        "h1": v((tl, D), bf16),
        "h1f": v((tl, D), f32),
        "slope": v((tl, U), f32),
        "qs": v((H, half, LANES), bf16),
        "kvs": v((H, tl, LANES), bf16),
        "qin": v((H, half, LANES), bf16),
        "KV": v((R, tl, LANES), bf16),
        "KVT": v((R, LANES, tl), bf16),
        "qall": v((NQ, LANES), bf16),
        "top8": v((8, NQ), f32),
        "sum8": v((8, NQ), f32),
        "top": v((1, NQ), f32),
        "inv": v((1, NQ), f32),
        "shift": v((1, NQ), f32),
        "acc": v((LANES, NQ), f32),
        "attf": v((HEAD_DIM, NQ), f32),
        "atts": v((H, HEAD_DIM, tl), bf16),
        "attT": v((H, HEAD_DIM, tl), bf16),
        "att": v((tl, HF), bf16),
        "rs_send": v((4, M, rm, D), bf16),
        "rs_recv": v((4, M - 1, rm, D), bf16),
        "mid": v((rm, D), f32),
        "n2": v((rm, D), f32),
        "r2": v((rm, LANES), f32),
        "h2": v((M, rm, D), bf16),
        "active": v((tl, U), bf16),
        "il": v((tl, U), bf16),
        "gm": v((rm, D), f32),
        "ml": v((M, rm, D), bf16),
        "ln2g": v((1, D), f32),
        "ln2b": v((1, D), f32),
        "lnrow": v((D // LANES, 8, LANES), f32),
        "lnr_in": v((R, 8, LANES), f32),
        "lnx": v((M, 8, LANES), f32),
        "G": v((R, rb, p.WC), bf16),
        "gs": v((H, half, LANES), bf16),
        "gin": v((H, half, LANES), bf16),
        "gall": v((NQ, LANES), bf16),
        "dkvs": v((g, H, tl, LANES), bf16),
        "dkvx": v((max(g - 1, 1), H, tl, LANES), bf16),
        "dkv_in": v((H, tl, LANES), bf16),
        "dqs": v((H, HEAD_DIM, tl), bf16),
        "dqT": v((H, HEAD_DIM, tl), bf16),
        "gmix": v((tl, 3 * HF), bf16),
        "res": v((M, rm, D), bf16),
        "gt": v((M, rm, D), bf16),
    }
    if p.keep:
        scratch["prob"] = v((R, tl, NQ), bf16)
    if p.whole_lanes:
        scratch["raw_out"] = v((HF, rb), bf16)
        scratch["raw_down"] = v((U, rb), bf16)
        scratch["lnall"] = v((R, 16, rb), bf16)
    for n, (_, _, width, _, hops) in enumerate(p.streams):
        scratch["came%d" % n] = v((hops, rb, width), bf16)
    sems = {
        "wg": (len(p.streams), p.far),
        "gg": (len(p.streams), p.far),
        "lg": (2, p.far),
        "lr": (R - 1,),
        "kv": (H,),
        "q": (H,),
        "kvx": (H, max(g - 1, 1)),
        "att": (H,),
        "rs": (4, M - 1),
        "ag": (4, M - 1),
        "ga": (H,),
        "dkv": (H,),
        "dkvx": (max(g - 1, 1), H),
        "dq": (H,),
        "ln": (M - 1,),
    }
    for name, shape in sems.items():
        scratch[name + "_s"] = pltpu.SemaphoreType.DMA(shape)
        scratch[name + "_r"] = pltpu.SemaphoreType.DMA(shape)
    scratch["loc"] = pltpu.SemaphoreType.DMA((6,))
    names = (*ins, *outs, *scratch)
    any_spec = pl.BlockSpec(memory_space=pl.ANY)
    flops = 6 * tl * D * p.WC + 14 * NQ * R * tl * HEAD_DIM
    return pl.pallas_call(
        functools.partial(kernel, p, names),
        out_shape=[jax.ShapeDtypeStruct(*one) for one in outs.values()],
        in_specs=[any_spec] * 6 + [pl.BlockSpec(memory_space=pltpu.VMEM), pl.BlockSpec(memory_space=pltpu.SMEM)],
        out_specs=[pl.BlockSpec(memory_space=pltpu.VMEM)] * len(outs),
        scratch_shapes=list(scratch.values()),
        compiler_params=pltpu.CompilerParams(
            collective_id=0, has_side_effects=True, vmem_limit_bytes=60 << 20
        ),
        cost_estimate=pl.CostEstimate(flops=flops, bytes_accessed=8 << 20, transcendentals=NQ * R * tl),
        name="layer",
    )(*ins.values())


def finish_kernel(*refs):
    hbm, outs, held, sem = refs[:7], refs[7:17], refs[17:24], refs[24]
    copies = [pltpu.make_async_copy(hbm[k], held[k], sem.at[k]) for k in range(7)]
    for one in copies:
        one.start()
    for one in copies:
        one.wait()
    result, tokens, qkv, out, up, down, ln = held
    o_result, o_tokens, o_qkv, o_out, o_up, o_down = outs[:6]
    o_result[...] = result[...].astype(f32)
    o_tokens[...] = tokens[...].astype(f32)
    o_qkv[...] = qkv[...]
    o_out[...] = out[...].T
    o_up[...] = up[...]
    o_down[...] = down[...].T
    for k in range(4):
        outs[6 + k][...] = ln[k, :]


def finish(p, parts):
    tl, D, rb, U, HF = p.tl, p.D, p.rb, p.U, p.HF
    shapes = [(tl, D), (tl, D), (rb, 3 * HF), (HF, rb), (rb, U), (U, rb)] + [(rb,)] * 4
    spec = pl.BlockSpec(memory_space=pltpu.VMEM)
    return pl.pallas_call(
        finish_kernel,
        out_shape=[jax.ShapeDtypeStruct(shape, f32) for shape in shapes],
        in_specs=[pl.BlockSpec(memory_space=pl.ANY)] * 7,
        out_specs=[spec] * 10,
        scratch_shapes=[pltpu.VMEM(one.shape, one.dtype) for one in parts]
        + [pltpu.SemaphoreType.DMA((7,))],
        compiler_params=pltpu.CompilerParams(vmem_limit_bytes=32 << 20),
        cost_estimate=pl.CostEstimate(flops=0, bytes_accessed=6 << 20, transcendentals=0),
        name="finish",
    )(*parts)


def on_device(
    tokens,
    w_qkv,
    w_out,
    w_up,
    w_down,
    ln1_gain,
    ln1_bias,
    ln2_gain,
    ln2_bias,
    scene_lengths,
    grad_out,
):
    p = Plan(tokens, w_qkv, w_up, scene_lengths, lax.axis_size("dp"), lax.axis_size("mp"))
    rb, D = p.rb, p.D
    vectors = jnp.stack([ln1_gain, ln1_bias, ln2_gain, ln2_bias])
    if not p.whole_lanes:
        vectors = lax.all_gather(vectors, "dp", axis=1, tiled=True)
        w_out, w_down = w_out.T, w_down.T
    vectors = jnp.pad(vectors, ((0, 12), (0, 0)))
    parts = layer(p, tokens, grad_out, w_qkv, w_out, w_up, w_down, vectors, scene_lengths)
    if p.whole_lanes:
        return finish(p, parts)
    result, grad_tokens, qkv, out, up, down, ln = parts
    first = lax.axis_index("dp") * rb % LANES
    ln = lax.dynamic_slice_in_dim(ln, first, rb, 1)
    return (
        result.astype(f32),
        grad_tokens.astype(f32),
        qkv,
        out.T,
        up,
        down.T,
        ln[0],
        ln[1],
        ln[2],
        ln[3],
    )


def solution(mesh):
    weights = (P("dp", "mp"), P("mp", "dp"), P("dp", "mp"), P("mp", "dp"))
    rows = P("dp", None)
    vector = P("dp")
    return jax.shard_map(
        on_device,
        mesh=mesh,
        in_specs=(rows, *weights, vector, vector, vector, vector, P(), rows),
        out_specs=(rows, rows, *weights, vector, vector, vector, vector),
        check_vma=False,
    )
```

time: 280 us -> 185 us (0.66)
  Pallas kernels: 263 us -> 175 us
  local copies, waits for them, and re-layouts: 13.8 us -> 7.41 us
    pallas_call x1, Pallas kernels: 263 us -> 173 us  [layer(): pl.pallas_call(functools.partial(kernel, p, names), out_shape=[jax.ShapeD...]
    unnamed x36 -> x22, local copies, waits for them, and re-layouts: 12.3 us -> 7.41 us
where the time goes in v2:
time: 185 us; the launch traced here: 184 us
  Pallas kernels  175 us (95%)
  local copies, waits for them, and re-layouts  7.41 us (4%)
    pallas_call x1, Pallas kernels, layer(): pl.pallas_call(functools.partial(kernel, p, names), out_shape=[jax.ShapeD...  173 us
    unnamed x22, local copies, waits for them, and re-layouts  7.41 us

profile of v2, /device:TPU:0, one launch (start us, length us, event | category | flops | bytes accessed | tf_op | source)
XLA Modules:
  0.0 184.2 jit_solution(1545016160454923946)
XLA Ops:
  0.6 0.0 copy-start.10
  0.7 0.0 copy-start.7
  0.7 0.0 copy-start.8
  0.7 0.0 copy-start.9
  0.7 0.6 copy-done.10
  1.3 0.0 copy-done.7
  1.3 0.0 copy-done.8
  1.3 0.0 copy-done.9
  1.3 0.6 fusion.6.refs_6_
  2.0 172.7 %layer.1 = (bf16[256,1024]{1,0:T(8,128)(2,1)}, bf16[256,1024]{1,0:T(8,128)(2,1)}, f32[128,768]{1,0:T(8,128)}, f32[128,256]{1,0:T(8,128)}, f32[128,1024]{1,0:T(8,...) custom-call(f32[256,1024]{1,0:T(8,128)} %refs_0_.1, f32[256,1024]{1,0:T(8,128)} %refs_1_.1, bf16[128,768]{1,0:T(8,128)(2,1)} %refs_2_.1, ...), custom_call_target="tpu_custom_call" | custom-call | flops 6710886400 | bytes 8388608 | tf_op jit(solution)/shard_map/layer/pallas_call | solution.py:744
  174.7 0.0 copy-start.6
  174.7 0.7 copy-done.6
  175.3 0.0 copy-start
  175.3 1.0 copy-done
  176.4 0.0 copy-start.1
  176.4 1.0 copy-done.1
  177.4 0.0 copy-start.2
  177.4 1.0 copy-done.2
  178.5 1.0 copy-done.3
  179.5 0.0 copy-start.4
  179.5 1.0 copy-done.4
  180.5 0.0 copy-start.5
  180.5 0.9 copy-done.5
  181.4 2.6 %finish.1 = (f32[256,1024]{1,0:T(8,128)}, f32[256,1024]{1,0:T(8,128)}, f32[128,768]{1,0:T(8,128)}, f32[256,128]{1,0:T(8,128)}, f32[128,1024]{1,0:T(8,128)}, /*in...) custom-call(bf16[256,1024]{1,0:T(8,128)(2,1)S(1)} %copy-done, ...), custom_call_target="tpu_custom_call" | custom-call | bytes 6291456 | tf_op jit(solution)/shard_map/finish/pallas_call | solution.py:781
  (1 shorter events, 0.0 us)
Async XLA Ops:
  0.6 0.7 copy-start.10
  0.7 0.7 copy-start.7
  0.7 0.7 copy-start.8
  0.7 0.7 copy-start.9
  174.7 0.7 copy-start.6
  175.3 1.0 copy-start
  176.4 1.0 copy-start.1
  177.4 1.0 copy-start.2
  178.5 1.0 copy-start.3
  179.5 1.0 copy-start.4
  180.5 0.9 copy-start.5

commit v3 on v2

--- a/solution.py
+++ b/solution.py
@@ -11,6 +11,42 @@
 LANES = 128
 FAR = -1e30
 MESH = pl.DeviceIdType.MESH
+PT = {
+    "o0": 3.3,
+    "op": 0.7,
+    "u0": 3.4,
+    "d0": 4.9,
+    "g1": 4.1,
+    "g2": 3.8,
+    "g3": 2.6,
+    "g4": [4.6, 5.1],
+    "g5": [5.1, 5.6],
+    "g6": 5.6,
+    "g7": 5.4,
+    "g8": 6.6,
+    "g9": 6.9,
+    "su": 0.5,
+    "s1": 0.8,
+    "s2": 1.3,
+    "s3": 1.8,
+    "so": 2.2,
+    "sop": 0.86,
+    "s4": 2.5,
+    "s4b": [1.8],
+    "s5": 3.6,
+    "s5b": [3.3],
+    "s6": 4.3,
+    "s7": 4.8,
+    "sq": 4.7,
+    "sqp": 0.8,
+    "up": 1.0,
+    "dp": 0.74,
+    "sdp": 1.0,
+    "sup": 1.2,
+    "s8": 5.3,
+    "s9": 6.3,
+    "s10": 7.3,
+}
 bf16 = jnp.bfloat16
 f32 = jnp.float32
 
@@ -136,14 +172,6 @@
         inverse = lax.rsqrt(jnp.mean(center * center, axis=-1, keepdims=True) + 1e-05)
         return center * inverse, inverse
 
-    local[1].wait()
-    h1f = r["h1f"]
-
-    @pl.loop(0, tl // 32)
-    def _(c):
-        rows = pl.ds(pl.multiple_of(c * 32, 32), 32)
-        h1f[rows, :] = norm(r["tok"][rows, :])[0]
-
     local[0].wait()
     pl.semaphore_wait(barrier, len(greeted))
 
@@ -151,14 +179,18 @@
         def __init__(self):
             self.steps = []
 
-        def add(self, streams, start):
+        def add(self, tag, streams, start, pace=1.0):
             for stream in streams:
-                self.steps += [(start + t, run) for t, run in enumerate(stream)]
+                self.steps += [(start + pace * t, tag, run) for t, run in enumerate(stream)]
             self.steps.sort(key=lambda one: one[0])
 
         def run(self, place):
             while self.steps and self.steps[0][0] <= place:
-                self.steps.pop(0)[1]()
+                self.steps.pop(0)[2]()
+
+        def need(self, tag):
+            while any(one[1] == tag for one in self.steps):
+                self.steps.pop(0)[2]()
 
     def gather_steps(block, name, index, way, hops):
         onward, before = (ring(pos + way), m), (ring(pos - way), m)
@@ -199,12 +231,21 @@
         lnall = r["lnall"]
         lnall[d] = r["ln_in"][...]
         for k, (way, hops) in enumerate(((1, p.far), (-1, R - 1 - p.far))):
-            gathers.add([gather_steps(lambda b: lnall.at[b], "lg", (k,), way, hops)], 0)
+            gathers.add(0, [gather_steps(lambda b: lnall.at[b], "lg", (k,), way, hops)], 0)
     else:
         lnp[...] = r["ln_in"][...].astype(f32)[0:8, :]
-    gathers.add(gather_streams(0), 0)
+    gathers.add(0, gather_streams(0), 0)
+    gathers.add(1, gather_streams(1), PT["o0"], PT["op"])
+    gathers.add(2, gather_streams(2), PT["u0"], PT["up"])
+    gathers.add(3, gather_streams(3), PT["d0"], PT["dp"])
     gathers.run(0)
-
+    local[1].wait()
+    h1f = r["h1f"]
+
+    @pl.loop(0, tl // 32)
+    def _(c):
+        rows = pl.ds(pl.multiple_of(c * 32, 32), 32)
+        h1f[rows, :] = norm(r["tok"][rows, :])[0]
     for n in range(2, 6):
         local[n].wait()
     if p.whole_lanes:
@@ -214,7 +255,7 @@
     outlow = r["outlow"]
     outlow[...] = r["go"][...].astype(bf16)
 
-    gathers.run(R)
+    gathers.need(0)
     if p.whole_lanes:
         for b in range(R):
             lnp[:, pl.ds(b * rb, rb)] = lnall[b].astype(f32)[0:8, :]
@@ -255,10 +296,7 @@
         peer = head_dev(h, di)
         send(kvs.at[h], KV.at[d], "kv", k, peer)
         send(qs.at[h], qin.at[dh], "q", k, peer)
-    gathers.add(gather_streams(1), 0)
-    gathers.add(gather_streams(2), 0.5)
-    gathers.add(gather_streams(3), 3)
-    gathers.run(0.5)
+    gathers.run(PT["g1"])
     KV[d] = kvs[dh]
     qin[dh] = qs[dh]
     for k in range(H):
@@ -268,6 +306,7 @@
             arrive(KV.at[own], "kv", k, head_dev(j, di))
         for q in range(1, g):
             send(KV.at[own], KV.at[own], "kvx", (k, q - 1), head_dev(dh, add(di, q, g)))
+    gathers.run(PT["g2"])
     for k in range(1, H):
         j = add(dh, H - k, H)
         arrive(qin.at[j], "q", k, head_dev(j, di))
@@ -277,7 +316,7 @@
             member = add(di, g - q, g)
             arrive(KV.at[j * g + member], "kvx", (k, q - 1), head_dev(dh, member))
 
-    gathers.run(1.5)
+    gathers.run(PT["g3"])
 
     qall, KVT = r["qall"], r["KVT"]
     for j in range(H):
@@ -323,8 +362,14 @@
             top8[...], jnp.max(masked_scores(o).reshape(tl // 8, 8, NQ), axis=0)
         )
 
-    pl.loop(0, R)(maxima)
-    gathers.run(2.5)
+    pieces = 8 if R % 8 == 0 else 1
+
+    def in_pieces(body, places):
+        for c in range(pieces):
+            pl.loop(c * R // pieces, (c + 1) * R // pieces)(body)
+            gathers.run(places[c * len(places) // pieces])
+
+    in_pieces(maxima, PT["g4"])
 
     top = r["top"]
     top[...] = jnp.max(top8[...], axis=0, keepdims=True)
@@ -337,9 +382,7 @@
             r["prob"][o] = low_expo
         acc[...] += nn(KVT[o], low_expo)
 
-    pl.loop(0, R // 2)(exponentials)
-    gathers.run(3)
-    pl.loop(R // 2, R)(exponentials)
+    in_pieces(exponentials, PT["g5"])
 
     scale_row = 1.0 / jnp.sum(sum8[...], axis=0, keepdims=True)
     inv = r["inv"]
@@ -352,7 +395,7 @@
         j = add(dh, k, H)
         send(atts.at[j], attT.at[dh], "att", k, head_dev(j, di))
     attT[dh] = atts[dh]
-    gathers.run(3.5)
+    gathers.run(PT["g6"])
     for k in range(1, H):
         h = add(dh, H - k, H)
         arrive(attT.at[h], "att", k, head_dev(h, di))
@@ -382,9 +425,10 @@
             b = add(m, M - k, M)
             arrive(ref.at[b], "ag", (n, k - 1), row_peer(M - k))
 
-    gathers.run(4)
+    gathers.run(PT["g7"])
+    gathers.need(1)
     rows_send(0, nt(att[...], weight(1)))
-    gathers.run(4.5)
+    gathers.run(PT["g8"])
     own_rows = pl.ds(pl.multiple_of(m * rm, rm), rm)
     mid, n2, r2, h2 = r["mid"], r["n2"], r["r2"], r["h2"]
     middle = r["tok"][own_rows, :] + rows_sum(0)
@@ -394,7 +438,8 @@
     r2[...] = jnp.broadcast_to(inverse, (rm, LANES))
     h2[m] = (normed * gain2 + bias2).astype(bf16)
     gather_send(0, h2)
-    gathers.run(5)
+    gathers.run(PT["g9"])
+    gathers.need(2)
     gather_end(0, h2)
 
     active, il, slope = r["active"], r["il"], r["slope"]
@@ -419,7 +464,15 @@
             value = tn(lhs, rhs[:, pl.ds(c * piece, piece)]).astype(bf16)
             G[:, :, pl.ds(c0 + c * piece, piece)] = value.reshape(R, rb, piece)
 
-    def sum_steps(n, stream, out):
+    leaving = []
+
+    def leave(value, out):
+        one = pltpu.make_async_copy(value, out, r["out"].at[len(leaving)])
+        one.start()
+        leaving.append(one)
+
+    def sum_steps(n, stream, name):
+        held, out = r["v" + name], r[name]
         s, first, width, way, hops = stream
         columns = pl.ds(p.cols[s][0] + first, width)
         G, came = r["G"], r["came%d" % n]
@@ -431,8 +484,14 @@
                 if t:
                     arrive(came.at[t - 1], "gg", (n, t - 1), before)
                 if t == hops:
-                    rest = G[b, :, columns] if hops < p.far else out[:, pl.ds(first, width)]
-                    out[:, pl.ds(first, width)] = rest.astype(f32) + came[t - 1].astype(f32)
+                    mine = pl.ds(first, width)
+                    rest = G[b, :, columns] if hops < p.far else held[:, mine]
+                    held[:, mine] = rest.astype(f32) + came[t - 1].astype(f32)
+                    if hops == p.far:
+                        if p.whole_lanes:
+                            leave(held.at[:, mine], out.at[:, mine])
+                        elif way < 0:
+                            leave(held, out)
                     return
                 if t:
                     value = G[b, :, columns].astype(f32) + came[t - 1].astype(f32)
@@ -443,24 +502,25 @@
 
         return [step(t) for t in range(hops + 1)]
 
-    def sum_streams(segment, out):
+    def sum_streams(segment, name):
         return [
-            sum_steps(n, stream, out) for n, stream in enumerate(p.streams) if stream[0] == segment
+            sum_steps(n, stream, name) for n, stream in enumerate(p.streams) if stream[0] == segment
         ]
 
     grad_part(3, outlow[...], active)
-    sums.add(sum_streams(3, r["o_down"]), 0)
+    sums.add(3, sum_streams(3, "o_down"), 0, PT["sdp"])
     sums.run(0)
-    gathers.run(R)
+    gathers.need(3)
     for c in range(U // step):
         dact = nn(outlow[...], weight(3, c * step, step))
         il[:, pl.ds(c * step, step)] = (dact * slope[:, pl.ds(c * step, step)]).astype(bf16)
     rows_send(1, nt(il[...], weight(2)))
 
     grad_part(2, h2[...].reshape(tl, D), il)
-    sums.add(sum_streams(2, r["o_up"]), 1)
-    sums.run(1)
+    sums.add(2, sum_streams(2, "o_up"), PT["su"], PT["sup"])
+    sums.run(PT["s1"])
     rows_send(2, nt(active[...], weight(3)))
+    sums.run(PT["s2"])
     back2 = rows_sum(1)
     gm, ml = r["gm"], r["ml"]
     grad_middle = r["go"][own_rows, :] + norm_back(back2, n2[...], r2[:, 0:1], gain2)
@@ -468,7 +528,7 @@
     ml[m] = grad_middle.astype(bf16)
     gather_send(1, ml)
 
-    sums.run(2)
+    sums.run(PT["s3"])
     ln2g, ln2b = r["ln2g"], r["ln2b"]
     ln2g[...] = jnp.sum(back2 * n2[...], axis=0, keepdims=True)
     ln2b[...] = jnp.sum(back2, axis=0, keepdims=True)
@@ -490,8 +550,8 @@
     gin[dh] = gs[dh]
 
     grad_part(1, midlow, att)
-    sums.add(sum_streams(1, r["o_out"]), 2.5)
-    sums.run(2.5)
+    sums.add(1, sum_streams(1, "o_out"), PT["so"], PT["sop"])
+    sums.run(PT["s4"])
     for k in range(1, H):
         j = add(dh, H - k, H)
         arrive(gin.at[j], "ga", k, head_dev(j, di))
@@ -528,7 +588,8 @@
             j = add(dh, k, H)
             dkvs[q, k] = key_grads(j * g + member).astype(bf16)
             send(dkvs.at[q, k], dkvx.at[q - 1, k], "dkvx", (q - 1, k), head_dev(dh, member))
-        sums.run(2.5 + q)
+            sums.run(PT["s4b"][k * len(PT["s4b"]) // H])
+        sums.run(PT["s5"])
     for k in [*range(1, H), 0]:
         j = add(dh, k, H)
         dkv = key_grads(j * g + di)
@@ -540,6 +601,7 @@
             send(dkvs.at[0, k], dkv_in.at[dh], "dkv", k, head_dev(j, di))
         else:
             dkv_in[dh] = dkv.astype(bf16)
+        sums.run(PT["s5b"][k * len(PT["s5b"]) // H])
 
     dqs, dqT = r["dqs"], r["dqT"]
     for j in range(H):
@@ -548,13 +610,13 @@
         j = add(dh, k, H)
         send(dqs.at[j], dqT.at[dh], "dq", k, head_dev(j, di))
     dqT[dh] = dqs[dh]
-    sums.run(4)
+    sums.run(PT["s6"])
 
     res = r["res"]
     res[m] = (mid[...] + rows_sum(2)).astype(bf16)
     gather_send(2, res)
 
-    sums.run(5)
+    sums.run(PT["s7"])
     for k in range(1, H):
         h = add(dh, H - k, H)
         arrive(dqT.at[h], "dq", k, head_dev(h, di))
@@ -575,10 +637,10 @@
         gmix[:, pl.ds(base + 2 * LANES, LANES)] = head_sum(2 * t + 1).astype(bf16)
 
     grad_part(0, h1[...], gmix)
-    sums.add(sum_streams(0, r["o_qkv"]), 10)
-    sums.run(10)
+    sums.add(0, sum_streams(0, "o_qkv"), PT["sq"], PT["sqp"])
+    sums.run(PT["s8"])
     rows_send(3, nt(gmix[...], weight(0)))
-    sums.run(11)
+    sums.run(PT["s9"])
     back1 = rows_sum(3)
     n1, r1 = norm(r["tok"][own_rows, :])
     gt = r["gt"]
@@ -605,29 +667,31 @@
         o = add(d, k, R)
         send(lnrow.at[lane_block(o)], lnr_in.at[d], "lr", k - 1, (o, m))
     lnr_in[d] = lnrow[lane_block(d)]
-    sums.run(12)
+    sums.run(PT["s10"])
     for k in range(1, R):
         o = add(d, R - k, R)
         arrive(lnr_in.at[o], "lr", k - 1, (o, m))
     value = lnr_in[0]
     for b in range(1, R):
         value = value + lnr_in[b]
+    gather_end(2, res)
+    leave(res, r["o_result"])
     lnx = r["lnx"]
     lnx[m] = value
     for k in range(1, M):
         send(lnx.at[m], lnx.at[m], "ln", k - 1, row_peer(k))
-    sums.run(10 + R)
-
-    gather_end(2, res)
-    r["o_result"][...] = res[...].reshape(tl, D)
+    sums.run(100)
+
     gather_end(3, gt)
-    r["o_tokens"][...] = gt[...].reshape(tl, D)
+    leave(gt, r["o_tokens"])
     for k in range(1, M):
         arrive(lnx.at[add(m, M - k, M)], "ln", k - 1, row_peer(M - k))
     value = lnx[0]
     for k in range(1, M):
         value = value + lnx[k]
     r["o_ln"][...] = value
+    for one in leaving:
+        one.wait()
     for one in sent:
         one.wait_send()
 
@@ -647,8 +711,8 @@
         "scene": scene,
     }
     outs = {
-        "o_result": ((tl, D), bf16),
-        "o_tokens": ((tl, D), bf16),
+        "o_result": ((M, rm, D), bf16),
+        "o_tokens": ((M, rm, D), bf16),
         "o_qkv": ((rb, 3 * HF), f32),
         "o_out": ((rb, HF), f32),
         "o_up": ((rb, U), f32),
@@ -656,7 +720,13 @@
         "o_ln": ((8, LANES), f32),
     }
     v = pltpu.VMEM
+    space = pl.BlockSpec(memory_space=pltpu.HBM)
+    out_specs = [space] * 6 + [pl.BlockSpec(memory_space=pltpu.VMEM)]
     scratch = {
+        "vo_qkv": v((rb, 3 * HF), f32),
+        "vo_out": v((rb, HF), f32),
+        "vo_up": v((rb, U), f32),
+        "vo_down": v((rb, U), f32),
         "W": v((R, rb, p.WC), bf16),
         "tok": v((tl, D), f32),
         "go": v((tl, D), f32),
@@ -737,15 +807,16 @@
     for name, shape in sems.items():
         scratch[name + "_s"] = pltpu.SemaphoreType.DMA(shape)
         scratch[name + "_r"] = pltpu.SemaphoreType.DMA(shape)
+    scratch["out"] = pltpu.SemaphoreType.DMA((10,))
     scratch["loc"] = pltpu.SemaphoreType.DMA((6,))
     names = (*ins, *outs, *scratch)
-    any_spec = pl.BlockSpec(memory_space=pl.ANY)
+    any_spec = pl.BlockSpec(memory_space=pltpu.HBM)
     flops = 6 * tl * D * p.WC + 14 * NQ * R * tl * HEAD_DIM
     return pl.pallas_call(
         functools.partial(kernel, p, names),
         out_shape=[jax.ShapeDtypeStruct(*one) for one in outs.values()],
         in_specs=[any_spec] * 6 + [pl.BlockSpec(memory_space=pltpu.VMEM), pl.BlockSpec(memory_space=pltpu.SMEM)],
-        out_specs=[pl.BlockSpec(memory_space=pltpu.VMEM)] * len(outs),
+        out_specs=out_specs,
         scratch_shapes=list(scratch.values()),
         compiler_params=pltpu.CompilerParams(
             collective_id=0, has_side_effects=True, vmem_limit_bytes=60 << 20
@@ -756,36 +827,48 @@
 
 
 def finish_kernel(*refs):
-    hbm, outs, held, sem = refs[:7], refs[7:17], refs[17:24], refs[24]
-    copies = [pltpu.make_async_copy(hbm[k], held[k], sem.at[k]) for k in range(7)]
-    for one in copies:
+    hbm, outs, held, made, sem, done = refs[:7], refs[7:17], refs[17:24], refs[24:28], refs[28], refs[29]
+    reads = [pltpu.make_async_copy(hbm[k], held[k], sem.at[k]) for k in range(7)]
+    order = (5, 4, 2, 3, 0, 1, 6)
+    for k in order:
+        reads[k].start()
+    writes = []
+    forms = {
+        0: (made[0], lambda v: v.reshape(-1, v.shape[-1]).astype(f32)),
+        1: (made[1], lambda v: v.reshape(-1, v.shape[-1]).astype(f32)),
+        3: (made[2], lambda v: v.T),
+        5: (made[3], lambda v: v.T),
+    }
+    for k in order:
+        reads[k].wait()
+        if k == 6:
+            for n in range(4):
+                outs[6 + n][...] = held[6][n, :]
+            break
+        value = held[k]
+        if k in forms:
+            value, form = forms[k]
+            value[...] = form(held[k][...])
+        one = pltpu.make_async_copy(value, outs[k], done.at[k])
         one.start()
-    for one in copies:
+        writes.append(one)
+    for one in writes:
         one.wait()
-    result, tokens, qkv, out, up, down, ln = held
-    o_result, o_tokens, o_qkv, o_out, o_up, o_down = outs[:6]
-    o_result[...] = result[...].astype(f32)
-    o_tokens[...] = tokens[...].astype(f32)
-    o_qkv[...] = qkv[...]
-    o_out[...] = out[...].T
-    o_up[...] = up[...]
-    o_down[...] = down[...].T
-    for k in range(4):
-        outs[6 + k][...] = ln[k, :]
 
 
 def finish(p, parts):
     tl, D, rb, U, HF = p.tl, p.D, p.rb, p.U, p.HF
     shapes = [(tl, D), (tl, D), (rb, 3 * HF), (HF, rb), (rb, U), (U, rb)] + [(rb,)] * 4
-    spec = pl.BlockSpec(memory_space=pltpu.VMEM)
+    held = [pltpu.VMEM(one.shape, one.dtype) for one in parts]
+    made = [pltpu.VMEM(shapes[k], f32) for k in (0, 1, 3, 5)]
     return pl.pallas_call(
         finish_kernel,
         out_shape=[jax.ShapeDtypeStruct(shape, f32) for shape in shapes],
-        in_specs=[pl.BlockSpec(memory_space=pl.ANY)] * 7,
-        out_specs=[spec] * 10,
-        scratch_shapes=[pltpu.VMEM(one.shape, one.dtype) for one in parts]
-        + [pltpu.SemaphoreType.DMA((7,))],
-        compiler_params=pltpu.CompilerParams(vmem_limit_bytes=32 << 20),
+        in_specs=[pl.BlockSpec(memory_space=pltpu.HBM)] * 7,
+        out_specs=[pl.BlockSpec(memory_space=pltpu.HBM)] * 6
+        + [pl.BlockSpec(memory_space=pltpu.VMEM)] * 4,
+        scratch_shapes=[*held, *made, pltpu.SemaphoreType.DMA((7,)), pltpu.SemaphoreType.DMA((6,))],
+        compiler_params=pltpu.CompilerParams(vmem_limit_bytes=62 << 20),
         cost_estimate=pl.CostEstimate(flops=0, bytes_accessed=6 << 20, transcendentals=0),
         name="finish",
     )(*parts)
@@ -805,7 +888,7 @@
     grad_out,
 ):
     p = Plan(tokens, w_qkv, w_up, scene_lengths, lax.axis_size("dp"), lax.axis_size("mp"))
-    rb, D = p.rb, p.D
+    rb, D, tl = p.rb, p.D, p.tl
     vectors = jnp.stack([ln1_gain, ln1_bias, ln2_gain, ln2_bias])
     if not p.whole_lanes:
         vectors = lax.all_gather(vectors, "dp", axis=1, tiled=True)
@@ -818,8 +901,8 @@
     first = lax.axis_index("dp") * rb % LANES
     ln = lax.dynamic_slice_in_dim(ln, first, rb, 1)
     return (
-        result.astype(f32),
-        grad_tokens.astype(f32),
+        result.reshape(tl, D).astype(f32),
+        grad_tokens.reshape(tl, D).astype(f32),
         qkv,
         out.T,
         up,

time: 185 us -> 165 us (0.89)
  Pallas kernels: 175 us -> 162 us
  local copies, waits for them, and re-layouts: 7.41 us -> 0.67 us
    pallas_call x1, Pallas kernels: 173 us -> 159 us  [layer(): pl.pallas_call(functools.partial(kernel, p, names), out_shape=[jax.ShapeD...]
    unnamed x22 -> x8, local copies, waits for them, and re-layouts: 7.41 us -> 0.67 us
where the time goes in v3:
time: 165 us; the launch traced here: 164 us
  Pallas kernels  162 us (98%)
    pallas_call x1, Pallas kernels, layer(): pl.pallas_call(functools.partial(kernel, p, names), out_shape=[jax.ShapeD...  159 us
    pallas_call x1, Pallas kernels, finish(): pl.pallas_call(finish_kernel, out_shape=[jax.ShapeDtypeStruct(shape, f32)...  3.72 us

profile of v3, /device:TPU:0, one launch (start us, length us, event | category | flops | bytes accessed | tf_op | source)
XLA Modules:
  0.0 164.4 jit_solution(7161644413283045136)
XLA Ops:
  0.6 0.0 copy-start.3
  0.7 0.0 copy-start
  0.7 0.0 copy-start.1
  0.7 0.0 copy-start.2
  0.7 0.6 copy-done.3
  1.3 0.0 copy-done
  1.3 0.0 copy-done.1
  1.3 0.0 copy-done.2
  1.3 0.6 fusion.6.refs_6_
  2.0 158.6 %layer.1 = (bf16[4,64,1024]{2,1,0:T(8,128)(2,1)}, bf16[4,64,1024]{2,1,0:T(8,128)(2,1)}, f32[128,768]{1,0:T(8,128)}, f32[128,256]{1,0:T(8,128)}, f32[128,1024]{1,...) custom-call(f32[256,1024]{1,0:T(8,128)} %refs_0_.1, f32[256,1024]{1,0:T(8,128)} %refs_1_.1, bf16[128,768]{1,0:T(8,128)(2,1)} %refs_2_.1, ...), custom_call_target="tpu_custom_call" | custom-call | flops 6710886400 | bytes 8388608 | tf_op jit(solution)/shard_map/layer/pallas_call | solution.py:815
  160.5 3.7 %finish.1 = (f32[256,1024]{1,0:T(8,128)}, f32[256,1024]{1,0:T(8,128)}, f32[128,768]{1,0:T(8,128)}, f32[256,128]{1,0:T(8,128)}, f32[128,1024]{1,0:T(8,128)}, /*in...) custom-call(bf16[4,64,1024]{2,1,0:T(8,128)(2,1)} %get-tuple-element.17.refs_0_, ...), custom_call_target="tpu_custom_call" | custom-call | bytes 6291456 | tf_op jit(solution)/shard_map/finish/pallas_call | solution.py:864
Async XLA Ops:
  0.6 0.7 copy-start.3
  0.7 0.7 copy-start
  0.7 0.7 copy-start.1
  0.7 0.7 copy-start.2

commit v4 on v3

--- a/solution.py
+++ b/solution.py
@@ -12,39 +12,41 @@
 FAR = -1e30
 MESH = pl.DeviceIdType.MESH
 PT = {
-    "o0": 3.3,
-    "op": 0.7,
-    "u0": 3.4,
-    "d0": 4.9,
-    "g1": 4.1,
-    "g2": 3.8,
-    "g3": 2.6,
-    "g4": [4.6, 5.1],
-    "g5": [5.1, 5.6],
-    "g6": 5.6,
-    "g7": 5.4,
-    "g8": 6.6,
-    "g9": 6.9,
-    "su": 0.5,
-    "s1": 0.8,
-    "s2": 1.3,
-    "s3": 1.8,
-    "so": 2.2,
-    "sop": 0.86,
-    "s4": 2.5,
-    "s4b": [1.8],
-    "s5": 3.6,
-    "s5b": [3.3],
-    "s6": 4.3,
-    "s7": 4.8,
-    "sq": 4.7,
-    "sqp": 0.8,
-    "up": 1.0,
-    "dp": 0.74,
-    "sdp": 1.0,
-    "sup": 1.2,
-    "s8": 5.3,
-    "s9": 6.3,
+    "g1b": -4.6,
+    "g0": 2.5,
+    "o0": 1.8,
+    "op": 0.96,
+    "u0": 1.3,
+    "d0": 4.5,
+    "g1": 2.8,
+    "g2": 4.3,
+    "g3": -1.5,
+    "g4": [1.7, 4.5, 1.8, 3.1, 3.6, 1.3, 4.6, 5.2],
+    "g5": [4.9, 5.4, 4.0, 5.1, 4.8, 4.5, 2.2, 5.4],
+    "g6": -11.4,
+    "g7": -10.9,
+    "g8": 7.2,
+    "g9": 8.3,
+    "su": 0.3,
+    "s1": -1.5,
+    "s2": 3.0,
+    "s3": 2.5,
+    "so": 2.1,
+    "sop": 1.6,
+    "s4": 3.2,
+    "s4b": [-13.5, -8.0, -5.3, -8.1],
+    "s5": -2.7,
+    "s5b": [-11.3, -5.4, -4.8, -6.8],
+    "s6": 5.2,
+    "s7": 5.3,
+    "sq": 9.5,
+    "sqp": 0.5,
+    "up": 1.44,
+    "dp": 0.98,
+    "sdp": 1.54,
+    "sup": 1.42,
+    "s8": 6.7,
+    "s9": -4.0,
     "s10": 7.3,
 }
 bf16 = jnp.bfloat16
@@ -78,7 +80,7 @@
         self.NQ = self.H * self.tl
         self.keep = dp * self.tl <= 4096
         self.whole_lanes = self.rb % LANES == 0
-        widths = (3 * self.HF, self.HF, self.U, self.U)
+        widths = (0, self.HF, self.U, self.U)
         self.cols = []
         start = 0
         for width in widths:
@@ -90,6 +92,8 @@
         self.streams = []
         for s, width in enumerate(widths):
             half = width // 2
+            if not width:
+                continue
             for first, way in ((0, 1), (half, -1)):
                 self.streams.append((s, first, half, way, far))
                 self.streams.append((s, first, half, -way, near))
@@ -127,10 +131,12 @@
     def arrive(dst, name, index, peer):
         copy(dst, dst, name, index, peer).wait_recv()
 
-    pair = (d + 1 - 2 * x, m)
-
-    def line(k):
-        return (add(z, k, L) * 2 + x, m)
+    def head_dev(h, member):
+        return (h * g + member, m)
+
+    m_side, m_core = lax.rem(m + 2, M), m + 1 - 2 * lax.rem(m, 2)
+    m_both = lax.rem(m_core + 2, M)
+    side, core = (d, m_side), (d, m_core)
 
     def row_peer(k):
         return (d, add(m, k, M))
@@ -150,7 +156,7 @@
     local = []
     for n, (src, dst) in enumerate(
         [
-            (r["w_qkv"], wcols(d, *p.cols[0])),
+            (r["w_qkv"], r["raw_qkv"]),
             (r["tokens"], r["tok"]),
             (r["w_up"], wcols(d, *p.cols[2])),
             (r["w_out"], r["raw_out"] if p.whole_lanes else wcols(d, *p.cols[1])),
@@ -163,7 +169,11 @@
         local.append(one)
 
     barrier = pltpu.get_barrier_semaphore()
-    greeted = [(ring(pos + 1), m), (ring(pos - 1), m)] + [row_peer(k) for k in range(1, M)]
+    greeted = [head_dev(add(dh, k, H), di) for k in range(1, H)]
+    greeted += [head_dev(dh, add(di, q, g)) for q in range(1, g)]
+    greeted += [row_peer(k) for k in range(1, M)]
+    if g != 2:
+        greeted += [(ring(pos + 1), m), (ring(pos - 1), m)]
     for peer in greeted:
         pl.semaphore_signal(barrier, 1, device_id=peer, device_id_type=MESH)
 
@@ -172,8 +182,43 @@
         inverse = lax.rsqrt(jnp.mean(center * center, axis=-1, keepdims=True) + 1e-05)
         return center * inverse, inverse
 
+    lane = lax.broadcasted_iota(jnp.int32, (1, LANES), 1)
+    low = lane < HEAD_DIM
+
+    def swap(v):
+        return pltpu.roll(v, HEAD_DIM, 1)
+
+    N, ws, Win = r["N"], r["ws"], r["Win"]
     local[0].wait()
+    vectors = 0.0
+    if p.whole_lanes:
+        before = jnp.zeros((HEAD_DIM, rb), f32)
+        after = jnp.zeros((HEAD_DIM - 16, rb), f32)
+        vectors = jnp.concatenate([before, r["ln_in"][...].astype(f32), after], axis=0).T
+    for t in range(H // 2):
+        t0, t1, t2 = (
+            r["raw_qkv"][:, pl.ds((3 * t + k) * LANES, LANES)].astype(f32) for k in range(3)
+        )
+        ws[2 * t, :, pl.ds(0, LANES)] = t0.astype(bf16)
+        ws[2 * t, :, pl.ds(LANES, LANES)] = jnp.where(low, t1, vectors).astype(bf16)
+        ws[2 * t + 1, :, pl.ds(0, LANES)] = jnp.where(low, swap(t1), swap(t2)).astype(bf16)
+        ws[2 * t + 1, :, pl.ds(LANES, LANES)] = jnp.where(low, swap(t2), vectors).astype(bf16)
+    local[1].wait()
+
+    def norm_quarter(b):
+        for c in range(rm // 32):
+            first = pl.multiple_of(b * rm + c * 32, 32)
+            N[dh, b, pl.ds(c * 32, 32), :] = norm(r["tok"][pl.ds(first, 32), :])[0].astype(bf16)
+
+    norm_quarter(m)
     pl.semaphore_wait(barrier, len(greeted))
+    for k in range(1, H):
+        h = add(dh, k, H)
+        send(N.at[dh, m], N.at[dh, m], "na", k, head_dev(h, di))
+        send(ws.at[h], Win.at[d], "wa", k, head_dev(h, di))
+    Win[d] = ws[dh]
+    for q in range(1, g):
+        send(Win.at[d], Win.at[d], "wax", (0, q - 1), head_dev(dh, add(di, q, g)))
 
     class Queue:
         def __init__(self):
@@ -227,25 +272,14 @@
 
     gathers = Queue()
     lnp = r["lnp"]
-    if p.whole_lanes:
-        lnall = r["lnall"]
-        lnall[d] = r["ln_in"][...]
-        for k, (way, hops) in enumerate(((1, p.far), (-1, R - 1 - p.far))):
-            gathers.add(0, [gather_steps(lambda b: lnall.at[b], "lg", (k,), way, hops)], 0)
-    else:
+    if not p.whole_lanes:
         lnp[...] = r["ln_in"][...].astype(f32)[0:8, :]
-    gathers.add(0, gather_streams(0), 0)
     gathers.add(1, gather_streams(1), PT["o0"], PT["op"])
     gathers.add(2, gather_streams(2), PT["u0"], PT["up"])
     gathers.add(3, gather_streams(3), PT["d0"], PT["dp"])
     gathers.run(0)
-    local[1].wait()
-    h1f = r["h1f"]
-
-    @pl.loop(0, tl // 32)
-    def _(c):
-        rows = pl.ds(pl.multiple_of(c * 32, 32), 32)
-        h1f[rows, :] = norm(r["tok"][rows, :])[0]
+    for k in range(1, M):
+        norm_quarter(add(m, k, M))
     for n in range(2, 6):
         local[n].wait()
     if p.whole_lanes:
@@ -255,10 +289,28 @@
     outlow = r["outlow"]
     outlow[...] = r["go"][...].astype(bf16)
 
-    gathers.need(0)
+    for k in range(1, H):
+        j = add(dh, H - k, H)
+        own = j * g + di
+        arrive(N.at[j, m], "na", k, head_dev(j, di))
+        send(N.at[j, m], N.at[j, m], "ny", k, side)
+        send(N.at[j, m], N.at[j, m], "nc", k, core)
+        arrive(Win.at[own], "wa", k, head_dev(j, di))
+        for q in range(1, g):
+            send(Win.at[own], Win.at[own], "wax", (k, q - 1), head_dev(dh, add(di, q, g)))
+        gathers.run(PT["g0"])
+    for k in range(1, H):
+        j = add(dh, H - k, H)
+        arrive(N.at[j, m_side], "ny", k, side)
+        send(N.at[j, m_side], N.at[j, m_side], "nd", k, core)
+    for k in range(H):
+        j = add(dh, H - k, H)
+        for q in range(1, g):
+            member = add(di, g - q, g)
+            arrive(Win.at[j * g + member], "wax", (k, q - 1), head_dev(dh, member))
     if p.whole_lanes:
-        for b in range(R):
-            lnp[:, pl.ds(b * rb, rb)] = lnall[b].astype(f32)[0:8, :]
+        columns = Win[:, :, pl.ds(LANES, LANES)].reshape(D, LANES).astype(f32)
+        lnp[...] = columns.T[HEAD_DIM : HEAD_DIM + 8, :]
     gain1, bias1, gain2, bias2 = (lnp[pl.ds(k, 1), :] for k in range(4))
 
     def norm_back(upstream, normed, inverse, gain):
@@ -271,45 +323,32 @@
 
     h1 = r["h1"]
 
-    h1[...] = (h1f[...] * gain1 + bias1).astype(bf16)
-    lane = lax.broadcasted_iota(jnp.int32, (1, LANES), 1)
-    low = lane < HEAD_DIM
-
-    def swap(v):
-        return pltpu.roll(v, HEAD_DIM, 1)
-
-    qs, kvs, qin, KV = r["qs"], r["kvs"], r["qin"], r["KV"]
-    for t in range(H // 2):
-        mixed = nn(h1[...], weight(0, 6 * HEAD_DIM * t, 6 * HEAD_DIM))
-        t0, t1, t2 = (mixed[:, k * LANES : (k + 1) * LANES] for k in range(3))
-        q_even, q_odd = t0 * 0.125, swap(t1) * 0.125
-        for h, q in ((2 * t, q_even), (2 * t + 1, q_odd)):
-            qs[h] = jnp.where(low, q[:half], swap(q[half:])).astype(bf16)
-        kvs[2 * t] = jnp.where(low, swap(t0), swap(t1)).astype(bf16)
-        kvs[2 * t + 1] = t2.astype(bf16)
-
-    def head_dev(h, member):
-        return (h * g + member, m)
-
+    def hidden(j):
+        part = N[j].reshape(tl, D).astype(f32) * gain1 + bias1
+        h1[pl.ds(pl.multiple_of(j * tl, tl), tl), :] = part.astype(bf16)
+
+    hidden(dh)
+    gathers.run(PT["g1"])
     for k in range(1, H):
-        h = add(dh, k, H)
-        peer = head_dev(h, di)
-        send(kvs.at[h], KV.at[d], "kv", k, peer)
-        send(qs.at[h], qin.at[dh], "q", k, peer)
-    gathers.run(PT["g1"])
-    KV[d] = kvs[dh]
-    qin[dh] = qs[dh]
+        j = add(dh, H - k, H)
+        arrive(N.at[j, m_core], "nc", k, core)
+        arrive(N.at[j, m_both], "nd", k, core)
+        hidden(j)
+        gathers.run(PT["g1b"])
+
+    KV, qall, KVT = r["KV"], r["qall"], r["KVT"]
+    head_weight = Win[...].reshape(D, 2 * LANES)
     for k in range(H):
         j = add(dh, H - k, H)
-        own = j * g + di
-        if k:
-            arrive(KV.at[own], "kv", k, head_dev(j, di))
+        rows = pl.ds(pl.multiple_of(j * tl, tl), tl)
+        mixed = nn(h1[rows, :], head_weight)
+        t0, t1 = mixed[:, :LANES], mixed[:, LANES:]
+        qall[rows, :] = jnp.where(low, t0 * 0.125, 0.0).astype(bf16)
+        KV[j * g + di] = jnp.where(low, swap(t0), swap(t1)).astype(bf16)
         for q in range(1, g):
+            own = j * g + di
             send(KV.at[own], KV.at[own], "kvx", (k, q - 1), head_dev(dh, add(di, q, g)))
     gathers.run(PT["g2"])
-    for k in range(1, H):
-        j = add(dh, H - k, H)
-        arrive(qin.at[j], "q", k, head_dev(j, di))
     for k in range(H):
         j = add(dh, H - k, H)
         for q in range(1, g):
@@ -317,12 +356,6 @@
             arrive(KV.at[j * g + member], "kvx", (k, q - 1), head_dev(dh, member))
 
     gathers.run(PT["g3"])
-
-    qall, KVT = r["qall"], r["KVT"]
-    for j in range(H):
-        packed = qin[j].astype(f32)
-        qall[pl.ds(j * tl, half), :] = jnp.where(low, packed, 0.0).astype(bf16)
-        qall[pl.ds(j * tl + half, half), :] = jnp.where(low, swap(packed), 0.0).astype(bf16)
 
     ends = []
     total = 0
@@ -573,7 +606,7 @@
     shift[...] = jnp.concatenate(shift_parts, axis=1)
 
     acc[...] = jnp.zeros((LANES, NQ), f32)
-    dkvs, dkvx, dkv_in = r["dkvs"], r["dkvx"], r["dkv_in"]
+    dkvs, dkvx, dkvf = r["dkvs"], r["dkvx"], r["dkvf"]
 
     def key_grads(o):
         prob = r["prob"][o] if p.keep else jnp.exp(masked_scores(o) - top[...]).astype(bf16)
@@ -596,52 +629,67 @@
         for q in range(1, g):
             arrive(dkvx.at[q - 1, k], "dkvx", (q - 1, k), head_dev(dh, add(di, g - q, g)))
             dkv = dkv + dkvx[q - 1, k].astype(f32)
+        dkvf[pl.ds(pl.multiple_of(j * tl, tl), tl), :] = dkv
+        sums.run(PT["s5b"][k * len(PT["s5b"]) // H])
+
+    gmix = r["gmix"]
+    dkv = swap(dkvf[...])
+    gmix[:, pl.ds(0, LANES)] = jnp.where(low, acc[...].T * 0.125, dkv).astype(bf16)
+    gmix[:, pl.ds(LANES, LANES)] = jnp.where(low, dkv, 0.0).astype(bf16)
+    bps, bcx, byx, bzx = r["bps"], r["bcx"], r["byx"], r["bzx"]
+    for k in [*range(1, H), 0]:
+        j = add(dh, k, H)
+        part = nt(gmix[pl.ds(pl.multiple_of(j * tl, tl), tl), :], head_weight)
+        bps[j] = part.astype(bf16).reshape(M, rm, D)
+        send(bps.at[j, m_both], bcx.at[j, 1], "bc", (k, 1), core)
+        send(bps.at[j, m_core], bcx.at[j, 0], "bc", (k, 0), core)
+    sums.run(PT["s6"])
+    dws, dwx, dwin = r["dws"], r["dwx"], r["dwin"]
+    dws[...] = tn(h1[...], gmix[...]).astype(bf16).reshape(R, rb, 2 * LANES)
+    for q in range(1, g):
+        member = add(di, q, g)
+        for k in [*range(1, H), 0]:
+            j = add(dh, k, H)
+            send(dws.at[j * g + member], dwx.at[q - 1, k], "dwx", (q - 1, k), head_dev(dh, member))
+    for k in [*range(1, H), 0]:
+        j = add(dh, k, H)
+        arrive(bcx.at[j, 1], "bc", (k, 1), core)
+        value = bps[j, m_side].astype(f32) + bcx[j, 1].astype(f32)
+        bps[j, m_side] = value.astype(bf16)
+        send(bps.at[j, m_side], byx.at[j], "by", k, side)
+    sums.run(PT["s7"])
+    for k in [*range(1, H), 0]:
+        j = add(dh, k, H)
+        arrive(bcx.at[j, 0], "bc", (k, 0), core)
+        arrive(byx.at[j], "by", k, side)
+        value = bps[j, m].astype(f32) + bcx[j, 0].astype(f32) + byx[j].astype(f32)
         if k:
-            dkvs[0, k] = dkv.astype(bf16)
-            send(dkvs.at[0, k], dkv_in.at[dh], "dkv", k, head_dev(j, di))
+            bps[j, m] = value.astype(bf16)
+            send(bps.at[j, m], bzx.at[dh], "bz", k, head_dev(j, di))
         else:
-            dkv_in[dh] = dkv.astype(bf16)
-        sums.run(PT["s5b"][k * len(PT["s5b"]) // H])
-
-    dqs, dqT = r["dqs"], r["dqT"]
-    for j in range(H):
-        dqs[j] = (acc[pl.ds(0, HEAD_DIM), pl.ds(j * tl, tl)] * 0.125).astype(bf16)
-    for k in range(1, H):
+            back1 = value
+    for k in [*range(1, H), 0]:
         j = add(dh, k, H)
-        send(dqs.at[j], dqT.at[dh], "dq", k, head_dev(j, di))
-    dqT[dh] = dqs[dh]
-    sums.run(PT["s6"])
+        value = dws[j * g + di].astype(f32)
+        for q in range(1, g):
+            arrive(dwx.at[q - 1, k], "dwx", (q - 1, k), head_dev(dh, add(di, g - q, g)))
+            value = value + dwx[q - 1, k].astype(f32)
+        if k:
+            dws[j * g + di] = value.astype(bf16)
+            send(dws.at[j * g + di], dwin.at[dh], "dwz", k, head_dev(j, di))
+        else:
+            dwin[dh] = value.astype(bf16)
+    sums.run(PT["s8"])
 
     res = r["res"]
     res[m] = (mid[...] + rows_sum(2)).astype(bf16)
     gather_send(2, res)
 
-    sums.run(PT["s7"])
+    sums.run(PT["s9"])
     for k in range(1, H):
         h = add(dh, H - k, H)
-        arrive(dqT.at[h], "dq", k, head_dev(h, di))
-        arrive(dkv_in.at[h], "dkv", k, head_dev(h, di))
-
-    gmix = r["gmix"]
-    dq = dqT[...].reshape(HF, tl).astype(f32).T
-
-    def head_sum(h):
-        return dkv_in[h].astype(f32)
-
-    for t in range(H // 2):
-        both = dq[:, t * LANES : (t + 1) * LANES]
-        even = swap(head_sum(2 * t))
-        base = 6 * HEAD_DIM * t
-        gmix[:, pl.ds(base, LANES)] = jnp.where(low, both, even).astype(bf16)
-        gmix[:, pl.ds(base + LANES, LANES)] = jnp.where(low, even, both).astype(bf16)
-        gmix[:, pl.ds(base + 2 * LANES, LANES)] = head_sum(2 * t + 1).astype(bf16)
-
-    grad_part(0, h1[...], gmix)
-    sums.add(0, sum_streams(0, "o_qkv"), PT["sq"], PT["sqp"])
-    sums.run(PT["s8"])
-    rows_send(3, nt(gmix[...], weight(0)))
-    sums.run(PT["s9"])
-    back1 = rows_sum(3)
+        arrive(bzx.at[h], "bz", k, head_dev(h, di))
+        back1 = back1 + bzx[h].astype(f32)
     n1, r1 = norm(r["tok"][own_rows, :])
     gt = r["gt"]
     gt[m] = (gm[...] + norm_back(back1, n1, r1, gain1)).astype(bf16)
@@ -681,6 +729,18 @@
     for k in range(1, M):
         send(lnx.at[m], lnx.at[m], "ln", k - 1, row_peer(k))
     sums.run(100)
+    for k in range(1, H):
+        h = add(dh, H - k, H)
+        arrive(dwin.at[h], "dwz", k, head_dev(h, di))
+    vqkv = r["vo_qkv"]
+    for t in range(H // 2):
+        even0, even1, odd0, odd1 = (
+            dwin[2 * t + b, :, pl.ds(c * LANES, LANES)].astype(f32) for b in (0, 1) for c in (0, 1)
+        )
+        vqkv[:, pl.ds(3 * t * LANES, LANES)] = even0
+        vqkv[:, pl.ds((3 * t + 1) * LANES, LANES)] = jnp.where(low, even1, swap(odd0))
+        vqkv[:, pl.ds((3 * t + 2) * LANES, LANES)] = jnp.where(low, swap(odd0), swap(odd1))
+    leave(vqkv, r["o_qkv"])
 
     gather_end(3, gt)
     leave(gt, r["o_tokens"])
@@ -732,12 +792,12 @@
         "go": v((tl, D), f32),
         "outlow": v((tl, D), bf16),
         "lnp": v((8, D), f32),
-        "h1": v((tl, D), bf16),
-        "h1f": v((tl, D), f32),
+        "raw_qkv": v((rb, 3 * HF), bf16),
+        "N": v((H, M, rm, D), bf16),
+        "ws": v((H, rb, 2 * LANES), bf16),
+        "Win": v((R, rb, 2 * LANES), bf16),
+        "h1": v((NQ, D), bf16),
         "slope": v((tl, U), f32),
-        "qs": v((H, half, LANES), bf16),
-        "kvs": v((H, tl, LANES), bf16),
-        "qin": v((H, half, LANES), bf16),
         "KV": v((R, tl, LANES), bf16),
         "KVT": v((R, LANES, tl), bf16),
         "qall": v((NQ, LANES), bf16),
@@ -751,8 +811,8 @@
         "atts": v((H, HEAD_DIM, tl), bf16),
         "attT": v((H, HEAD_DIM, tl), bf16),
         "att": v((tl, HF), bf16),
-        "rs_send": v((4, M, rm, D), bf16),
-        "rs_recv": v((4, M - 1, rm, D), bf16),
+        "rs_send": v((3, M, rm, D), bf16),
+        "rs_recv": v((3, M - 1, rm, D), bf16),
         "mid": v((rm, D), f32),
         "n2": v((rm, D), f32),
         "r2": v((rm, LANES), f32),
@@ -772,10 +832,15 @@
         "gall": v((NQ, LANES), bf16),
         "dkvs": v((g, H, tl, LANES), bf16),
         "dkvx": v((max(g - 1, 1), H, tl, LANES), bf16),
-        "dkv_in": v((H, tl, LANES), bf16),
-        "dqs": v((H, HEAD_DIM, tl), bf16),
-        "dqT": v((H, HEAD_DIM, tl), bf16),
-        "gmix": v((tl, 3 * HF), bf16),
+        "dkvf": v((NQ, LANES), f32),
+        "gmix": v((NQ, 2 * LANES), bf16),
+        "bps": v((H, M, rm, D), bf16),
+        "bcx": v((H, 2, rm, D), bf16),
+        "byx": v((H, rm, D), bf16),
+        "bzx": v((H, rm, D), bf16),
+        "dws": v((R, rb, 2 * LANES), bf16),
+        "dwx": v((max(g - 1, 1), H, rb, 2 * LANES), bf16),
+        "dwin": v((H, rb, 2 * LANES), bf16),
         "res": v((M, rm, D), bf16),
         "gt": v((M, rm, D), bf16),
     }
@@ -784,24 +849,29 @@
     if p.whole_lanes:
         scratch["raw_out"] = v((HF, rb), bf16)
         scratch["raw_down"] = v((U, rb), bf16)
-        scratch["lnall"] = v((R, 16, rb), bf16)
     for n, (_, _, width, _, hops) in enumerate(p.streams):
         scratch["came%d" % n] = v((hops, rb, width), bf16)
     sems = {
         "wg": (len(p.streams), p.far),
         "gg": (len(p.streams), p.far),
-        "lg": (2, p.far),
         "lr": (R - 1,),
-        "kv": (H,),
-        "q": (H,),
+        "na": (H,),
+        "ny": (H,),
+        "nc": (H,),
+        "nd": (H,),
+        "wa": (H,),
+        "wax": (H, max(g - 1, 1)),
+        "bc": (H, 2),
+        "by": (H,),
+        "bz": (H,),
+        "dwz": (H,),
         "kvx": (H, max(g - 1, 1)),
         "att": (H,),
-        "rs": (4, M - 1),
+        "rs": (3, M - 1),
         "ag": (4, M - 1),
         "ga": (H,),
-        "dkv": (H,),
         "dkvx": (max(g - 1, 1), H),
-        "dq": (H,),
+        "dwx": (max(g - 1, 1), H),
         "ln": (M - 1,),
     }
     for name, shape in sems.items():

time: 165 us -> 159 us (0.964)
  Pallas kernels: 162 us -> 156 us
    pallas_call x1, Pallas kernels: 159 us -> 153 us  [layer(): pl.pallas_call(functools.partial(kernel, p, names), out_shape=[jax.ShapeD...]
where the time goes in v4:
time: 159 us; the launch traced here: 158 us
  Pallas kernels  156 us (98%)
    pallas_call x1, Pallas kernels, layer(): pl.pallas_call(functools.partial(kernel, p, names), out_shape=[jax.ShapeD...  153 us
    pallas_call x1, Pallas kernels, finish(): pl.pallas_call(finish_kernel, out_shape=[jax.ShapeDtypeStruct(shape, f32)...  3.72 us

profile of v4, /device:TPU:0, one launch (start us, length us, event | category | flops | bytes accessed | tf_op | source)
XLA Modules:
  0.0 158.5 jit_solution(9267246997995746356)
XLA Ops:
  0.6 0.0 copy-start.3
  0.7 0.0 copy-start
  0.7 0.0 copy-start.1
  0.7 0.0 copy-start.2
  0.7 0.6 copy-done.3
  1.3 0.0 copy-done
  1.3 0.0 copy-done.1
  1.3 0.0 copy-done.2
  1.3 0.6 fusion.6.refs_6_
  2.0 152.6 %layer.1 = (bf16[4,64,1024]{2,1,0:T(8,128)(2,1)}, bf16[4,64,1024]{2,1,0:T(8,128)(2,1)}, f32[128,768]{1,0:T(8,128)}, f32[128,256]{1,0:T(8,128)}, f32[128,1024]{1,...) custom-call(f32[256,1024]{1,0:T(8,128)} %refs_0_.1, f32[256,1024]{1,0:T(8,128)} %refs_1_.1, bf16[128,768]{1,0:T(8,128)(2,1)} %refs_2_.1, ...), custom_call_target="tpu_custom_call" | custom-call | flops 5502926848 | bytes 8388608 | tf_op jit(solution)/shard_map/layer/pallas_call | solution.py:885
  154.6 3.7 %finish.1 = (f32[256,1024]{1,0:T(8,128)}, f32[256,1024]{1,0:T(8,128)}, f32[128,768]{1,0:T(8,128)}, f32[256,128]{1,0:T(8,128)}, f32[128,1024]{1,0:T(8,128)}, /*in...) custom-call(bf16[4,64,1024]{2,1,0:T(8,128)(2,1)} %get-tuple-element.17.refs_0_, ...), custom_call_target="tpu_custom_call" | custom-call | bytes 6291456 | tf_op jit(solution)/shard_map/finish/pallas_call | solution.py:934
Async XLA Ops:
  0.6 0.7 copy-start.3
  0.7 0.7 copy-start
  0.7 0.7 copy-start.1
  0.7 0.7 copy-start.2

commit v5 on v4

--- a/solution.py
+++ b/solution.py
@@ -1,4 +1,5 @@
 import functools
+import types
 
 import jax
 import jax.numpy as jnp
@@ -11,44 +12,46 @@
 LANES = 128
 FAR = -1e30
 MESH = pl.DeviceIdType.MESH
-PT = {
-    "g1b": -4.6,
-    "g0": 2.5,
-    "o0": 1.8,
-    "op": 0.96,
-    "u0": 1.3,
-    "d0": 4.5,
-    "g1": 2.8,
-    "g2": 4.3,
-    "g3": -1.5,
-    "g4": [1.7, 4.5, 1.8, 3.1, 3.6, 1.3, 4.6, 5.2],
-    "g5": [4.9, 5.4, 4.0, 5.1, 4.8, 4.5, 2.2, 5.4],
-    "g6": -11.4,
-    "g7": -10.9,
-    "g8": 7.2,
-    "g9": 8.3,
-    "su": 0.3,
-    "s1": -1.5,
-    "s2": 3.0,
-    "s3": 2.5,
-    "so": 2.1,
-    "sop": 1.6,
-    "s4": 3.2,
-    "s4b": [-13.5, -8.0, -5.3, -8.1],
-    "s5": -2.7,
-    "s5b": [-11.3, -5.4, -4.8, -6.8],
-    "s6": 5.2,
-    "s7": 5.3,
-    "sq": 9.5,
-    "sqp": 0.5,
-    "up": 1.44,
-    "dp": 0.98,
-    "sdp": 1.54,
-    "sup": 1.42,
-    "s8": 6.7,
-    "s9": -4.0,
-    "s10": 7.3,
-}
+class PT:
+    g1b = -4.6
+    g0 = 2.5
+    o0 = 1.8
+    op = 0.96
+    u0 = 1.3
+    d0 = 4.6
+    g1 = 2.8
+    g2 = 4.4
+    g3 = -2.5
+    g4 = [0.7, 3.5, 2.8, 1.2, 3.9, 1.3, 4.6, 5.2]
+    g5 = [4.9, 5.2, 4.2, 5.1, 4.9, 5.1, 2.2, 4.4]
+    g6 = -11.7
+    g7 = -11.2
+    g8 = 6.9
+    g9 = 8.0
+    su = 0.25
+    s1 = -1.5
+    s2 = 2.6
+    s3 = 2.5
+    so = 2.7
+    sop = 1.6
+    s4 = 4.2
+    s4b = [-13.5, -6.9, -6.2, -7.4]
+    s5 = -2.6
+    s5b = [-11.2, -5.3, -2.7, -4.7]
+    s6 = 5.3
+    s7 = 6.0
+    sq = 9.5
+    sqp = 0.44
+    up = 1.44
+    dp = 1.0
+    sdp = 1.56
+    sup = 1.48
+    s8 = 5.1
+    s9 = -3.7
+    s10 = 8.3
+
+
+TWO_STEPS = (3,)
 bf16 = jnp.bfloat16
 f32 = jnp.float32
 
@@ -100,7 +103,7 @@
 
 
 def kernel(p, names, *refs):
-    r = dict(zip(names, refs))
+    r = types.SimpleNamespace(**dict(zip(names, refs)))
     R, M, L, H, g = p.R, p.M, p.L, p.H, p.g
     tl, D, rb, rm, U, HF, NQ = p.tl, p.D, p.rb, p.rm, p.U, p.HF, p.NQ
     half = tl // 2
@@ -117,8 +120,8 @@
         return pltpu.make_async_remote_copy(
             src_ref=src,
             dst_ref=dst,
-            send_sem=r[name + "_s"].at[index],
-            recv_sem=r[name + "_r"].at[index],
+            send_sem=getattr(r, name + "_s").at[index],
+            recv_sem=getattr(r, name + "_r").at[index],
             device_id=peer,
             device_id_type=MESH,
         )
@@ -134,6 +137,8 @@
     def head_dev(h, member):
         return (h * g + member, m)
 
+    h_near, h_far = dh + 1 - 2 * lax.rem(dh, 2), lax.rem(dh + 2, H)
+    h_both = lax.rem(h_near + 2, H)
     m_side, m_core = lax.rem(m + 2, M), m + 1 - 2 * lax.rem(m, 2)
     m_both = lax.rem(m_core + 2, M)
     side, core = (d, m_side), (d, m_core)
@@ -148,7 +153,7 @@
         far = q // L
         return 2 * q * (1 - far) + (2 * (R - 1 - q) + 1) * far
 
-    W = r["W"]
+    W = r.W
 
     def wcols(b, c0, width):
         return W.at[b, :, pl.ds(c0, width)]
@@ -156,15 +161,15 @@
     local = []
     for n, (src, dst) in enumerate(
         [
-            (r["w_qkv"], r["raw_qkv"]),
-            (r["tokens"], r["tok"]),
-            (r["w_up"], wcols(d, *p.cols[2])),
-            (r["w_out"], r["raw_out"] if p.whole_lanes else wcols(d, *p.cols[1])),
-            (r["w_down"], r["raw_down"] if p.whole_lanes else wcols(d, *p.cols[3])),
-            (r["grad_out"], r["go"]),
+            (r.w_qkv, r.raw_qkv),
+            (r.tokens, r.tok),
+            (r.w_up, wcols(d, *p.cols[2])),
+            (r.w_out, r.raw_out if p.whole_lanes else wcols(d, *p.cols[1])),
+            (r.w_down, r.raw_down if p.whole_lanes else wcols(d, *p.cols[3])),
+            (r.grad_out, r.go),
         ]
     ):
-        one = pltpu.make_async_copy(src, dst, r["loc"].at[n])
+        one = pltpu.make_async_copy(src, dst, r.loc.at[n])
         one.start()
         local.append(one)
 
@@ -188,16 +193,16 @@
     def swap(v):
         return pltpu.roll(v, HEAD_DIM, 1)
 
-    N, ws, Win = r["N"], r["ws"], r["Win"]
+    N, ws, Win = r.N, r.ws, r.Win
     local[0].wait()
     vectors = 0.0
     if p.whole_lanes:
         before = jnp.zeros((HEAD_DIM, rb), f32)
         after = jnp.zeros((HEAD_DIM - 16, rb), f32)
-        vectors = jnp.concatenate([before, r["ln_in"][...].astype(f32), after], axis=0).T
+        vectors = jnp.concatenate([before, r.ln_in[...].astype(f32), after], axis=0).T
     for t in range(H // 2):
         t0, t1, t2 = (
-            r["raw_qkv"][:, pl.ds((3 * t + k) * LANES, LANES)].astype(f32) for k in range(3)
+            r.raw_qkv[:, pl.ds((3 * t + k) * LANES, LANES)].astype(f32) for k in range(3)
         )
         ws[2 * t, :, pl.ds(0, LANES)] = t0.astype(bf16)
         ws[2 * t, :, pl.ds(LANES, LANES)] = jnp.where(low, t1, vectors).astype(bf16)
@@ -208,13 +213,14 @@
     def norm_quarter(b):
         for c in range(rm // 32):
             first = pl.multiple_of(b * rm + c * 32, 32)
-            N[dh, b, pl.ds(c * 32, 32), :] = norm(r["tok"][pl.ds(first, 32), :])[0].astype(bf16)
+            N[dh, b, pl.ds(c * 32, 32), :] = norm(r.tok[pl.ds(first, 32), :])[0].astype(bf16)
 
     norm_quarter(m)
     pl.semaphore_wait(barrier, len(greeted))
+    send(N.at[dh, m], N.at[dh, m], "na", 2, head_dev(h_far, di))
+    send(N.at[dh, m], N.at[dh, m], "na", 1, head_dev(h_near, di))
     for k in range(1, H):
         h = add(dh, k, H)
-        send(N.at[dh, m], N.at[dh, m], "na", k, head_dev(h, di))
         send(ws.at[h], Win.at[d], "wa", k, head_dev(h, di))
     Win[d] = ws[dh]
     for q in range(1, g):
@@ -271,36 +277,40 @@
         return W[:, :, pl.ds(c0 + first, width)].reshape(D, width)
 
     gathers = Queue()
-    lnp = r["lnp"]
+    lnp = r.lnp
     if not p.whole_lanes:
-        lnp[...] = r["ln_in"][...].astype(f32)[0:8, :]
-    gathers.add(1, gather_streams(1), PT["o0"], PT["op"])
-    gathers.add(2, gather_streams(2), PT["u0"], PT["up"])
-    gathers.add(3, gather_streams(3), PT["d0"], PT["dp"])
+        lnp[...] = r.ln_in[...].astype(f32)[0:8, :]
+    gathers.add(1, gather_streams(1), PT.o0, PT.op)
+    gathers.add(2, gather_streams(2), PT.u0, PT.up)
+    gathers.add(3, gather_streams(3), PT.d0, PT.dp)
     gathers.run(0)
     for k in range(1, M):
         norm_quarter(add(m, k, M))
     for n in range(2, 6):
         local[n].wait()
     if p.whole_lanes:
-        for raw, (c0, width) in ((r["raw_out"], p.cols[1]), (r["raw_down"], p.cols[3])):
+        for raw, (c0, width) in ((r.raw_out, p.cols[1]), (r.raw_down, p.cols[3])):
             W[d, :, pl.ds(c0, width)] = raw[...].astype(f32).T.astype(bf16)
 
-    outlow = r["outlow"]
-    outlow[...] = r["go"][...].astype(bf16)
-
+    outlow = r.outlow
+    outlow[...] = r.go[...].astype(bf16)
+
+    passed = {1: (2, h_far, h_far), 2: (1, h_near, h_near), 3: (3, h_both, h_near)}
     for k in range(1, H):
+        n, j, giver = passed[k]
+        arrive(N.at[j, m], "na", n, head_dev(giver, di))
+        if k == 1:
+            send(N.at[j, m], N.at[j, m], "na", 3, head_dev(h_near, di))
+        send(N.at[j, m], N.at[j, m], "ny", k, side)
+        send(N.at[j, m], N.at[j, m], "nc", k, core)
         j = add(dh, H - k, H)
         own = j * g + di
-        arrive(N.at[j, m], "na", k, head_dev(j, di))
-        send(N.at[j, m], N.at[j, m], "ny", k, side)
-        send(N.at[j, m], N.at[j, m], "nc", k, core)
         arrive(Win.at[own], "wa", k, head_dev(j, di))
         for q in range(1, g):
             send(Win.at[own], Win.at[own], "wax", (k, q - 1), head_dev(dh, add(di, q, g)))
-        gathers.run(PT["g0"])
+        gathers.run(PT.g0)
     for k in range(1, H):
-        j = add(dh, H - k, H)
+        j = passed[k][1]
         arrive(N.at[j, m_side], "ny", k, side)
         send(N.at[j, m_side], N.at[j, m_side], "nd", k, core)
     for k in range(H):
@@ -321,22 +331,22 @@
             - normed * jnp.mean(scaled * normed, axis=-1, keepdims=True)
         )
 
-    h1 = r["h1"]
+    h1 = r.h1
 
     def hidden(j):
         part = N[j].reshape(tl, D).astype(f32) * gain1 + bias1
         h1[pl.ds(pl.multiple_of(j * tl, tl), tl), :] = part.astype(bf16)
 
     hidden(dh)
-    gathers.run(PT["g1"])
+    gathers.run(PT.g1)
     for k in range(1, H):
-        j = add(dh, H - k, H)
+        j = passed[k][1]
         arrive(N.at[j, m_core], "nc", k, core)
         arrive(N.at[j, m_both], "nd", k, core)
         hidden(j)
-        gathers.run(PT["g1b"])
-
-    KV, qall, KVT = r["KV"], r["qall"], r["KVT"]
+        gathers.run(PT.g1b)
+
+    KV, qall, KVT = r.KV, r.qall, r.KVT
     head_weight = Win[...].reshape(D, 2 * LANES)
     for k in range(H):
         j = add(dh, H - k, H)
@@ -348,19 +358,19 @@
         for q in range(1, g):
             own = j * g + di
             send(KV.at[own], KV.at[own], "kvx", (k, q - 1), head_dev(dh, add(di, q, g)))
-    gathers.run(PT["g2"])
+    gathers.run(PT.g2)
     for k in range(H):
         j = add(dh, H - k, H)
         for q in range(1, g):
             member = add(di, g - q, g)
             arrive(KV.at[j * g + member], "kvx", (k, q - 1), head_dev(dh, member))
 
-    gathers.run(PT["g3"])
+    gathers.run(PT.g3)
 
     ends = []
     total = 0
     for k in range(p.scenes):
-        total = total + r["scene"][k]
+        total = total + r.scene[k]
         ends.append(total)
 
     def scene_of(pos):
@@ -384,7 +394,7 @@
         == lax.broadcasted_iota(jnp.int32, (LANES, LANES), 1)
     ).astype(bf16)
 
-    top8, sum8, acc = r["top8"], r["sum8"], r["acc"]
+    top8, sum8, acc = r.top8, r.sum8, r.acc
     top8[...] = jnp.full((8, NQ), FAR, f32)
     sum8[...] = jnp.zeros((8, NQ), f32)
     acc[...] = jnp.zeros((LANES, NQ), f32)
@@ -402,9 +412,9 @@
             pl.loop(c * R // pieces, (c + 1) * R // pieces)(body)
             gathers.run(places[c * len(places) // pieces])
 
-    in_pieces(maxima, PT["g4"])
-
-    top = r["top"]
+    in_pieces(maxima, PT.g4)
+
+    top = r.top
     top[...] = jnp.max(top8[...], axis=0, keepdims=True)
 
     def exponentials(o):
@@ -412,15 +422,15 @@
         sum8[...] += jnp.sum(expo.reshape(tl // 8, 8, NQ), axis=0)
         low_expo = expo.astype(bf16)
         if p.keep:
-            r["prob"][o] = low_expo
+            r.prob[o] = low_expo
         acc[...] += nn(KVT[o], low_expo)
 
-    in_pieces(exponentials, PT["g5"])
+    in_pieces(exponentials, PT.g5)
 
     scale_row = 1.0 / jnp.sum(sum8[...], axis=0, keepdims=True)
-    inv = r["inv"]
+    inv = r.inv
     inv[...] = scale_row
-    attf, atts, attT = r["attf"], r["atts"], r["attT"]
+    attf, atts, attT = r.attf, r.atts, r.attT
     attf[...] = acc[pl.ds(HEAD_DIM, HEAD_DIM), :] * scale_row
     for j in range(H):
         atts[j] = attf[:, pl.ds(j * tl, tl)].astype(bf16)
@@ -428,14 +438,14 @@
         j = add(dh, k, H)
         send(atts.at[j], attT.at[dh], "att", k, head_dev(j, di))
     attT[dh] = atts[dh]
-    gathers.run(PT["g6"])
+    gathers.run(PT.g6)
     for k in range(1, H):
         h = add(dh, H - k, H)
         arrive(attT.at[h], "att", k, head_dev(h, di))
-    att = r["att"]
+    att = r.att
     att[...] = attT[...].reshape(HF, tl).astype(f32).T.astype(bf16)
 
-    rs_send, rs_recv = r["rs_send"], r["rs_recv"]
+    rs_send, rs_recv = r.rs_send, r.rs_recv
 
     def rows_send(n, values):
         rs_send[n] = values.astype(bf16).reshape(M, rm, D)
@@ -450,32 +460,42 @@
         return value
 
     def gather_send(n, ref):
+        if n in TWO_STEPS:
+            send(ref.at[m], ref.at[m], "ah", (n, 0), side)
+            send(ref.at[m], ref.at[m], "ah", (n, 1), core)
+            return
         for k in range(1, M):
             send(ref.at[m], ref.at[m], "ag", (n, k - 1), row_peer(k))
 
     def gather_end(n, ref):
+        if n in TWO_STEPS:
+            arrive(ref.at[m_side], "ah", (n, 0), side)
+            send(ref.at[m_side], ref.at[m_side], "ah", (n, 2), core)
+            arrive(ref.at[m_core], "ah", (n, 1), core)
+            arrive(ref.at[m_both], "ah", (n, 2), core)
+            return
         for k in range(1, M):
             b = add(m, M - k, M)
             arrive(ref.at[b], "ag", (n, k - 1), row_peer(M - k))
 
-    gathers.run(PT["g7"])
+    gathers.run(PT.g7)
     gathers.need(1)
     rows_send(0, nt(att[...], weight(1)))
-    gathers.run(PT["g8"])
+    gathers.run(PT.g8)
     own_rows = pl.ds(pl.multiple_of(m * rm, rm), rm)
-    mid, n2, r2, h2 = r["mid"], r["n2"], r["r2"], r["h2"]
-    middle = r["tok"][own_rows, :] + rows_sum(0)
+    mid, n2, r2, h2 = r.mid, r.n2, r.r2, r.h2
+    middle = r.tok[own_rows, :] + rows_sum(0)
     mid[...] = middle
     normed, inverse = norm(middle)
     n2[...] = normed
     r2[...] = jnp.broadcast_to(inverse, (rm, LANES))
     h2[m] = (normed * gain2 + bias2).astype(bf16)
     gather_send(0, h2)
-    gathers.run(PT["g9"])
+    gathers.run(PT.g9)
     gathers.need(2)
     gather_end(0, h2)
 
-    active, il, slope = r["active"], r["il"], r["slope"]
+    active, il, slope = r.active, r.il, r.slope
     c_one, c_two = 0.7978845608028654, 0.044715
     step = 256
     for c in range(U // step):
@@ -491,7 +511,7 @@
 
     def grad_part(s, lhs, rhs):
         c0, width = p.cols[s]
-        G = r["G"]
+        G = r.G
         piece = 256 if width % 256 == 0 else LANES
         for c in range(width // piece):
             value = tn(lhs, rhs[:, pl.ds(c * piece, piece)]).astype(bf16)
@@ -500,15 +520,15 @@
     leaving = []
 
     def leave(value, out):
-        one = pltpu.make_async_copy(value, out, r["out"].at[len(leaving)])
+        one = pltpu.make_async_copy(value, out, r.out.at[len(leaving)])
         one.start()
         leaving.append(one)
 
     def sum_steps(n, stream, name):
-        held, out = r["v" + name], r[name]
+        held, out = getattr(r, "v" + name), getattr(r, name)
         s, first, width, way, hops = stream
         columns = pl.ds(p.cols[s][0] + first, width)
-        G, came = r["G"], r["came%d" % n]
+        G, came = r.G, getattr(r, "came%d" % n)
         onward, before = (ring(pos + way), m), (ring(pos - way), m)
 
         def step(t):
@@ -541,7 +561,7 @@
         ]
 
     grad_part(3, outlow[...], active)
-    sums.add(3, sum_streams(3, "o_down"), 0, PT["sdp"])
+    sums.add(3, sum_streams(3, "o_down"), 0, PT.sdp)
     sums.run(0)
     gathers.need(3)
     for c in range(U // step):
@@ -550,26 +570,26 @@
     rows_send(1, nt(il[...], weight(2)))
 
     grad_part(2, h2[...].reshape(tl, D), il)
-    sums.add(2, sum_streams(2, "o_up"), PT["su"], PT["sup"])
-    sums.run(PT["s1"])
+    sums.add(2, sum_streams(2, "o_up"), PT.su, PT.sup)
+    sums.run(PT.s1)
     rows_send(2, nt(active[...], weight(3)))
-    sums.run(PT["s2"])
+    sums.run(PT.s2)
     back2 = rows_sum(1)
-    gm, ml = r["gm"], r["ml"]
-    grad_middle = r["go"][own_rows, :] + norm_back(back2, n2[...], r2[:, 0:1], gain2)
+    gm, ml = r.gm, r.ml
+    grad_middle = r.go[own_rows, :] + norm_back(back2, n2[...], r2[:, 0:1], gain2)
     gm[...] = grad_middle
     ml[m] = grad_middle.astype(bf16)
     gather_send(1, ml)
 
-    sums.run(PT["s3"])
-    ln2g, ln2b = r["ln2g"], r["ln2b"]
+    sums.run(PT.s3)
+    ln2g, ln2b = r.ln2g, r.ln2b
     ln2g[...] = jnp.sum(back2 * n2[...], axis=0, keepdims=True)
     ln2b[...] = jnp.sum(back2, axis=0, keepdims=True)
 
     gather_end(1, ml)
     midlow = ml[...].reshape(tl, D)
 
-    gs, gin, gall = r["gs"], r["gin"], r["gall"]
+    gs, gin, gall = r.gs, r.gin, r.gall
     gatt = nn(midlow, weight(1))
     for h in range(H):
         tile = gatt[:, (h // 2) * LANES : (h // 2 + 1) * LANES]
@@ -583,11 +603,15 @@
     gin[dh] = gs[dh]
 
     grad_part(1, midlow, att)
-    sums.add(1, sum_streams(1, "o_out"), PT["so"], PT["sop"])
-    sums.run(PT["s4"])
+    sums.add(1, sum_streams(1, "o_out"), PT.so, PT.sop)
+    sums.run(PT.s4)
     for k in range(1, H):
         j = add(dh, H - k, H)
         arrive(gin.at[j], "ga", k, head_dev(j, di))
+
+    res = r.res
+    res[m] = (mid[...] + rows_sum(2)).astype(bf16)
+    gather_send(2, res)
 
     inv_col = jnp.broadcast_to(inv[...], (LANES, NQ)).T
     shift_parts = []
@@ -602,14 +626,14 @@
             * inv[:, pl.ds(j * tl, tl)]
         )
         gall[pl.ds(j * tl, tl), :] = (ga * inv_col[j * tl : (j + 1) * tl]).astype(bf16)
-    shift = r["shift"]
+    shift = r.shift
     shift[...] = jnp.concatenate(shift_parts, axis=1)
 
     acc[...] = jnp.zeros((LANES, NQ), f32)
-    dkvs, dkvx, dkvf = r["dkvs"], r["dkvx"], r["dkvf"]
+    dkvs, dkvx, dkvf = r.dkvs, r.dkvx, r.dkvf
 
     def key_grads(o):
-        prob = r["prob"][o] if p.keep else jnp.exp(masked_scores(o) - top[...]).astype(bf16)
+        prob = r.prob[o] if p.keep else jnp.exp(masked_scores(o) - top[...]).astype(bf16)
         dprob = nt(KV[o], gall[...])
         dscore = (prob.astype(f32) * (dprob - shift[...])).astype(bf16)
         acc[...] += nn(KVT[o], dscore)
@@ -621,8 +645,8 @@
             j = add(dh, k, H)
             dkvs[q, k] = key_grads(j * g + member).astype(bf16)
             send(dkvs.at[q, k], dkvx.at[q - 1, k], "dkvx", (q - 1, k), head_dev(dh, member))
-            sums.run(PT["s4b"][k * len(PT["s4b"]) // H])
-        sums.run(PT["s5"])
+            sums.run(PT.s4b[k * len(PT.s4b) // H])
+        sums.run(PT.s5)
     for k in [*range(1, H), 0]:
         j = add(dh, k, H)
         dkv = key_grads(j * g + di)
@@ -630,21 +654,21 @@
             arrive(dkvx.at[q - 1, k], "dkvx", (q - 1, k), head_dev(dh, add(di, g - q, g)))
             dkv = dkv + dkvx[q - 1, k].astype(f32)
         dkvf[pl.ds(pl.multiple_of(j * tl, tl), tl), :] = dkv
-        sums.run(PT["s5b"][k * len(PT["s5b"]) // H])
-
-    gmix = r["gmix"]
+        sums.run(PT.s5b[k * len(PT.s5b) // H])
+
+    gmix = r.gmix
     dkv = swap(dkvf[...])
     gmix[:, pl.ds(0, LANES)] = jnp.where(low, acc[...].T * 0.125, dkv).astype(bf16)
     gmix[:, pl.ds(LANES, LANES)] = jnp.where(low, dkv, 0.0).astype(bf16)
-    bps, bcx, byx, bzx = r["bps"], r["bcx"], r["byx"], r["bzx"]
+    bps, bcx, byx, bzx = r.bps, r.bcx, r.byx, r.bzx
     for k in [*range(1, H), 0]:
         j = add(dh, k, H)
         part = nt(gmix[pl.ds(pl.multiple_of(j * tl, tl), tl), :], head_weight)
         bps[j] = part.astype(bf16).reshape(M, rm, D)
         send(bps.at[j, m_both], bcx.at[j, 1], "bc", (k, 1), core)
         send(bps.at[j, m_core], bcx.at[j, 0], "bc", (k, 0), core)
-    sums.run(PT["s6"])
-    dws, dwx, dwin = r["dws"], r["dwx"], r["dwin"]
+    sums.run(PT.s6)
+    dws, dwx, dwin = r.dws, r.dwx, r.dwin
     dws[...] = tn(h1[...], gmix[...]).astype(bf16).reshape(R, rb, 2 * LANES)
     for q in range(1, g):
         member = add(di, q, g)
@@ -657,7 +681,7 @@
         value = bps[j, m_side].astype(f32) + bcx[j, 1].astype(f32)
         bps[j, m_side] = value.astype(bf16)
         send(bps.at[j, m_side], byx.at[j], "by", k, side)
-    sums.run(PT["s7"])
+    sums.run(PT.s7)
     for k in [*range(1, H), 0]:
         j = add(dh, k, H)
         arrive(bcx.at[j, 0], "bc", (k, 0), core)
@@ -679,19 +703,16 @@
             send(dws.at[j * g + di], dwin.at[dh], "dwz", k, head_dev(j, di))
         else:
             dwin[dh] = value.astype(bf16)
-    sums.run(PT["s8"])
-
-    res = r["res"]
-    res[m] = (mid[...] + rows_sum(2)).astype(bf16)
-    gather_send(2, res)
-
-    sums.run(PT["s9"])
+    sums.run(PT.s8)
+
+
+    sums.run(PT.s9)
     for k in range(1, H):
         h = add(dh, H - k, H)
         arrive(bzx.at[h], "bz", k, head_dev(h, di))
         back1 = back1 + bzx[h].astype(f32)
-    n1, r1 = norm(r["tok"][own_rows, :])
-    gt = r["gt"]
+    n1, r1 = norm(r.tok[own_rows, :])
+    gt = r.gt
     gt[m] = (gm[...] + norm_back(back1, n1, r1, gain1)).astype(bf16)
     gather_send(3, gt)
     ln_rows = jnp.concatenate(
@@ -704,7 +725,7 @@
         ],
         axis=0,
     )
-    lnrow, lnr_in = r["lnrow"], r["lnr_in"]
+    lnrow, lnr_in = r.lnrow, r.lnr_in
     for b in range(D // LANES):
         lnrow[b] = ln_rows[:, b * LANES : (b + 1) * LANES]
 
@@ -715,7 +736,7 @@
         o = add(d, k, R)
         send(lnrow.at[lane_block(o)], lnr_in.at[d], "lr", k - 1, (o, m))
     lnr_in[d] = lnrow[lane_block(d)]
-    sums.run(PT["s10"])
+    sums.run(PT.s10)
     for k in range(1, R):
         o = add(d, R - k, R)
         arrive(lnr_in.at[o], "lr", k - 1, (o, m))
@@ -723,8 +744,8 @@
     for b in range(1, R):
         value = value + lnr_in[b]
     gather_end(2, res)
-    leave(res, r["o_result"])
-    lnx = r["lnx"]
+    leave(res, r.o_result)
+    lnx = r.lnx
     lnx[m] = value
     for k in range(1, M):
         send(lnx.at[m], lnx.at[m], "ln", k - 1, row_peer(k))
@@ -732,7 +753,7 @@
     for k in range(1, H):
         h = add(dh, H - k, H)
         arrive(dwin.at[h], "dwz", k, head_dev(h, di))
-    vqkv = r["vo_qkv"]
+    vqkv = r.vo_qkv
     for t in range(H // 2):
         even0, even1, odd0, odd1 = (
             dwin[2 * t + b, :, pl.ds(c * LANES, LANES)].astype(f32) for b in (0, 1) for c in (0, 1)
@@ -740,16 +761,16 @@
         vqkv[:, pl.ds(3 * t * LANES, LANES)] = even0
         vqkv[:, pl.ds((3 * t + 1) * LANES, LANES)] = jnp.where(low, even1, swap(odd0))
         vqkv[:, pl.ds((3 * t + 2) * LANES, LANES)] = jnp.where(low, swap(odd0), swap(odd1))
-    leave(vqkv, r["o_qkv"])
+    leave(vqkv, r.o_qkv)
 
     gather_end(3, gt)
-    leave(gt, r["o_tokens"])
+    leave(gt, r.o_tokens)
     for k in range(1, M):
         arrive(lnx.at[add(m, M - k, M)], "ln", k - 1, row_peer(M - k))
     value = lnx[0]
     for k in range(1, M):
         value = value + lnx[k]
-    r["o_ln"][...] = value
+    r.o_ln[...] = value
     for one in leaving:
         one.wait()
     for one in sent:
@@ -760,125 +781,126 @@
     R, M, L, H, g = p.R, p.M, p.L, p.H, p.g
     tl, D, rb, rm, U, HF, NQ = p.tl, p.D, p.rb, p.rm, p.U, p.HF, p.NQ
     half = tl // 2
-    ins = {
-        "tokens": tokens,
-        "grad_out": grad_out,
-        "w_qkv": w_qkv,
-        "w_out": w_out,
-        "w_up": w_up,
-        "w_down": w_down,
-        "ln_in": ln_in,
-        "scene": scene,
-    }
-    outs = {
-        "o_result": ((M, rm, D), bf16),
-        "o_tokens": ((M, rm, D), bf16),
-        "o_qkv": ((rb, 3 * HF), f32),
-        "o_out": ((rb, HF), f32),
-        "o_up": ((rb, U), f32),
-        "o_down": ((rb, U), f32),
-        "o_ln": ((8, LANES), f32),
-    }
+    ins = dict(
+        tokens=tokens,
+        grad_out=grad_out,
+        w_qkv=w_qkv,
+        w_out=w_out,
+        w_up=w_up,
+        w_down=w_down,
+        ln_in=ln_in,
+        scene=scene,
+    )
+    outs = dict(
+        o_result=((M, rm, D), bf16),
+        o_tokens=((M, rm, D), bf16),
+        o_qkv=((rb, 3 * HF), f32),
+        o_out=((rb, HF), f32),
+        o_up=((rb, U), f32),
+        o_down=((rb, U), f32),
+        o_ln=((8, LANES), f32),
+    )
     v = pltpu.VMEM
     space = pl.BlockSpec(memory_space=pltpu.HBM)
     out_specs = [space] * 6 + [pl.BlockSpec(memory_space=pltpu.VMEM)]
-    scratch = {
-        "vo_qkv": v((rb, 3 * HF), f32),
-        "vo_out": v((rb, HF), f32),
-        "vo_up": v((rb, U), f32),
-        "vo_down": v((rb, U), f32),
-        "W": v((R, rb, p.WC), bf16),
-        "tok": v((tl, D), f32),
-        "go": v((tl, D), f32),
-        "outlow": v((tl, D), bf16),
-        "lnp": v((8, D), f32),
-        "raw_qkv": v((rb, 3 * HF), bf16),
-        "N": v((H, M, rm, D), bf16),
-        "ws": v((H, rb, 2 * LANES), bf16),
-        "Win": v((R, rb, 2 * LANES), bf16),
-        "h1": v((NQ, D), bf16),
-        "slope": v((tl, U), f32),
-        "KV": v((R, tl, LANES), bf16),
-        "KVT": v((R, LANES, tl), bf16),
-        "qall": v((NQ, LANES), bf16),
-        "top8": v((8, NQ), f32),
-        "sum8": v((8, NQ), f32),
-        "top": v((1, NQ), f32),
-        "inv": v((1, NQ), f32),
-        "shift": v((1, NQ), f32),
-        "acc": v((LANES, NQ), f32),
-        "attf": v((HEAD_DIM, NQ), f32),
-        "atts": v((H, HEAD_DIM, tl), bf16),
-        "attT": v((H, HEAD_DIM, tl), bf16),
-        "att": v((tl, HF), bf16),
-        "rs_send": v((3, M, rm, D), bf16),
-        "rs_recv": v((3, M - 1, rm, D), bf16),
-        "mid": v((rm, D), f32),
-        "n2": v((rm, D), f32),
-        "r2": v((rm, LANES), f32),
-        "h2": v((M, rm, D), bf16),
-        "active": v((tl, U), bf16),
-        "il": v((tl, U), bf16),
-        "gm": v((rm, D), f32),
-        "ml": v((M, rm, D), bf16),
-        "ln2g": v((1, D), f32),
-        "ln2b": v((1, D), f32),
-        "lnrow": v((D // LANES, 8, LANES), f32),
-        "lnr_in": v((R, 8, LANES), f32),
-        "lnx": v((M, 8, LANES), f32),
-        "G": v((R, rb, p.WC), bf16),
-        "gs": v((H, half, LANES), bf16),
-        "gin": v((H, half, LANES), bf16),
-        "gall": v((NQ, LANES), bf16),
-        "dkvs": v((g, H, tl, LANES), bf16),
-        "dkvx": v((max(g - 1, 1), H, tl, LANES), bf16),
-        "dkvf": v((NQ, LANES), f32),
-        "gmix": v((NQ, 2 * LANES), bf16),
-        "bps": v((H, M, rm, D), bf16),
-        "bcx": v((H, 2, rm, D), bf16),
-        "byx": v((H, rm, D), bf16),
-        "bzx": v((H, rm, D), bf16),
-        "dws": v((R, rb, 2 * LANES), bf16),
-        "dwx": v((max(g - 1, 1), H, rb, 2 * LANES), bf16),
-        "dwin": v((H, rb, 2 * LANES), bf16),
-        "res": v((M, rm, D), bf16),
-        "gt": v((M, rm, D), bf16),
-    }
+    scratch = dict(
+        vo_qkv=v((rb, 3 * HF), f32),
+        vo_out=v((rb, HF), f32),
+        vo_up=v((rb, U), f32),
+        vo_down=v((rb, U), f32),
+        W=v((R, rb, p.WC), bf16),
+        tok=v((tl, D), f32),
+        go=v((tl, D), f32),
+        outlow=v((tl, D), bf16),
+        lnp=v((8, D), f32),
+        raw_qkv=v((rb, 3 * HF), bf16),
+        N=v((H, M, rm, D), bf16),
+        ws=v((H, rb, 2 * LANES), bf16),
+        Win=v((R, rb, 2 * LANES), bf16),
+        h1=v((NQ, D), bf16),
+        slope=v((tl, U), f32),
+        KV=v((R, tl, LANES), bf16),
+        KVT=v((R, LANES, tl), bf16),
+        qall=v((NQ, LANES), bf16),
+        top8=v((8, NQ), f32),
+        sum8=v((8, NQ), f32),
+        top=v((1, NQ), f32),
+        inv=v((1, NQ), f32),
+        shift=v((1, NQ), f32),
+        acc=v((LANES, NQ), f32),
+        attf=v((HEAD_DIM, NQ), f32),
+        atts=v((H, HEAD_DIM, tl), bf16),
+        attT=v((H, HEAD_DIM, tl), bf16),
+        att=v((tl, HF), bf16),
+        rs_send=v((3, M, rm, D), bf16),
+        rs_recv=v((3, M - 1, rm, D), bf16),
+        mid=v((rm, D), f32),
+        n2=v((rm, D), f32),
+        r2=v((rm, LANES), f32),
+        h2=v((M, rm, D), bf16),
+        active=v((tl, U), bf16),
+        il=v((tl, U), bf16),
+        gm=v((rm, D), f32),
+        ml=v((M, rm, D), bf16),
+        ln2g=v((1, D), f32),
+        ln2b=v((1, D), f32),
+        lnrow=v((D // LANES, 8, LANES), f32),
+        lnr_in=v((R, 8, LANES), f32),
+        lnx=v((M, 8, LANES), f32),
+        G=v((R, rb, p.WC), bf16),
+        gs=v((H, half, LANES), bf16),
+        gin=v((H, half, LANES), bf16),
+        gall=v((NQ, LANES), bf16),
+        dkvs=v((g, H, tl, LANES), bf16),
+        dkvx=v((max(g - 1, 1), H, tl, LANES), bf16),
+        dkvf=v((NQ, LANES), f32),
+        gmix=v((NQ, 2 * LANES), bf16),
+        bps=v((H, M, rm, D), bf16),
+        bcx=v((H, 2, rm, D), bf16),
+        byx=v((H, rm, D), bf16),
+        bzx=v((H, rm, D), bf16),
+        dws=v((R, rb, 2 * LANES), bf16),
+        dwx=v((max(g - 1, 1), H, rb, 2 * LANES), bf16),
+        dwin=v((H, rb, 2 * LANES), bf16),
+        res=v((M, rm, D), bf16),
+        gt=v((M, rm, D), bf16),
+    )
     if p.keep:
-        scratch["prob"] = v((R, tl, NQ), bf16)
+        scratch.update(prob=v((R, tl, NQ), bf16))
     if p.whole_lanes:
-        scratch["raw_out"] = v((HF, rb), bf16)
-        scratch["raw_down"] = v((U, rb), bf16)
+        scratch.update(raw_out=v((HF, rb), bf16))
+        scratch.update(raw_down=v((U, rb), bf16))
     for n, (_, _, width, _, hops) in enumerate(p.streams):
         scratch["came%d" % n] = v((hops, rb, width), bf16)
-    sems = {
-        "wg": (len(p.streams), p.far),
-        "gg": (len(p.streams), p.far),
-        "lr": (R - 1,),
-        "na": (H,),
-        "ny": (H,),
-        "nc": (H,),
-        "nd": (H,),
-        "wa": (H,),
-        "wax": (H, max(g - 1, 1)),
-        "bc": (H, 2),
-        "by": (H,),
-        "bz": (H,),
-        "dwz": (H,),
-        "kvx": (H, max(g - 1, 1)),
-        "att": (H,),
-        "rs": (3, M - 1),
-        "ag": (4, M - 1),
-        "ga": (H,),
-        "dkvx": (max(g - 1, 1), H),
-        "dwx": (max(g - 1, 1), H),
-        "ln": (M - 1,),
-    }
+    sems = dict(
+        wg=(len(p.streams), p.far),
+        gg=(len(p.streams), p.far),
+        lr=(R - 1,),
+        na=(H,),
+        ny=(H,),
+        nc=(H,),
+        nd=(H,),
+        wa=(H,),
+        wax=(H, max(g - 1, 1)),
+        bc=(H, 2),
+        by=(H,),
+        bz=(H,),
+        dwz=(H,),
+        kvx=(H, max(g - 1, 1)),
+        att=(H,),
+        rs=(3, M - 1),
+        ag=(4, M - 1),
+        ah=(4, 3),
+        ga=(H,),
+        dkvx=(max(g - 1, 1), H),
+        dwx=(max(g - 1, 1), H),
+        ln=(M - 1,),
+    )
     for name, shape in sems.items():
         scratch[name + "_s"] = pltpu.SemaphoreType.DMA(shape)
         scratch[name + "_r"] = pltpu.SemaphoreType.DMA(shape)
-    scratch["out"] = pltpu.SemaphoreType.DMA((10,))
-    scratch["loc"] = pltpu.SemaphoreType.DMA((6,))
+    scratch.update(out=pltpu.SemaphoreType.DMA((10,)))
+    scratch.update(loc=pltpu.SemaphoreType.DMA((6,)))
     names = (*ins, *outs, *scratch)
     any_spec = pl.BlockSpec(memory_space=pltpu.HBM)
     flops = 6 * tl * D * p.WC + 14 * NQ * R * tl * HEAD_DIM

time: 159 us -> 155 us (0.975)
  Pallas kernels: 156 us -> 153 us
    pallas_call x1, Pallas kernels: 153 us -> 149 us  [layer(): pl.pallas_call(functools.partial(kernel, p, names), out_shape=[jax.ShapeD...]
where the time goes in v5:
time: 155 us
  Pallas kernels  153 us (99%)
    pallas_call x1, Pallas kernels, layer(): pl.pallas_call(functools.partial(kernel, p, names), out_shape=[jax.ShapeD...  149 us
    pallas_call x1, Pallas kernels, finish(): pl.pallas_call(finish_kernel, out_shape=[jax.ShapeDtypeStruct(shape, f32)...  3.72 us

profile of v5, /device:TPU:0, one launch (start us, length us, event | category | flops | bytes accessed | tf_op | source)
XLA Modules:
  0.0 154.8 jit_solution(13124837713914323632)
XLA Ops:
  0.6 0.0 copy-start.3
  0.7 0.0 copy-start
  0.7 0.0 copy-start.1
  0.7 0.0 copy-start.2
  0.7 0.6 copy-done.3
  1.3 0.0 copy-done
  1.3 0.0 copy-done.1
  1.3 0.0 copy-done.2
  1.3 0.6 fusion.6.refs_6_
  2.0 149.0 %layer.1 = (bf16[4,64,1024]{2,1,0:T(8,128)(2,1)}, bf16[4,64,1024]{2,1,0:T(8,128)(2,1)}, f32[128,768]{1,0:T(8,128)}, f32[128,256]{1,0:T(8,128)}, f32[128,1024]{1,...) custom-call(f32[256,1024]{1,0:T(8,128)} %refs_0_.1, f32[256,1024]{1,0:T(8,128)} %refs_1_.1, bf16[128,768]{1,0:T(8,128)(2,1)} %refs_2_.1, ...), custom_call_target="tpu_custom_call" | custom-call | flops 5502926848 | bytes 8388608 | tf_op jit(solution)/shard_map/layer/pallas_call | solution.py:907
  150.9 3.7 %finish.1 = (f32[256,1024]{1,0:T(8,128)}, f32[256,1024]{1,0:T(8,128)}, f32[128,768]{1,0:T(8,128)}, f32[256,128]{1,0:T(8,128)}, f32[128,1024]{1,0:T(8,128)}, /*in...) custom-call(bf16[4,64,1024]{2,1,0:T(8,128)(2,1)} %get-tuple-element.17.refs_0_, ...), custom_call_target="tpu_custom_call" | custom-call | bytes 6291456 | tf_op jit(solution)/shard_map/finish/pallas_call | solution.py:956
Async XLA Ops:
  0.6 0.7 copy-start.3
  0.7 0.7 copy-start
  0.7 0.7 copy-start.1
  0.7 0.7 copy-start.2

commit v6 on v5

--- a/solution.py
+++ b/solution.py
@@ -51,7 +51,7 @@
     s10 = 8.3
 
 
-TWO_STEPS = (3,)
+TWO_STEPS = (0, 1, 3)
 bf16 = jnp.bfloat16
 f32 = jnp.float32
 
@@ -198,8 +198,12 @@
     vectors = 0.0
     if p.whole_lanes:
         before = jnp.zeros((HEAD_DIM, rb), f32)
-        after = jnp.zeros((HEAD_DIM - 16, rb), f32)
-        vectors = jnp.concatenate([before, r.ln_in[...].astype(f32), after], axis=0).T
+        after = jnp.zeros((HEAD_DIM - 8, rb), f32)
+        row = lax.broadcasted_iota(jnp.int32, (8, rb), 0)
+        eight = jnp.zeros((8, rb), f32)
+        for k, one in enumerate((r.ln_a, r.ln_b, r.ln_c, r.ln_d)):
+            eight = jnp.where(row == k, one[...].astype(f32), eight)
+        vectors = jnp.concatenate([before, eight, after], axis=0).T
     for t in range(H // 2):
         t0, t1, t2 = (
             r.raw_qkv[:, pl.ds((3 * t + k) * LANES, LANES)].astype(f32) for k in range(3)
@@ -788,7 +792,7 @@
         w_out=w_out,
         w_up=w_up,
         w_down=w_down,
-        ln_in=ln_in,
+        **dict(zip(("ln_a", "ln_b", "ln_c", "ln_d") if p.whole_lanes else ("ln_in",), ln_in)),
         scene=scene,
     )
     outs = dict(
@@ -907,7 +911,9 @@
     return pl.pallas_call(
         functools.partial(kernel, p, names),
         out_shape=[jax.ShapeDtypeStruct(*one) for one in outs.values()],
-        in_specs=[any_spec] * 6 + [pl.BlockSpec(memory_space=pltpu.VMEM), pl.BlockSpec(memory_space=pltpu.SMEM)],
+        in_specs=[any_spec] * 6
+        + [pl.BlockSpec(memory_space=pltpu.VMEM)] * len(ln_in)
+        + [pl.BlockSpec(memory_space=pltpu.SMEM)],
         out_specs=out_specs,
         scratch_shapes=list(scratch.values()),
         compiler_params=pltpu.CompilerParams(
@@ -981,11 +987,13 @@
 ):
     p = Plan(tokens, w_qkv, w_up, scene_lengths, lax.axis_size("dp"), lax.axis_size("mp"))
     rb, D, tl = p.rb, p.D, p.tl
-    vectors = jnp.stack([ln1_gain, ln1_bias, ln2_gain, ln2_bias])
-    if not p.whole_lanes:
-        vectors = lax.all_gather(vectors, "dp", axis=1, tiled=True)
+    vectors = [ln1_gain, ln1_bias, ln2_gain, ln2_bias]
+    if p.whole_lanes:
+        vectors = [one.reshape(1, rb) for one in vectors]
+    else:
+        vectors = lax.all_gather(jnp.stack(vectors), "dp", axis=1, tiled=True)
+        vectors = [jnp.pad(vectors, ((0, 12), (0, 0)))]
         w_out, w_down = w_out.T, w_down.T
-    vectors = jnp.pad(vectors, ((0, 12), (0, 0)))
     parts = layer(p, tokens, grad_out, w_qkv, w_out, w_up, w_down, vectors, scene_lengths)
     if p.whole_lanes:
         return finish(p, parts)

time: 155 us -> 153 us (0.987)
  no operation moved by 1% of the time
where the time goes in v6:
time: 153 us
  Pallas kernels  152 us (99%)
    pallas_call x1, Pallas kernels, layer(): pl.pallas_call(functools.partial(kernel, p, names), out_shape=[jax.ShapeD...  149 us
    pallas_call x1, Pallas kernels, finish(): pl.pallas_call(finish_kernel, out_shape=[jax.ShapeDtypeStruct(shape, f32)...  3.72 us

profile of v6, /device:TPU:0, one launch (start us, length us, event | category | flops | bytes accessed | tf_op | source)
XLA Modules:
  0.0 153.3 jit_solution(5682653250955378171)
XLA Ops:
  0.6 148.7 %layer.1 = (bf16[4,64,1024]{2,1,0:T(8,128)(2,1)}, bf16[4,64,1024]{2,1,0:T(8,128)(2,1)}, f32[128,768]{1,0:T(8,128)}, f32[128,256]{1,0:T(8,128)}, f32[128,1024]{1,...) custom-call(f32[256,1024]{1,0:T(8,128)} %refs_0_.1, f32[256,1024]{1,0:T(8,128)} %refs_1_.1, bf16[128,768]{1,0:T(8,128)(2,1)} %refs_2_.1, ...), custom_call_target="tpu_custom_call" | custom-call | flops 5502926848 | bytes 8388608 | tf_op jit(solution)/shard_map/layer/pallas_call | solution.py:911
  149.4 3.7 %finish.1 = (f32[256,1024]{1,0:T(8,128)}, f32[256,1024]{1,0:T(8,128)}, f32[128,768]{1,0:T(8,128)}, f32[256,128]{1,0:T(8,128)}, f32[128,1024]{1,0:T(8,128)}, /*in...) custom-call(bf16[4,64,1024]{2,1,0:T(8,128)(2,1)} %get-tuple-element.17.refs_0_, ...), custom_call_target="tpu_custom_call" | custom-call | bytes 6291456 | tf_op jit(solution)/shard_map/finish/pallas_call | solution.py:962
